TPU v7x, 128 devices: a whole 4x4x4 slice. The times are simulated.
128 devices in a mesh: dp: 2 (over y_hi), row: 16 (over y_lo, z, core), col: 4 (over x).
Axes of the slice: x: 4, y: 4 (y_hi: 2, y_lo: 2; y = y_hi * 2 + y_lo), z: 4, core: 2. Of those that a mesh axis runs over, the one named last changes fastest.
Arguments:
- features: bfloat16 [2, 320, 320, 512], P('dp', 'row', 'col'), parts along dimension 0, may hold values from -6 to 6
- hole_mask: int32 [2, 320, 320], P('dp', 'row', 'col'), parts along dimension 0, may hold values 0 or 1
- cotangent: bfloat16 [2, 320, 320, 512], P('dp', 'row', 'col'), parts along dimension 0, may hold values from -6 to 6
- w_local: bfloat16 [3, 3, 512, 128], replicated, may hold values from -0.09375 to 0.09375
- w_cross: bfloat16 [3, 3, 128, 384], replicated, may hold values from -0.1875 to 0.1875
- w_in: bfloat16 [384, 192], replicated, may hold values from -0.3125 to 0.3125
- w_freq: bfloat16 [384, 384], replicated, may hold values from -0.3125 to 0.3125
- w_out: bfloat16 [192, 384], replicated, may hold values from -0.4375 to 0.4375
Outputs:
- output: bfloat16 [2, 320, 320, 512], P('dp', ('row', 'col')), parts along dimension 0
- grad_features: bfloat16 [2, 320, 320, 512], P('dp', ('row', 'col')), parts along dimension 0
- grad_local: float32 [6, 3, 512, 128], P('dp'), parts along dimension 0
- grad_cross: float32 [6, 3, 128, 384], P('dp'), parts along dimension 0
- grad_in: float32 [768, 192], P('dp'), parts along dimension 0
- grad_freq: float32 [768, 384], P('dp'), parts along dimension 0
- grad_out: float32 [384, 384], P('dp'), parts along dimension 0
There are 2 independent parts, one for each index of `dp`. A program takes and returns all parts, laid end to end along the dimension named above; an argument that names none is the same for every part. Nothing has to cross between parts.
All inputs are finite; a program needn't handle non-finite values. No bound on the sum of `hole_mask` on one device may be relied on, other than what follows from the above.
Results may differ from a plain program's by a relative error of at most 0.025.
Values may be sent and summed in bfloat16 or wider, within the bound.
No kernel may reach another device: no remote copies, remote signals or barrier semaphores. Data moves between devices by JAX's collectives and lax.ppermute only.
A program may use at most 128 MiB of HBM per device.

v0:
```python
import functools
import math

import jax
import jax.numpy as jnp
import numpy as np
from jax import lax
from jax.experimental import pallas as pl
from jax.experimental.pallas import tpu as pltpu
from jax.sharding import PartitionSpec as P

AXES = ("row", "col")
HOLE = 64.0
BF = jnp.bfloat16
F32 = jnp.float32
ROWS_OF = ((0,), (0,))


def dot(a, b, dims=((1,), (0,))):
    return lax.dot_general(a, b, (dims, ((), ())), preferred_element_type=F32)


def line_tables(rows, width, count, lines, slots):
    cos = np.zeros((rows, count, slots, width), np.float32)
    sin = np.zeros((rows, count, slots, width), np.float32)
    freq = lines * np.arange(count)[:, None] + np.arange(lines)[None]
    angle = 2.0 * np.pi * (freq[..., None] * np.arange(width) % width) / width
    valid = (freq <= width // 2)[..., None]
    for y in range(rows):
        cos[y, :, y * lines : (y + 1) * lines] = np.cos(angle) * valid
        sin[y, :, y * lines : (y + 1) * lines] = np.sin(angle) * valid
    shape = (rows, count * slots, width)
    return cos.reshape(shape).astype(BF), sin.reshape(shape).astype(BF)


def column_tables(rows, count, lines, slots):
    height = rows * count
    cos = np.zeros((count, slots, count, slots), np.float32)
    sin = np.zeros((count, slots, count, slots), np.float32)
    h = np.arange(height).reshape(count, rows)
    angle = 2.0 * np.pi * (h[:, :, None, None] * h[None, None] % height) / height
    for y in range(rows):
        for z in range(rows):
            for j in range(lines):
                cos[:, y * lines + j, :, z * lines + j] = np.cos(angle[:, y, :, z])
                sin[:, y * lines + j, :, z * lines + j] = np.sin(angle[:, y, :, z])
    shape = (count * slots, count * slots)
    return cos.reshape(shape).astype(BF), sin.reshape(shape).astype(BF)


def slope_and_silu(value):
    sigma = 1.0 / (1.0 + jnp.exp(-value))
    return sigma * (1.0 + value * (1.0 - sigma)), value * sigma


def lanes_below(shape, bound):
    return lax.broadcasted_iota(jnp.int32, shape, 1) < bound


def packed(re, im):
    mid = jnp.where(lanes_below(re[:, 128:].shape, 64), re[:, 128:], im[:, 128:])
    return jnp.concatenate([re[:, :128], mid, im[:, :128]], 1)


def turned(p, q, sign):
    mid = pltpu.roll(q[:, 128:256], 64, 1)
    flip = jnp.where(lanes_below(mid.shape, 64), sign, -sign)
    return jnp.concatenate(
        [p[:, :128] + sign * q[:, 256:], p[:, 128:256] + flip * mid, p[:, 256:] - sign * q[:, :128]], 1
    )


def pack_order(cs):
    return [(0, 128), (128, cs), (cs + 128, 2 * cs), (cs, cs + 128)]


def pack_dim(x, dim, cs):
    return jnp.concatenate([lax.slice_in_dim(x, a, b, axis=dim) for a, b in pack_order(cs)], dim)


def unpack_dim(x, dim, cs):
    cuts = [(0, 128), (128, cs), (256, 384), (cs, 256)]
    return jnp.concatenate([lax.slice_in_dim(x, a, b, axis=dim) for a, b in cuts], dim)


def call(body, name, grid, ins, outs, scratch=(), flops=0, bytes_=0):
    def spec(shape, block, index):
        if block is None:
            zeros = (0,) * len(shape)
            return pl.BlockSpec(shape, lambda *_: zeros)
        return pl.BlockSpec(block, index)

    return pl.pallas_call(
        body,
        grid=grid,
        in_specs=[spec(a.shape, block, index) for a, block, index in ins],
        out_specs=[spec(shape, block, index) for shape, _, block, index in outs],
        out_shape=[jax.ShapeDtypeStruct(shape, dtype) for shape, dtype, _, _ in outs],
        scratch_shapes=list(scratch),
        compiler_params=pltpu.CompilerParams(vmem_limit_bytes=56 << 20),
        cost_estimate=pl.CostEstimate(flops=flops, bytes_accessed=bytes_, transcendentals=0),
        name=name,
    )(*[a for a, _, _ in ins])


def head_kernel(norm, cl, marked, w_in, tc, ts, masked, unit, sent, acc_c, acc_s):
    y = pl.program_id(0)
    x = marked[...].reshape(-1, marked.shape[-1])
    keep = x[:, :1].astype(F32) < 0.5 * HOLE
    x = jnp.where(keep, x, jnp.zeros_like(x))
    masked[0] = x
    u = slope_and_silu(dot(x[:, cl:], w_in[...]))[1].astype(BF)
    unit[0] = u
    transform_out(y, norm, u, tc, ts, sent, acc_c, acc_s)


def transform_out(y, norm, u, tc, ts, sent, acc_c, acc_s):
    re, im = dot(tc[0], u), dot(ts[0], u)

    @pl.when(y == 0)
    def _():
        acc_c[...] = re
        acc_s[...] = im

    @pl.when(y > 0)
    def _():
        acc_c[...] += re
        acc_s[...] += im

    @pl.when(y == pl.num_programs(0) - 1)
    def _():
        sent[...] = packed(acc_c[...] * norm, acc_s[...] * -norm).astype(BF)


def frequency_kernel(norm, tile, got, tc, ts, w_freq, weight, sign, stacked, sent, z):
    def first(k, carry):
        rows = pl.ds(pl.multiple_of(k * tile, tile), tile)
        spec = turned(dot(tc[rows, :], got[...]), dot(ts[rows, :], got[...]), 1.0) * norm
        st = spec.astype(BF)
        stacked[rows, :] = st
        pos = slope_and_silu(dot(st, w_freq[...]))[1]
        neg = slope_and_silu(dot((st.astype(F32) * sign[...]).astype(BF), w_freq[...]))[1]
        z[rows, :] = (weight[rows, :] * (pos + sign[...] * neg)).astype(BF)
        return carry

    def second(k, carry):
        rows = pl.ds(pl.multiple_of(k * tile, tile), tile)
        sent[rows, :] = (turned(dot(tc[rows, :], z[...]), dot(ts[rows, :], z[...]), -1.0) * norm).astype(BF)
        return carry

    steps = got.shape[0] // tile
    lax.fori_loop(0, steps, first, 0)
    lax.fori_loop(0, steps, second, 0)


def frequency_back_kernel(
    norm, tile, got, tc, ts, w_freq, w_freq_t, weight, sign, stacked, sent, grad, z, acc_p, acc_m
):
    acc_p[...] = jnp.zeros_like(acc_p)
    acc_m[...] = jnp.zeros_like(acc_m)

    def first(k, carry):
        rows = pl.ds(pl.multiple_of(k * tile, tile), tile)
        dz = turned(dot(tc[rows, :], got[...]), dot(ts[rows, :], got[...]), 1.0) * norm
        st = stacked[rows, :]
        pos = slope_and_silu(dot(st, w_freq[...]))[0]
        neg = slope_and_silu(dot((st.astype(F32) * sign[...]).astype(BF), w_freq[...]))[0]
        pos = (dz * pos).astype(BF).astype(F32)
        neg = (dz * sign[...] * neg).astype(BF).astype(F32)
        total = (weight[rows, :] * (pos + neg)).astype(BF)
        delta = (weight[rows, :] * (pos - neg)).astype(BF)
        acc_p[...] += dot(st[:, :256], total, ROWS_OF)
        acc_m[...] += dot(st[:, 128:], delta, ROWS_OF)
        re = dot(total, w_freq_t[:, :256])
        im = dot(delta, w_freq_t[:, 128:])
        mid = jnp.where(lanes_below((tile, 128), 64), re[:, 128:], im[:, :128])
        z[rows, :] = jnp.concatenate([re[:, :128], mid, im[:, 128:]], 1).astype(BF)
        return carry

    def second(k, carry):
        rows = pl.ds(pl.multiple_of(k * tile, tile), tile)
        sent[rows, :] = (turned(dot(tc[rows, :], z[...]), dot(ts[rows, :], z[...]), -1.0) * norm).astype(BF)
        return carry

    steps = got.shape[0] // tile
    lax.fori_loop(0, steps, first, 0)
    lax.fori_loop(0, steps, second, 0)
    grad[0:192, :] = acc_p[0:192, :].astype(BF)
    grad[192:256, :] = acc_m[64:128, :].astype(BF)
    grad[256:384, :] = acc_m[128:256, :].astype(BF)


def imag_first(got):
    mid = pltpu.roll(got[:, 128:256].astype(F32), 64, 1).astype(BF)
    return jnp.concatenate([got[:, 256:], mid], 1)


def middle_kernel(
    norm, cl, got, tct, tst, tc, ts, unit, pre, cot, w_out, w_out_t,
    output, d_out, d_joined, sent, grad, got_s, acc_c, acc_s, acc_g,
):
    y = pl.program_id(0)

    @pl.when(y == 0)
    def _():
        got_s[...] = imag_first(got[...])

    back = ((dot(tct[0], got[:, :256]) - dot(tst[0], got_s[...])) * norm).astype(BF)
    joined = (unit[0].astype(F32) + back.astype(F32)).astype(BF)
    pre_all = jnp.concatenate([pre[0, :, :cl], pre[0, :, cl:] + dot(joined, w_out[...])], 1)
    slope, silu = slope_and_silu(pre_all)
    output[0] = silu.astype(BF)
    d = (cot[...].reshape(-1, cot.shape[-1]).astype(F32) * slope).astype(BF)
    d_out[0] = d
    dj = dot(d[:, cl:], w_out_t[...]).astype(BF)
    d_joined[0] = dj
    g = dot(joined, d[:, cl:], ROWS_OF)

    @pl.when(y == 0)
    def _():
        acc_g[...] = g

    @pl.when(y > 0)
    def _():
        acc_g[...] += g

    transform_out(y, norm, dj, tc, ts, sent, acc_c, acc_s)

    @pl.when(y == pl.num_programs(0) - 1)
    def _():
        grad[...] = acc_g[0 : grad.shape[0], :].astype(BF)


def tail_kernel(
    norm, cl, got, tct, tst, masked, marked, d_joined, d_conv, w_in, w_in_t, grad_features, grad, got_s, acc_g
):
    y = pl.program_id(0)

    @pl.when(y == 0)
    def _():
        got_s[...] = imag_first(got[...])

    back = ((dot(tct[0], got[:, :256]) - dot(tst[0], got_s[...])) * norm).astype(BF)
    x = masked[0, :, cl:]
    slope = slope_and_silu(dot(x, w_in[...]))[0]
    du = ((d_joined[0].astype(F32) + back.astype(F32)) * slope).astype(BF)
    g = dot(x, du, ROWS_OF)

    @pl.when(y == 0)
    def _():
        acc_g[...] = g

    @pl.when(y > 0)
    def _():
        acc_g[...] += g

    keep = marked[...].reshape(-1, marked.shape[-1])[:, :1].astype(F32) < 0.5 * HOLE
    total = jnp.concatenate([d_conv[0, :, :cl], d_conv[0, :, cl:] + dot(du, w_in_t[...])], 1)
    grad_features[0] = jnp.where(keep, total, 0.0).astype(BF)

    @pl.when(y == pl.num_programs(0) - 1)
    def _():
        grad[...] = acc_g[...].astype(BF)


def shifted(x, step):
    n = x.shape[0]
    at = lax.broadcasted_iota(jnp.int32, x.shape, 0)
    if step == 1:
        return jnp.where(at == 0, 0.0, pltpu.roll(x, 1, 0))
    return jnp.where(at == n - 1, 0.0, pltpu.roll(x, n - 1, 0))


def three(x):
    f = x.astype(F32)
    return jnp.concatenate([shifted(f, -1).astype(BF), x, shifted(f, 1).astype(BF)], 1)


def conv_kernel(cl, above, masked, below, w_local, w_cross, pre, pad):
    y = pl.program_id(0)
    rows = masked.shape[0]

    @pl.when(y == 0)
    def _():
        pad[0] = above[0]
        pad[1 : rows + 1] = masked[...]
        pad[rows + 1] = below[0]

    local = dot(pad[y], w_local[0]) + dot(pad[y + 1], w_local[1]) + dot(pad[y + 2], w_local[2])
    near = jnp.concatenate([pad[y, :, :cl], pad[y + 1, :, :cl], pad[y + 2, :, :cl]], 1)
    cross = dot(near, w_cross[...])
    c, g = cl, w_cross.shape[1] // 3
    pre[0, :, :cl] = shifted(local[:, :c], 1) + local[:, c : 2 * c] + shifted(local[:, 2 * c :], -1)
    pre[0, :, cl:] = shifted(cross[:, :g], 1) + cross[:, g : 2 * g] + shifted(cross[:, 2 * g :], -1)


def conv_grad_kernel(cl, above, masked, below, d_out, g_local, g_cross, pad, acc_l, acc_c):
    y = pl.program_id(0)
    rows = masked.shape[0]

    @pl.when(y == 0)
    def _():
        pad[0] = above[0]
        pad[1 : rows + 1] = masked[...]
        pad[rows + 1] = below[0]
        acc_l[...] = jnp.zeros_like(acc_l)
        acc_c[...] = jnp.zeros_like(acc_c)

    d_local = three(d_out[0, :, :cl])
    d_global = three(d_out[0, :, cl:])
    g = d_global.shape[1] // 3
    for i in range(3):
        x = pad[y + i]
        acc_l[i] += dot(x, d_local, ROWS_OF)
        acc_c[i] += dot(x[:, :cl], d_global, ROWS_OF)

    @pl.when(y == pl.num_programs(0) - 1)
    def _():
        for i in range(3):
            g_local[i] = acc_l[i].astype(BF)
            for j in range(3):
                g_cross[i, j] = acc_c[i, :, j * g : (j + 1) * g].astype(BF)


def conv_back_kernel(cl, above, d_out, below, w_local, w_cross, d_conv, pad_l, pad_g):
    y = pl.program_id(0)
    rows = d_out.shape[0]

    @pl.when(y == 0)
    def _():
        for k in range(rows + 2):
            line = above[0] if k == 0 else below[0] if k == rows + 1 else d_out[k - 1]
            pad_l[k] = three(line[:, :cl])
            pad_g[k] = three(line[:, cl:])

    total = dot(pad_l[y + 2], w_local[0]) + dot(pad_l[y + 1], w_local[1]) + dot(pad_l[y], w_local[2])
    cross = dot(pad_g[y + 2], w_cross[0]) + dot(pad_g[y + 1], w_cross[1]) + dot(pad_g[y], w_cross[2])
    d_conv[0, :, :cl] = total[:, :cl] + cross
    d_conv[0, :, cl:] = total[:, cl:]


def swap(x, count):
    return lax.all_to_all(x.reshape(count, -1, x.shape[-1]), AXES, 0, 0, tiled=True).reshape(x.shape)


def to_rows(field, cols):
    h, w, c = field.shape
    return lax.all_to_all(field.reshape(cols, h // cols, w, c), "col", 0, 0, tiled=True)


def edges(field, count):
    down = lax.ppermute(field[-1:], AXES, [(i, i + 1) for i in range(count - 1)])
    up = lax.ppermute(field[:1], AXES, [(i + 1, i) for i in range(count - 1)])
    return down, up


def scatter_sum(x, count):
    x = lax.all_to_all(x.reshape(count, -1, x.shape[-1]), AXES, 0, 0, tiled=True)
    return x.astype(F32).sum(0).astype(BF)


def gather(x, count):
    x = lax.all_to_all(jnp.broadcast_to(x[None], (count,) + x.shape), AXES, 0, 0, tiled=True)
    return x.reshape(-1, x.shape[-1])


def tie(value, *after):
    return lax.optimization_barrier((value,) + after)[0]


def shards(features, hole_mask, cotangent, w_local, w_cross, w_in, w_freq, w_out):
    cols = lax.axis_size("col")
    count = lax.axis_size("row") * cols
    me = lax.axis_index(AXES)
    _, h, w, ch = features.shape
    rows, width = h // cols, w * cols
    height = rows * count
    cl, cg, cs = w_local.shape[3], w_cross.shape[3], w_in.shape[1]
    lines = -(-(width // 2 + 1) // count)
    slots = -(-(rows * lines) // 16) * 16
    n = count * slots
    tile = min(256, n)
    tc, ts = line_tables(rows, width, count, lines, slots)
    tct, tst = jnp.asarray(tc.transpose(0, 2, 1)), jnp.asarray(ts.transpose(0, 2, 1))
    tc, ts = jnp.asarray(tc), jnp.asarray(ts)
    hc, hs = (jnp.asarray(t) for t in column_tables(rows, count, lines, slots))
    norm_w, norm_h = 1.0 / math.sqrt(width), 1.0 / math.sqrt(height)
    freq = lines * me + jnp.arange(slots) % lines
    weight = jnp.where((freq == 0) | (freq * 2 == width), 0.5, jnp.where(freq * 2 < width, 1.0, 0.0))
    weight = jnp.tile(weight.astype(F32), count)[:, None]
    sign = np.where((np.arange(384) < 192), 1.0, -1.0).astype(np.float32)
    sign = jnp.asarray(sign[None])

    w_in_d = jnp.concatenate([w_in, w_in[:, 128:]], 1)
    w_in_t = jnp.pad(w_in.T, ((0, 64), (0, 0)))
    w_out_z = jnp.pad(w_out, ((0, 64), (0, 0)))
    w_out_t = jnp.concatenate([w_out, w_out[128:]], 0).T
    w_freq_p = pack_dim(pack_dim(w_freq, 0, cs), 1, cs)
    w_freq_t = w_freq_p.T
    wl = jnp.transpose(w_local, (0, 2, 1, 3)).reshape(3, ch, 3 * cl)
    wc = jnp.transpose(w_cross, (0, 2, 1, 3)).reshape(3 * cl, 3 * cg)
    wl_t = jnp.transpose(w_local, (0, 1, 3, 2)).reshape(3, 3 * cl, ch)
    wc_t = jnp.transpose(w_cross, (0, 1, 3, 2)).reshape(3, 3 * cg, cl)

    at_y = lambda y: (y, 0, 0)
    one_row = lambda c: (1, width, c)
    blocks = lambda c: (cols, 1, w, c)
    at_blocks = lambda y: (0, y, 0, 0)
    line_table = (1, n, width)
    back_table = (1, width, n)
    wide = (rows, width, ch)
    pix = rows * width
    vm = pltpu.VMEM

    marked = jnp.where(hole_mask[0][..., None] == 1, HOLE, features[0]).astype(BF)
    marked = to_rows(marked, cols)
    cot = to_rows(tie(cotangent[0], marked), cols)

    masked, unit, sent = call(
        functools.partial(head_kernel, norm_w, cl),
        "head",
        (rows,),
        [(marked, blocks(ch), at_blocks), (w_in_d, None, None), (tc, line_table, at_y), (ts, line_table, at_y)],
        [(wide, BF, one_row(ch), at_y), ((rows, width, 256), BF, one_row(256), at_y), ((n, 384), BF, None, None)],
        [vm((n, 256), F32), vm((n, 256), F32)],
        flops=4 * n * pix * 256, bytes_=12 << 20,
    )
    got = swap(sent, count)
    above, below = edges(masked, count)
    (pre,) = call(
        functools.partial(conv_kernel, cl),
        "conv",
        (rows,),
        [(above, None, None), (masked, None, None), (below, None, None), (wl, None, None), (wc, None, None)],
        [(wide, F32, one_row(ch), at_y)],
        [vm((rows + 2, width, ch), BF)],
        flops=18 * pix * (ch * cl + cl * cg), bytes_=9 << 20,
    )
    stacked, sent = call(
        functools.partial(frequency_kernel, norm_h, tile),
        "frequency",
        (1,),
        [(got, None, None), (hc, None, None), (hs, None, None), (w_freq_p, None, None), (weight, None, None), (sign, None, None)],
        [((n, 384), BF, None, None), ((n, 384), BF, None, None)],
        [vm((n, 384), BF)],
        flops=8 * n * n * 384, bytes_=7 << 20,
    )
    got = swap(sent, count)
    cot = tie(cot, got)
    output, d_out, d_joined, sent, grad_out = call(
        functools.partial(middle_kernel, norm_w, cl),
        "middle",
        (rows,),
        [
            (got, None, None), (tct, back_table, at_y), (tst, back_table, at_y), (tc, line_table, at_y),
            (ts, line_table, at_y), (unit, one_row(256), at_y), (pre, one_row(ch), at_y), (cot, blocks(ch), at_blocks),
            (w_out_z, None, None), (w_out_t, None, None),
        ],
        [
            (wide, BF, one_row(ch), at_y), (wide, BF, one_row(ch), at_y), ((rows, width, 256), BF, one_row(256), at_y),
            ((n, 384), BF, None, None), ((cs, cg), BF, None, None),
        ],
        [vm((n, 256), BF), vm((n, 256), F32), vm((n, 256), F32), vm((256, cg), F32)],
        flops=8 * n * pix * 256, bytes_=24 << 20,
    )
    got = swap(sent, count)
    grad_local, grad_cross = call(
        functools.partial(conv_grad_kernel, cl),
        "conv_grad",
        (rows,),
        [(above, None, None), (masked, None, None), (below, None, None), (d_out, one_row(ch), at_y)],
        [((3, ch, 3 * cl), BF, None, None), ((3, 3, cl, cg), BF, None, None)],
        [vm((rows + 2, width, ch), BF), vm((3, ch, 3 * cl), F32), vm((3, cl, 3 * cg), F32)],
        flops=18 * pix * (ch * cl + cl * cg), bytes_=7 << 20,
    )
    d_above, d_below = edges(d_out, count)
    got = tie(got, grad_local)
    sent, grad_freq = call(
        functools.partial(frequency_back_kernel, norm_h, tile),
        "frequency_back",
        (1,),
        [
            (got, None, None), (hc, None, None), (hs, None, None), (w_freq_p, None, None), (w_freq_t, None, None),
            (weight, None, None), (sign, None, None), (stacked, None, None),
        ],
        [((n, 384), BF, None, None), ((384, 384), BF, None, None)],
        [vm((n, 384), BF), vm((256, 384), F32), vm((256, 384), F32)],
        flops=8 * n * n * 384, bytes_=8 << 20,
    )
    got = swap(sent, count)
    pieces = [grad_local.reshape(-1, 384), grad_cross.reshape(-1, 384), grad_freq, grad_out]
    sizes = [p.shape[0] for p in pieces]
    room = -(-sum(sizes) // (16 * count)) * 16 * count
    early = scatter_sum(jnp.pad(jnp.concatenate(pieces, 0), ((0, room - sum(sizes)), (0, 0))), count)
    (d_conv,) = call(
        functools.partial(conv_back_kernel, cl),
        "conv_back",
        (rows,),
        [(d_above, None, None), (d_out, None, None), (d_below, None, None), (wl_t, None, None), (wc_t, None, None)],
        [(wide, F32, one_row(ch), at_y)],
        [vm((rows + 2, width, 3 * cl), BF), vm((rows + 2, width, 3 * cg), BF)],
        flops=18 * pix * (ch * cl + cl * cg), bytes_=9 << 20,
    )
    grad_features, grad_in = call(
        functools.partial(tail_kernel, norm_w, cl),
        "tail",
        (rows,),
        [
            (got, None, None), (tct, back_table, at_y), (tst, back_table, at_y), (masked, one_row(ch), at_y),
            (marked, blocks(128), at_blocks), (d_joined, one_row(256), at_y), (d_conv, one_row(ch), at_y),
            (w_in_d, None, None), (w_in_t, None, None),
        ],
        [(wide, BF, one_row(ch), at_y), ((cg, 256), BF, None, None)],
        [vm((n, 256), BF), vm((cg, 256), F32)],
        flops=4 * n * pix * 256, bytes_=16 << 20,
    )
    early = gather(early, count)
    outs, at = [], 0
    for size in sizes:
        outs.append(early[at : at + size].astype(F32))
        at += size
    grad_local, grad_cross, grad_freq, grad_out = outs
    late = gather(scatter_sum(grad_in[:, :cs].reshape(-1, 128), count), count)
    grad_in = late.reshape(cg, cs).astype(F32)
    grad_local = jnp.transpose(grad_local.reshape(3, ch, 3, cl), (0, 2, 1, 3))
    grad_cross = grad_cross.reshape(3, 3, cl, cg)
    grad_freq = unpack_dim(unpack_dim(grad_freq, 0, cs), 1, cs)
    return output[None], grad_features[None], grad_local, grad_cross, grad_in, grad_freq, grad_out


def solution(mesh):
    return jax.shard_map(
        shards,
        mesh=mesh,
        in_specs=(
            P("dp", "row", "col", None),
            P("dp", "row", "col"),
            P("dp", "row", "col", None),
            P(),
            P(),
            P(),
            P(),
            P(),
        ),
        out_specs=(
            P("dp", ("row", "col"), None, None),
            P("dp", ("row", "col"), None, None),
            P("dp", None, None, None),
            P("dp", None, None, None),
            P("dp", None),
            P("dp", None),
            P("dp", None),
        ),
        check_vma=False,
    )
```

profile of v0, /device:TPU:1, one launch (start us, length us, event | category | flops | bytes accessed | tf_op | source)
XLA Modules:
  0.0 368.5 jit_solution(3550300215386455315)
XLA Ops:
  4.3 4.8 %all-to-all-start = ((bf16[4,5,80,512]{3,2,1,0:T(8,128)(2,1)}), bf16[4,5,80,512]{3,2,1,0:T(8,128)(2,1)S(1)}, u32[]{:S(2)}, u32[]{:S(2)}) async-start(bf16[4,5,80,512]{3,2,1,0:T(8,128)(2,1)} %broadcast_select_fusion), calls=%async_computation | async-start | bytes 3276800 | tf_op jit(solution)/shard_map/all_to_all | solution.py:348
  10.1 19.6 %all-to-all-done.marked = bf16[4,5,80,512]{3,2,1,0:T(8,128)(2,1)S(1)} async-done(((bf16[4,5,80,512]{3,2,1,0:T(8,128)(2,1)}), bf16[4,5,80,512]{3,2,1,0:T(8,128)(2,1)S(1)}, u32[]{:S(2)}, u32[]{:S(2)}) %all-to-all-start) | async-done | bytes 1638432 | tf_op jit(solution)/shard_map/all_to_all | solution.py:348
  30.8 9.5 %head.1 = (bf16[5,320,512]{2,1,0:T(8,128)(2,1)}, bf16[5,320,256]{2,1,0:T(8,128)(2,1)}, bf16[1024,384]{1,0:T(8,128)(2,1)}) custom-call(bf16[4,5,80,512]{3,2,1,0:T(8,128)(2,1)} %copy-done, bf16[384,256]{1,0:T(8,128)(2,1)} %pad_maximum_fusion.3.w_in, bf16[5,1024,320]{2,1,0:T(8,128)(2,1)} %constant.60.clone.tc, bf16[5,1024,320]{2,1,0:T(8,128)(2,1)} %constant.61.clone.ts), custom_call_target="tpu_custom_call" | custom-call | flops 1677721600 | bytes 12582912 | tf_op jit(solution)/shard_map/head/pallas_call | solution.py:93
  40.4 9.5 %all-to-all-start.1 = ((bf16[64,16,384]{2,1,0:T(8,128)(2,1)}), bf16[64,16,384]{2,1,0:T(8,128)(2,1)S(1)}, u32[]{:S(2)}, u32[]{:S(2)}) async-start(bf16[64,16,384]{2,1,0:T(8,128)(2,1)} %bitcast.64), calls=%async_computation.1 | async-start | bytes 1572864 | tf_op jit(solution)/shard_map/all_to_all | solution.py:343
  49.9 15.4 %all-to-all-done.1 = bf16[64,16,384]{2,1,0:T(8,128)(2,1)S(1)} async-done(((bf16[64,16,384]{2,1,0:T(8,128)(2,1)}), bf16[64,16,384]{2,1,0:T(8,128)(2,1)S(1)}, u32[]{:S(2)}, u32[]{:S(2)}) %all-to-all-start.1) | async-done | bytes 786464 | tf_op jit(solution)/shard_map/all_to_all | solution.py:343
  71.6 11.3 %frequency.1 = (bf16[1024,384]{1,0:T(8,128)(2,1)}, bf16[1024,384]{1,0:T(8,128)(2,1)}) custom-call(bf16[1024,384]{1,0:T(8,128)(2,1)} %bitcast.59, bf16[1024,1024]{1,0:T(8,128)(2,1)} %constant.62.clone.tc, bf16[1024,1024]{1,0:T(8,128)(2,1)} %constant.63.clone.ts, bf16[384,384]{1,0:T(8,128)(2,1)} %copy.41.w_freq, f32[1024,1]{1,0:T(8,128)} %broadcast_in_dim_tile.4.weight, ...), custom_call_target="tpu_custom_call" | custom-call | flops 3221225472 | bytes 7340032 | tf_op jit(solution)/shard_map/frequency/pallas_call | solution.py:93
  82.9 6.9 %all-to-all-done.3.cot = bf16[4,5,80,512]{3,2,1,0:T(8,128)(2,1)S(1)} async-done(((bf16[4,5,80,512]{3,2,1,0:T(8,128)(2,1)}), bf16[4,5,80,512]{3,2,1,0:T(8,128)(2,1)S(1)}, u32[]{:S(2)}, u32[]{:S(2)}) %all-to-all-start.3) | async-done | bytes 1638432 | tf_op jit(solution)/shard_map/all_to_all | solution.py:348
  89.8 6.3 %all-to-all-start.2 = ((bf16[64,16,384]{2,1,0:T(8,128)(2,1)}), bf16[64,16,384]{2,1,0:T(8,128)(2,1)}, u32[]{:S(2)}, u32[]{:S(2)}) async-start(bf16[64,16,384]{2,1,0:T(8,128)(2,1)} %bitcast.60), calls=%async_computation.2 | async-start | bytes 1572864 | tf_op jit(solution)/shard_map/all_to_all | solution.py:343
  114.9 8.7 %conv.1.pre = f32[5,320,512]{2,1,0:T(8,128)} custom-call(bf16[1,320,512]{2,1,0:T(8,128)(2,1)} %collective-permute-done.above, bf16[5,320,512]{2,1,0:T(8,128)(2,1)} %get-tuple-element.29.masked, bf16[1,320,512]{2,1,0:T(8,128)(2,1)} %collective-permute-done.1.below, bf16[3,512,384]{2,1,0:T(8,128)(2,1)} %copy.45.w_local, bf16[384,1152]{1,0:T(8,128)(2,1)} %bitcast.56), custom_call_target="tpu_custom_call" | custom-call | flops 3303014400 | bytes 9437184 | tf_op jit(solution)/shard_map/conv/pallas_call | solution.py:93
  123.6 15.1 %middle.1 = (bf16[5,320,512]{2,1,0:T(8,128)(2,1)}, bf16[5,320,512]{2,1,0:T(8,128)(2,1)}, bf16[5,320,256]{2,1,0:T(8,128)(2,1)}, bf16[1024,384]{1,0:T(8,128)(2,1)}, bf16[192,384]{1,0:T(8,128)(2,1)}) custom-call(bf16[1024,384]{1,0:T(8,128)(2,1)} %bitcast.4.got, bf16[5,320,1024]{2,1,0:T(8,128)(2,1)} %constant.58.clone.tct, ...), custom_call_target="tpu_custom_call" | custom-call | flops 3355443200 | bytes 25165824 | tf_op jit(solution)/shard_map/middle/pallas_call | solution.py:93
  138.7 7.8 %all-to-all-start.4 = ((bf16[64,16,384]{2,1,0:T(8,128)(2,1)}), bf16[64,16,384]{2,1,0:T(8,128)(2,1)S(1)}, u32[]{:S(2)}, u32[]{:S(2)}) async-start(bf16[64,16,384]{2,1,0:T(8,128)(2,1)} %bitcast.63), calls=%async_computation.4 | async-start | bytes 1572864 | tf_op jit(solution)/shard_map/all_to_all | solution.py:343
  146.4 10.9 %conv_grad.1 = (bf16[3,512,384]{2,1,0:T(8,128)(2,1)}, bf16[3,3,128,384]{3,2,1,0:T(8,128)(2,1)}) custom-call(bf16[1,320,512]{2,1,0:T(8,128)(2,1)} %collective-permute-done.above, bf16[5,320,512]{2,1,0:T(8,128)(2,1)} %get-tuple-element.29.masked, bf16[1,320,512]{2,1,0:T(8,128)(2,1)} %collective-permute-done.1.below, bf16[5,320,512]{2,1,0:T(8,128)(2,1)} %get-tuple-element.34.d_out), custom_call_target="tpu_custom_call" | custom-call | flops 3303014400 | bytes 7340032 | tf_op jit(solution)/shard_map/conv_grad/pallas_call | solution.py:93
  162.7 13.4 %frequency_back.1 = (bf16[1024,384]{1,0:T(8,128)(2,1)}, bf16[384,384]{1,0:T(8,128)(2,1)}) custom-call(bf16[1024,384]{1,0:T(8,128)(2,1)} %bitcast.62, bf16[1024,1024]{1,0:T(8,128)(2,1)} %constant.62.clone.tc, bf16[1024,1024]{1,0:T(8,128)(2,1)} %constant.63.clone.ts, bf16[384,384]{1,0:T(8,128)(2,1)} %copy.41.w_freq, bf16[384,384]{1,0:T(8,128)(2,1)} %bitcast.51, ...), custom_call_target="tpu_custom_call" | custom-call | flops 3221225472 | bytes 8388608 | tf_op jit(solution)/shard_map/frequency_back/pallas_call | solution.py:93
  176.2 5.6 %all-to-all-start.5 = ((bf16[64,16,384]{2,1,0:T(8,128)(2,1)}), bf16[64,16,384]{2,1,0:T(8,128)(2,1)}, u32[]{:S(2)}, u32[]{:S(2)}) async-start(bf16[64,16,384]{2,1,0:T(8,128)(2,1)} %bitcast.61), calls=%async_computation.5 | async-start | bytes 1572864 | tf_op jit(solution)/shard_map/all_to_all | solution.py:343
  193.9 6.6 %collective-permute-done.2.above = bf16[1,320,512]{2,1,0:T(8,128)(2,1)} collective-permute-done((bf16[1,320,512]{2,1,0:T(8,128)(2,1)S(1)}, bf16[1,320,512]{2,1,0:T(8,128)(2,1)}, u32[]{:S(2)}, u32[]{:S(2)}) %collective-permute-start.2) | collective-permute-done | bytes 327712 | tf_op jit(solution)/shard_map/ppermute | solution.py:352
  200.5 10.5 %conv_back.1.d_conv = f32[5,320,512]{2,1,0:T(8,128)} custom-call(bf16[1,320,512]{2,1,0:T(8,128)(2,1)} %collective-permute-done.2.above, bf16[5,320,512]{2,1,0:T(8,128)(2,1)} %get-tuple-element.34.d_out, bf16[1,320,512]{2,1,0:T(8,128)(2,1)} %collective-permute-done.3.below, bf16[3,384,512]{2,1,0:T(8,128)(2,1)} %bitcast.52, bf16[3,1152,128]{2,1,0:T(8,128)(2,1)} %bitcast.55), custom_call_target="tpu_custom_call" | custom-call | flops 3303014400 | bytes 9437184 | tf_op jit(solution)/shard_map/conv_back/pallas_call | solution.py:93
  211.1 10.7 %tail.1 = (bf16[5,320,512]{2,1,0:T(8,128)(2,1)}, bf16[384,256]{1,0:T(8,128)(2,1)}) custom-call(bf16[1024,384]{1,0:T(8,128)(2,1)} %bitcast.16.got, bf16[5,320,1024]{2,1,0:T(8,128)(2,1)} %constant.58.clone.tct, bf16[5,320,1024]{2,1,0:T(8,128)(2,1)} %constant.59.clone.tst, bf16[5,320,512]{2,1,0:T(8,128)(2,1)} %get-tuple-element.29.masked, ...), custom_call_target="tpu_custom_call" | custom-call | flops 1677721600 | bytes 16777216 | tf_op jit(solution)/shard_map/tail/pallas_call | solution.py:93
  223.6 7.6 %all-to-all-start.8 = ((bf16[64,9,128]{2,1,0:T(8,128)(2,1)}), bf16[64,9,128]{2,1,0:T(8,128)(2,1)S(1)}, u32[]{:S(2)}, u32[]{:S(2)}) async-start(bf16[64,9,128]{2,1,0:T(8,128)(2,1)} %reshape_reshape.4), calls=%async_computation.8 | async-start | bytes 524288 | tf_op jit(solution)/shard_map/all_to_all | solution.py:358
  231.3 11.5 %fusion.6 = bf16[4096,384]{1,0:T(8,128)(2,1)} fusion(bf16[192,384]{1,0:T(8,128)(2,1)S(1)} %copy-done.15, bf16[384,384]{1,0:T(8,128)(2,1)S(1)} %copy-done.14, bf16[1152,384]{1,0:T(8,128)(2,1)S(1)} %bitcast.57, bf16[1536,384]{1,0:T(8,128)(2,1)S(1)} %bitcast.54), kind=kLoop, calls=%fused_computation.7 | loop fusion | flops 20447232 | bytes 5652480 | tf_op jit(solution)/shard_map/concatenate | solution.py:494
  242.8 8.9 %all-to-all-start.6 = ((bf16[64,64,384]{2,1,0:T(8,128)(2,1)}), bf16[64,64,384]{2,1,0:T(8,128)(2,1)S(1)}, u32[]{:S(2)}, u32[]{:S(2)}) async-start(bf16[64,64,384]{2,1,0:T(8,128)(2,1)} %bitcast.42), calls=%async_computation.6 | async-start | bytes 6291456 | tf_op jit(solution)/shard_map/all_to_all | solution.py:358
  251.8 41.0 %all-to-all-done.6 = bf16[64,64,384]{2,1,0:T(8,128)(2,1)S(1)} async-done(((bf16[64,64,384]{2,1,0:T(8,128)(2,1)}), bf16[64,64,384]{2,1,0:T(8,128)(2,1)S(1)}, u32[]{:S(2)}, u32[]{:S(2)}) %all-to-all-start.6) | async-done | bytes 3145760 | tf_op jit(solution)/shard_map/all_to_all | solution.py:358
  293.5 5.3 %all-to-all-start.9 = ((bf16[64,9,128]{2,1,0:T(8,128)(2,1)}), bf16[64,9,128]{2,1,0:T(8,128)(2,1)S(1)}, u32[]{:S(2)}, u32[]{:S(2)}) async-start(bf16[64,9,128]{2,1,0:T(8,128)(2,1)} %broadcast_in_dim.50), calls=%async_computation.9 | async-start | bytes 524288 | tf_op jit(solution)/shard_map/all_to_all | solution.py:363
  299.3 9.5 %all-to-all-done.9 = bf16[64,9,128]{2,1,0:T(8,128)(2,1)S(1)} async-done(((bf16[64,9,128]{2,1,0:T(8,128)(2,1)}), bf16[64,9,128]{2,1,0:T(8,128)(2,1)S(1)}, u32[]{:S(2)}, u32[]{:S(2)}) %all-to-all-start.9) | async-done | bytes 147488 | tf_op jit(solution)/shard_map/all_to_all | solution.py:363
  317.6 39.1 %all-to-all-done.7 = bf16[64,64,384]{2,1,0:T(8,128)(2,1)S(1)} async-done(((bf16[64,64,384]{2,1,0:T(8,128)(2,1)}), bf16[64,64,384]{2,1,0:T(8,128)(2,1)S(1)}, u32[]{:S(2)}, u32[]{:S(2)}) %all-to-all-start.7) | async-done | bytes 3145760 | tf_op jit(solution)/shard_map/all_to_all | solution.py:363
  (107 shorter events, 71.9 us)
Async XLA Ops:
  4.3 25.3 %all-to-all-start = ((bf16[4,5,80,512]{3,2,1,0:T(8,128)(2,1)}), bf16[4,5,80,512]{3,2,1,0:T(8,128)(2,1)S(1)}, u32[]{:S(2)}, u32[]{:S(2)}) async-start(bf16[4,5,80,512]{3,2,1,0:T(8,128)(2,1)} %broadcast_select_fusion), calls=%async_computation | async-start | bytes 3276800 | tf_op jit(solution)/shard_map/all_to_all | solution.py:348
  40.4 28.5 %slice-start.4 = ((bf16[384,384]{1,0:T(8,128)(2,1)}), bf16[128,384]{1,0:T(8,128)(2,1)S(1)}, s32[]{:S(2)}) async-start(bf16[384,384]{1,0:T(8,128)(2,1)} %param.21), calls=%async_computation.14 | async-start | bytes 196608 | tf_op jit(solution)/shard_map/slice | solution.py:78
  40.4 28.7 %slice-start.5 = ((bf16[384,384]{1,0:T(8,128)(2,1)}), bf16[64,384]{1,0:T(8,128)(2,1)S(1)}, s32[]{:S(2)}) async-start(bf16[384,384]{1,0:T(8,128)(2,1)} %param.21), calls=%async_computation.15 | async-start | bytes 98304 | tf_op jit(solution)/shard_map/slice | solution.py:78
  40.4 28.8 %slice-start.6 = ((bf16[384,384]{1,0:T(8,128)(2,1)}), bf16[192,384]{1,0:T(8,128)(2,1)S(1)}, s32[]{:S(2)}) async-start(bf16[384,384]{1,0:T(8,128)(2,1)} %param.21), calls=%async_computation.16 | async-start | bytes 294912 | tf_op jit(solution)/shard_map/slice | solution.py:78
  40.4 24.9 %all-to-all-start.1 = ((bf16[64,16,384]{2,1,0:T(8,128)(2,1)}), bf16[64,16,384]{2,1,0:T(8,128)(2,1)S(1)}, u32[]{:S(2)}, u32[]{:S(2)}) async-start(bf16[64,16,384]{2,1,0:T(8,128)(2,1)} %bitcast.64), calls=%async_computation.1 | async-start | bytes 1572864 | tf_op jit(solution)/shard_map/all_to_all | solution.py:343
  65.3 24.5 %all-to-all-start.3 = ((bf16[4,5,80,512]{3,2,1,0:T(8,128)(2,1)}), bf16[4,5,80,512]{3,2,1,0:T(8,128)(2,1)S(1)}, u32[]{:S(2)}, u32[]{:S(2)}) async-start(bf16[4,5,80,512]{3,2,1,0:T(8,128)(2,1)} %bitcast.9), calls=%async_computation.3 | async-start | bytes 3276800 | tf_op jit(solution)/shard_map/all_to_all | solution.py:348
  82.9 21.9 %copy-start.3 = (bf16[3,3,512,128]{3,2,1,0:T(8,128)(2,1)S(1)}, bf16[3,3,512,128]{3,2,1,0:T(8,128)(2,1)}, u32[]{:S(2)}) copy-start(bf16[3,3,512,128]{3,2,1,0:T(8,128)(2,1)} %param.18) | copy-start | bytes 3538948
  89.8 18.9 %copy-start.2 = (bf16[4,5,80,512]{3,2,1,0:T(8,128)(2,1)}, bf16[4,5,80,512]{3,2,1,0:T(8,128)(2,1)S(1)}, u32[]{:S(2)}) copy-start(bf16[4,5,80,512]{3,2,1,0:T(8,128)(2,1)S(1)} %all-to-all-done.3.cot) | copy-start | bytes 4915204
  89.8 33.8 %all-to-all-start.2 = ((bf16[64,16,384]{2,1,0:T(8,128)(2,1)}), bf16[64,16,384]{2,1,0:T(8,128)(2,1)}, u32[]{:S(2)}, u32[]{:S(2)}) async-start(bf16[64,16,384]{2,1,0:T(8,128)(2,1)} %bitcast.60), calls=%async_computation.2 | async-start | bytes 1572864 | tf_op jit(solution)/shard_map/all_to_all | solution.py:343
  98.1 16.8 %collective-permute-start = (bf16[1,320,512]{2,1,0:T(8,128)(2,1)}, bf16[1,320,512]{2,1,0:T(8,128)(2,1)}, u32[]{:S(2)}, u32[]{:S(2)}) collective-permute-start(bf16[1,320,512]{2,1,0:T(8,128)(2,1)} %get-tuple-element.55), channel_id=1, source_target_pairs={{0,1},{1,2},{2,3},{3,4},{4,5},{5,6},{6,7},{7,8},{8,9},{9,10},{10,1... | collective-permute-start | bytes 983048 | tf_op jit(solution)/shard_map/ppermute | solution.py:352
  101.4 13.5 %collective-permute-start.1 = (bf16[1,320,512]{2,1,0:T(8,128)(2,1)}, bf16[1,320,512]{2,1,0:T(8,128)(2,1)}, u32[]{:S(2)}, u32[]{:S(2)}) collective-permute-start(bf16[1,320,512]{2,1,0:T(8,128)(2,1)} %get-tuple-element.54), channel_id=1, source_target_pairs={{1,0},{2,1},{3,2},{4,3},{5,4},{6,5},{7,6},{8,7},{9,8},{10,9},{11,1... | collective-permute-start | bytes 983048 | tf_op jit(solution)/shard_map/ppermute | solution.py:353
  138.7 23.2 %all-to-all-start.4 = ((bf16[64,16,384]{2,1,0:T(8,128)(2,1)}), bf16[64,16,384]{2,1,0:T(8,128)(2,1)S(1)}, u32[]{:S(2)}, u32[]{:S(2)}) async-start(bf16[64,16,384]{2,1,0:T(8,128)(2,1)} %bitcast.63), calls=%async_computation.4 | async-start | bytes 1572864 | tf_op jit(solution)/shard_map/all_to_all | solution.py:343
  176.2 14.9 %copy-start.4 = (bf16[3,3,128,384]{3,2,1,0:T(8,128)(2,1)S(1)}, bf16[3,3,128,384]{3,2,1,0:T(8,128)(2,1)}, u32[]{:S(2)}) copy-start(bf16[3,3,128,384]{3,2,1,0:T(8,128)(2,1)} %param.19) | copy-start | bytes 2654212
  176.2 34.9 %all-to-all-start.5 = ((bf16[64,16,384]{2,1,0:T(8,128)(2,1)}), bf16[64,16,384]{2,1,0:T(8,128)(2,1)}, u32[]{:S(2)}, u32[]{:S(2)}) async-start(bf16[64,16,384]{2,1,0:T(8,128)(2,1)} %bitcast.61), calls=%async_computation.5 | async-start | bytes 1572864 | tf_op jit(solution)/shard_map/all_to_all | solution.py:343
  182.9 17.7 %collective-permute-start.2 = (bf16[1,320,512]{2,1,0:T(8,128)(2,1)S(1)}, bf16[1,320,512]{2,1,0:T(8,128)(2,1)}, u32[]{:S(2)}, u32[]{:S(2)}) collective-permute-start(bf16[1,320,512]{2,1,0:T(8,128)(2,1)S(1)} %get-tuple-element.53), channel_id=1, source_target_pairs={{0,1},{1,2},{2,3},{3,4},{4,5},{5,6},{6,7},{7,8},{8,9},{9,10},{10,1... | collective-permute-start | bytes 983048 | tf_op jit(solution)/shard_map/ppermute | solution.py:352
  186.1 14.4 %collective-permute-start.3 = (bf16[1,320,512]{2,1,0:T(8,128)(2,1)S(1)}, bf16[1,320,512]{2,1,0:T(8,128)(2,1)}, u32[]{:S(2)}, u32[]{:S(2)}) collective-permute-start(bf16[1,320,512]{2,1,0:T(8,128)(2,1)S(1)} %get-tuple-element.52), channel_id=1, source_target_pairs={{1,0},{2,1},{3,2},{4,3},{5,4},{6,5},{7,6},{8,7},{9,8},{10,9},{11,1... | collective-permute-start | bytes 983048 | tf_op jit(solution)/shard_map/ppermute | solution.py:353
  211.0 20.2 %copy-start.7 = (bf16[3,512,384]{2,1,0:T(8,128)(2,1)S(1)}, bf16[3,512,384]{2,1,0:T(8,128)(2,1)}, u32[]{:S(2)}) copy-start(bf16[3,512,384]{2,1,0:T(8,128)(2,1)} %get-tuple-element.35) | copy-start | bytes 3538948
  211.0 20.2 %copy-start.9 = (bf16[3,3,128,384]{3,2,1,0:T(8,128)(2,1)S(1)}, bf16[3,3,128,384]{3,2,1,0:T(8,128)(2,1)}, u32[]{:S(2)}) copy-start(bf16[3,3,128,384]{3,2,1,0:T(8,128)(2,1)} %get-tuple-element.41) | copy-start | bytes 2654212
  211.0 20.2 %copy-start.14 = (bf16[384,384]{1,0:T(8,128)(2,1)S(1)}, bf16[384,384]{1,0:T(8,128)(2,1)}, u32[]{:S(2)}) copy-start(bf16[384,384]{1,0:T(8,128)(2,1)} %get-tuple-element.42) | copy-start | bytes 884740
  211.1 20.2 %copy-start.15 = (bf16[192,384]{1,0:T(8,128)(2,1)S(1)}, bf16[192,384]{1,0:T(8,128)(2,1)}, u32[]{:S(2)}) copy-start(bf16[192,384]{1,0:T(8,128)(2,1)} %get-tuple-element.43) | copy-start | bytes 442372
  223.6 19.2 %all-to-all-start.8 = ((bf16[64,9,128]{2,1,0:T(8,128)(2,1)}), bf16[64,9,128]{2,1,0:T(8,128)(2,1)S(1)}, u32[]{:S(2)}, u32[]{:S(2)}) async-start(bf16[64,9,128]{2,1,0:T(8,128)(2,1)} %reshape_reshape.4), calls=%async_computation.8 | async-start | bytes 524288 | tf_op jit(solution)/shard_map/all_to_all | solution.py:358
  242.8 50.0 %all-to-all-start.6 = ((bf16[64,64,384]{2,1,0:T(8,128)(2,1)}), bf16[64,64,384]{2,1,0:T(8,128)(2,1)S(1)}, u32[]{:S(2)}, u32[]{:S(2)}) async-start(bf16[64,64,384]{2,1,0:T(8,128)(2,1)} %bitcast.42), calls=%async_computation.6 | async-start | bytes 6291456 | tf_op jit(solution)/shard_map/all_to_all | solution.py:358
  293.5 15.3 %all-to-all-start.9 = ((bf16[64,9,128]{2,1,0:T(8,128)(2,1)}), bf16[64,9,128]{2,1,0:T(8,128)(2,1)S(1)}, u32[]{:S(2)}, u32[]{:S(2)}) async-start(bf16[64,9,128]{2,1,0:T(8,128)(2,1)} %broadcast_in_dim.50), calls=%async_computation.9 | async-start | bytes 524288 | tf_op jit(solution)/shard_map/all_to_all | solution.py:363
  310.9 45.9 %all-to-all-start.7 = ((bf16[64,64,384]{2,1,0:T(8,128)(2,1)}), bf16[64,64,384]{2,1,0:T(8,128)(2,1)S(1)}, u32[]{:S(2)}, u32[]{:S(2)}) async-start(bf16[64,64,384]{2,1,0:T(8,128)(2,1)} %broadcast_in_dim.49), calls=%async_computation.7 | async-start | bytes 6291456 | tf_op jit(solution)/shard_map/all_to_all | solution.py:363
  (13 other events, 44.9 us)
where the time goes:
time: 370 us; the launch traced here: 368 us
  waiting for transfers between devices  144 us (39%)
  Pallas kernels  90.2 us (24%)
  starting transfers between devices  77.6 us (21%)
  local copies, waits for them, and re-layouts  33.2 us (9%)
  other arithmetic  22.4 us (6%)
    pallas_call x8, Pallas kernels, call(): pl.pallas_call(body, grid=grid, in_specs=[spec(a.shape, block, index) for...  90.2 us
    all_to_all x2, waiting for transfers between devices, gather(): lax.all_to_all(jnp.broadcast_to(x[None], (count,) + x.shape), AXES, 0, 0,...  48.6 us
    all_to_all x2, waiting for transfers between devices, scatter_sum(): lax.all_to_all(x.reshape(count, -1, x.shape[-1]), AXES, 0, 0, tiled=True)  41 us
    all_to_all x4, starting transfers between devices, swap(): lax.all_to_all(x.reshape(count, -1, x.shape[-1]), AXES, 0, 0, tiled=True)  29.1 us
    all_to_all x2, waiting for transfers between devices, to_rows(): lax.all_to_all(field.reshape(cols, h // cols, w, c), 'col', 0, 0, tiled=T...  26.4 us
    all_to_all x4, waiting for transfers between devices, swap(): lax.all_to_all(x.reshape(count, -1, x.shape[-1]), AXES, 0, 0, tiled=True)  19.9 us
    all_to_all x2, starting transfers between devices, scatter_sum(): lax.all_to_all(x.reshape(count, -1, x.shape[-1]), AXES, 0, 0, tiled=True)  16.5 us
    concatenate x1, other arithmetic, shards(): jnp.concatenate(pieces, 0)  11.5 us
  transfers between devices with their start and end apart: 14, of which 9 were waited for; matrix products, arithmetic and copies ran while one was open for 9% of the time, Pallas kernels for 11%

commit v1 on v0

--- a/solution.py
+++ b/solution.py
@@ -70,6 +70,12 @@
     )
 
 
+def natural_lanes(x):
+    mid, im = x[:, 128:256], pltpu.roll(x[:, 256:], 64, 1)
+    low = lanes_below(mid.shape, 64)
+    return jnp.concatenate([x[:, :128], jnp.where(low, mid, im), jnp.where(low, im, mid)], 1)
+
+
 def pack_order(cs):
     return [(0, 128), (128, cs), (cs + 128, 2 * cs), (cs, cs + 128)]
 
@@ -78,13 +84,10 @@
     return jnp.concatenate([lax.slice_in_dim(x, a, b, axis=dim) for a, b in pack_order(cs)], dim)
 
 
-def unpack_dim(x, dim, cs):
-    cuts = [(0, 128), (128, cs), (256, 384), (cs, 256)]
-    return jnp.concatenate([lax.slice_in_dim(x, a, b, axis=dim) for a, b in cuts], dim)
-
-
 def call(body, name, grid, ins, outs, scratch=(), flops=0, bytes_=0):
     def spec(shape, block, index):
+        if shape == (1, 1):
+            return pl.BlockSpec(memory_space=pltpu.SMEM)
         if block is None:
             zeros = (0,) * len(shape)
             return pl.BlockSpec(shape, lambda *_: zeros)
@@ -185,9 +188,9 @@
     steps = got.shape[0] // tile
     lax.fori_loop(0, steps, first, 0)
     lax.fori_loop(0, steps, second, 0)
-    grad[0:192, :] = acc_p[0:192, :].astype(BF)
-    grad[192:256, :] = acc_m[64:128, :].astype(BF)
-    grad[256:384, :] = acc_m[128:256, :].astype(BF)
+    grad[0:192, :] = natural_lanes(acc_p[0:192, :]).astype(BF)
+    grad[192:320, :] = natural_lanes(acc_m[128:256, :]).astype(BF)
+    grad[320:384, :] = natural_lanes(acc_m[64:128, :]).astype(BF)
 
 
 def imag_first(got):
@@ -196,10 +199,15 @@
 
 
 def middle_kernel(
-    norm, cl, got, tct, tst, tc, ts, unit, pre, cot, w_out, w_out_t,
-    output, d_out, d_joined, sent, grad, got_s, acc_c, acc_s, acc_g,
+    norm, cl, cols, got, tct, tst, tc, ts, unit, pre, w_out, w_out_t, my_col, *refs,
 ):
+    cots = refs[:cols]
+    output, d_out, d_joined, sent, grad, got_s, cot, acc_c, acc_s, acc_g = refs[cols:]
     y = pl.program_id(0)
+    w = cots[0].shape[1]
+    for k in range(cols):
+        at = lax.rem(my_col[0, 0] + (cols - k), cols)
+        cot[pl.ds(pl.multiple_of(at * w, w), w), :] = cots[k][0]
 
     @pl.when(y == 0)
     def _():
@@ -210,7 +218,7 @@
     pre_all = jnp.concatenate([pre[0, :, :cl], pre[0, :, cl:] + dot(joined, w_out[...])], 1)
     slope, silu = slope_and_silu(pre_all)
     output[0] = silu.astype(BF)
-    d = (cot[...].reshape(-1, cot.shape[-1]).astype(F32) * slope).astype(BF)
+    d = (cot[...].astype(F32) * slope).astype(BF)
     d_out[0] = d
     dj = dot(d[:, cl:], w_out_t[...]).astype(BF)
     d_joined[0] = dj
@@ -232,7 +240,8 @@
 
 
 def tail_kernel(
-    norm, cl, got, tct, tst, masked, marked, d_joined, d_conv, w_in, w_in_t, grad_features, grad, got_s, acc_g
+    norm, cl, got, tct, tst, masked, marked, d_joined, d_conv, w_in, w_in_t, grad_freq,
+    grad_features, late, got_s, acc_g,
 ):
     y = pl.program_id(0)
 
@@ -244,7 +253,7 @@
     x = masked[0, :, cl:]
     slope = slope_and_silu(dot(x, w_in[...]))[0]
     du = ((d_joined[0].astype(F32) + back.astype(F32)) * slope).astype(BF)
-    g = dot(x, du, ROWS_OF)
+    g = dot(du, x, ROWS_OF)
 
     @pl.when(y == 0)
     def _():
@@ -260,7 +269,12 @@
 
     @pl.when(y == pl.num_programs(0) - 1)
     def _():
-        grad[...] = acc_g[...].astype(BF)
+        at = 0
+        for part, size in ((grad_freq, 384), (acc_g, 192)):
+            for k in range(3):
+                late[at : at + size, :] = part[0:size, k * 128 : (k + 1) * 128].astype(BF)
+                at += size
+        late[at:, :] = jnp.zeros((late.shape[0] - at, 128), BF)
 
 
 def shifted(x, step):
@@ -294,7 +308,7 @@
     pre[0, :, cl:] = shifted(cross[:, :g], 1) + cross[:, g : 2 * g] + shifted(cross[:, 2 * g :], -1)
 
 
-def conv_grad_kernel(cl, above, masked, below, d_out, g_local, g_cross, pad, acc_l, acc_c):
+def conv_grad_kernel(cl, above, masked, below, d_out, g_out, early, pad, acc_l, acc_c):
     y = pl.program_id(0)
     rows = masked.shape[0]
 
@@ -316,10 +330,29 @@
 
     @pl.when(y == pl.num_programs(0) - 1)
     def _():
+        ch = masked.shape[2]
         for i in range(3):
-            g_local[i] = acc_l[i].astype(BF)
+            early[0, i * ch : (i + 1) * ch, :] = acc_l[i].astype(BF)
             for j in range(3):
-                g_cross[i, j] = acc_c[i, :, j * g : (j + 1) * g].astype(BF)
+                at = (3 * i + j) * cl
+                early[1, at : at + cl, :] = acc_c[i, :, j * g : (j + 1) * g].astype(BF)
+        at, size = 9 * cl, g_out.shape[0]
+        early[1, at : at + size, :] = g_out[...]
+        early[1, at + size :, :] = jnp.zeros((early.shape[1] - at - size, g), BF)
+
+
+def unpack_kernel(cl, got, g_local, g_cross, g_out):
+    rows, ch = got.shape[2], g_local.shape[2]
+    for at in range(0, 3 * ch, 64):
+        block = got[at // rows, 0, at % rows : at % rows + 64, :].astype(F32)
+        for j in range(3):
+            g_local[at // ch, j, at % ch : at % ch + 64, :] = block[:, j * cl : (j + 1) * cl]
+    for at in range(0, 9 * cl + g_out.shape[0], 64):
+        block = got[at // rows, 1, at % rows : at % rows + 64, :].astype(F32)
+        if at < 9 * cl:
+            g_cross[at : at + 64, :] = block
+        else:
+            g_out[at - 9 * cl : at - 9 * cl + 64, :] = block
 
 
 def conv_back_kernel(cl, above, d_out, below, w_local, w_cross, d_conv, pad_l, pad_g):
@@ -348,6 +381,44 @@
     return lax.all_to_all(field.reshape(cols, h // cols, w, c), "col", 0, 0, tiled=True)
 
 
+def turn(field, cols):
+    h, w, c = field.shape
+    blocks = field.reshape(cols, h // cols, w, c)
+    me = lax.axis_index("col")
+    out = []
+    for k in range(cols):
+        part = lax.dynamic_index_in_dim(blocks, (me + k) % cols, 0, keepdims=False)
+        out.append(lax.ppermute(part, "col", [(i, (i + k) % cols) for i in range(cols)]) if k else part)
+    return out
+
+
+def reduce_halves(early, count):
+    pairs = lax.axis_size("row")
+    cols = count // pairs
+    core = lax.axis_index("row") % 2
+    mine = lax.dynamic_index_in_dim(early, core, 0, keepdims=False)
+    other = lax.dynamic_index_in_dim(early, 1 - core, 0, keepdims=False)
+    other = lax.ppermute(other, "row", [(i, i ^ 1) for i in range(pairs)])
+    total = (mine.astype(F32) + other.astype(F32)).astype(BF)
+    groups = [[cols * r + c for r in range(k, pairs, 2) for c in range(cols)] for k in range(2)]
+    got = lax.all_to_all(
+        total.reshape(count // 2, -1, total.shape[-1]), AXES, 0, 0, axis_index_groups=groups, tiled=True
+    )
+    return total, got
+
+
+def gather_halves(x, cols):
+    me = lax.axis_index("col")
+    parts = [x]
+    for k in range(1, cols):
+        parts.append(lax.ppermute(x, "col", [((i + k) % cols, i) for i in range(cols)]))
+    both = jnp.concatenate(parts + parts[:-1], 0)
+    size = x.shape[0]
+    x = lax.dynamic_slice_in_dim(both, (cols - me) % cols * size, cols * size, 0)
+    x = lax.all_gather(x, "row", axis=0)
+    return x.reshape(x.shape[0] // 2, 2, *x.shape[1:])
+
+
 def edges(field, count):
     down = lax.ppermute(field[-1:], AXES, [(i, i + 1) for i in range(count - 1)])
     up = lax.ppermute(field[:1], AXES, [(i + 1, i) for i in range(count - 1)])
@@ -366,6 +437,10 @@
 
 def tie(value, *after):
     return lax.optimization_barrier((value,) + after)[0]
+
+
+def tied(*values):
+    return lax.optimization_barrier(values)
 
 
 def shards(features, hole_mask, cotangent, w_local, w_cross, w_in, w_freq, w_out):
@@ -414,7 +489,11 @@
 
     marked = jnp.where(hole_mask[0][..., None] == 1, HOLE, features[0]).astype(BF)
     marked = to_rows(marked, cols)
-    cot = to_rows(tie(cotangent[0], marked), cols)
+    w_in_d, w_in_t, w_out_z, w_out_t, w_freq_p, w_freq_t, wl, wc, wl_t, wc_t, weight = tied(
+        w_in_d, w_in_t, w_out_z, w_out_t, w_freq_p, w_freq_t, wl, wc, wl_t, wc_t, weight
+    )
+    cots = turn(tie(cotangent[0], marked), cols)
+    my_col = lax.axis_index("col").astype(jnp.int32).reshape(1, 1)
 
     masked, unit, sent = call(
         functools.partial(head_kernel, norm_w, cl),
@@ -425,8 +504,8 @@
         [vm((n, 256), F32), vm((n, 256), F32)],
         flops=4 * n * pix * 256, bytes_=12 << 20,
     )
-    got = swap(sent, count)
     above, below = edges(masked, count)
+    got = tie(swap(sent, count), above, below)
     (pre,) = call(
         functools.partial(conv_kernel, cl),
         "conv",
@@ -445,36 +524,38 @@
         [vm((n, 384), BF)],
         flops=8 * n * n * 384, bytes_=7 << 20,
     )
+    sent, *cots = tied(sent, *cots)
     got = swap(sent, count)
-    cot = tie(cot, got)
     output, d_out, d_joined, sent, grad_out = call(
-        functools.partial(middle_kernel, norm_w, cl),
+        functools.partial(middle_kernel, norm_w, cl, cols),
         "middle",
         (rows,),
         [
             (got, None, None), (tct, back_table, at_y), (tst, back_table, at_y), (tc, line_table, at_y),
-            (ts, line_table, at_y), (unit, one_row(256), at_y), (pre, one_row(ch), at_y), (cot, blocks(ch), at_blocks),
-            (w_out_z, None, None), (w_out_t, None, None),
-        ],
+            (ts, line_table, at_y), (unit, one_row(256), at_y), (pre, one_row(ch), at_y),
+            (w_out_z, None, None), (w_out_t, None, None), (my_col, None, None),
+        ]
+        + [(c, (1, w, ch), at_y) for c in cots],
         [
             (wide, BF, one_row(ch), at_y), (wide, BF, one_row(ch), at_y), ((rows, width, 256), BF, one_row(256), at_y),
             ((n, 384), BF, None, None), ((cs, cg), BF, None, None),
         ],
-        [vm((n, 256), BF), vm((n, 256), F32), vm((n, 256), F32), vm((256, cg), F32)],
+        [vm((n, 256), BF), vm((width, ch), BF), vm((n, 256), F32), vm((n, 256), F32), vm((256, cg), F32)],
         flops=8 * n * pix * 256, bytes_=24 << 20,
     )
     got = swap(sent, count)
-    grad_local, grad_cross = call(
+    d_above, d_below = edges(d_out, count)
+    (early,) = call(
         functools.partial(conv_grad_kernel, cl),
         "conv_grad",
         (rows,),
-        [(above, None, None), (masked, None, None), (below, None, None), (d_out, one_row(ch), at_y)],
-        [((3, ch, 3 * cl), BF, None, None), ((3, 3, cl, cg), BF, None, None)],
+        [(above, None, None), (masked, None, None), (below, None, None), (d_out, one_row(ch), at_y), (grad_out, None, None)],
+        [((2, 3 * ch, 384), BF, None, None)],
         [vm((rows + 2, width, ch), BF), vm((3, ch, 3 * cl), F32), vm((3, cl, 3 * cg), F32)],
         flops=18 * pix * (ch * cl + cl * cg), bytes_=7 << 20,
     )
-    d_above, d_below = edges(d_out, count)
-    got = tie(got, grad_local)
+    total, early = reduce_halves(early, count)
+    got = tied(got, d_above, d_below, total)[0]
     sent, grad_freq = call(
         functools.partial(frequency_back_kernel, norm_h, tile),
         "frequency_back",
@@ -487,11 +568,10 @@
         [vm((n, 384), BF), vm((256, 384), F32), vm((256, 384), F32)],
         flops=8 * n * n * 384, bytes_=8 << 20,
     )
+    early = early.astype(F32).sum(0).astype(BF)
+    sent, early = tied(sent, early)
     got = swap(sent, count)
-    pieces = [grad_local.reshape(-1, 384), grad_cross.reshape(-1, 384), grad_freq, grad_out]
-    sizes = [p.shape[0] for p in pieces]
-    room = -(-sum(sizes) // (16 * count)) * 16 * count
-    early = scatter_sum(jnp.pad(jnp.concatenate(pieces, 0), ((0, room - sum(sizes)), (0, 0))), count)
+    early = gather_halves(early, cols)
     (d_conv,) = call(
         functools.partial(conv_back_kernel, cl),
         "conv_back",
@@ -501,30 +581,35 @@
         [vm((rows + 2, width, 3 * cl), BF), vm((rows + 2, width, 3 * cg), BF)],
         flops=18 * pix * (ch * cl + cl * cg), bytes_=9 << 20,
     )
-    grad_features, grad_in = call(
+    got = tie(got, d_conv)
+    late_rows = -(-(3 * 384 + 3 * cs) // (16 * count)) * 16 * count
+    grad_features, late = call(
         functools.partial(tail_kernel, norm_w, cl),
         "tail",
         (rows,),
         [
             (got, None, None), (tct, back_table, at_y), (tst, back_table, at_y), (masked, one_row(ch), at_y),
             (marked, blocks(128), at_blocks), (d_joined, one_row(256), at_y), (d_conv, one_row(ch), at_y),
-            (w_in_d, None, None), (w_in_t, None, None),
+            (w_in_d, None, None), (w_in_t, None, None), (grad_freq, None, None),
         ],
-        [(wide, BF, one_row(ch), at_y), ((cg, 256), BF, None, None)],
-        [vm((n, 256), BF), vm((cg, 256), F32)],
+        [(wide, BF, one_row(ch), at_y), ((late_rows, 128), BF, None, None)],
+        [vm((n, 256), BF), vm((256, cg), F32)],
         flops=4 * n * pix * 256, bytes_=16 << 20,
     )
-    early = gather(early, count)
-    outs, at = [], 0
-    for size in sizes:
-        outs.append(early[at : at + size].astype(F32))
-        at += size
-    grad_local, grad_cross, grad_freq, grad_out = outs
-    late = gather(scatter_sum(grad_in[:, :cs].reshape(-1, 128), count), count)
-    grad_in = late.reshape(cg, cs).astype(F32)
-    grad_local = jnp.transpose(grad_local.reshape(3, ch, 3, cl), (0, 2, 1, 3))
+    late = scatter_sum(late, count)
+    grad_local, grad_cross, grad_out = call(
+        functools.partial(unpack_kernel, cl),
+        "unpack",
+        (1,),
+        [(early, None, None)],
+        [((3, 3, ch, cl), F32, None, None), ((9 * cl, cg), F32, None, None), ((cs, cg), F32, None, None)],
+        flops=1, bytes_=7 << 20,
+    )
+    late = gather(late, count)
+    grad_freq = jnp.concatenate([late[k * 384 : (k + 1) * 384] for k in range(3)], 1).astype(F32)
+    at = 3 * 384
+    grad_in = jnp.concatenate([late[at + k * cs : at + (k + 1) * cs] for k in range(3)], 1).astype(F32).T
     grad_cross = grad_cross.reshape(3, 3, cl, cg)
-    grad_freq = unpack_dim(unpack_dim(grad_freq, 0, cs), 1, cs)
     return output[None], grad_features[None], grad_local, grad_cross, grad_in, grad_freq, grad_out
 
 

time: 370 us -> 303 us (0.82)
  waiting for transfers between devices: 144 us -> 57.7 us
  blocking collectives: 0 us -> 34.1 us
  between operations: 1.06 us -> 14.5 us
  starting transfers between devices: 77.6 us -> 64.2 us
  other arithmetic: 22.4 us -> 9.89 us
  local copies, waits for them, and re-layouts: 33.2 us -> 25.9 us
  Pallas kernels: 90.2 us -> 95.5 us
    all_to_all x4 -> x1, waiting for transfers between devices: 89.6 us -> 0.01 us  [reduce_halves(): lax.all_to_all(total.reshape(count // 2, -1, total.shape[-1]), AXES, 0, 0...]
    all_to_all x0 -> x2, blocking collectives: none -> 34.1 us  [the longest x1 17.5 us: scatter_sum(): lax.all_to_all(x.reshape(count, -1, x.shape[-1]), AXES, 0, 0, tiled=True)]
    all_to_all x4 -> x1, starting transfers between devices: 26.5 us -> 3.94 us  [reduce_halves(): lax.all_to_all(total.reshape(count // 2, -1, total.shape[-1]), AXES, 0, 0...]
    all_to_all x2 -> x1, waiting for transfers between devices: 26.4 us -> 7.32 us  [to_rows(): lax.all_to_all(field.reshape(cols, h // cols, w, c), 'col', 0, 0, tiled=T...]
    concatenate x3 -> x0, other arithmetic: 12.6 us -> none  [the longest x1 11.5 us: shards(): jnp.concatenate(pieces, 0)]
    ppermute x2, waiting for transfers between devices: 8.14 us -> 18.9 us  [edges(): lax.ppermute(field[-1:], AXES, [(i, i + 1) for i in range(count - 1)])]
    ppermute x0 -> x7, waiting for transfers between devices: none -> 8.8 us  [the longest x3 4.97 us: turn(): lax.ppermute(part, 'col', [(i, (i + k) % cols) for i in range(cols)])]
    all_to_all x4, starting transfers between devices: 29.1 us -> 35.6 us  [swap(): lax.all_to_all(x.reshape(count, -1, x.shape[-1]), AXES, 0, 0, tiled=True)]
  transfers between devices with their start and end apart: 14 -> 18, of which waited for: 9 -> 10; matrix products, arithmetic and copies ran while one was open for 9% -> 8% of each run, Pallas kernels for 11% -> 18%
where the time goes in v1:
time: 303 us; the launch traced here: 302 us
  Pallas kernels  95.5 us (32%)
  starting transfers between devices  64.2 us (21%)
  waiting for transfers between devices  57.7 us (19%)
  blocking collectives  34.1 us (11%)
  local copies, waits for them, and re-layouts  25.9 us (9%)
  between operations  14.5 us (5%)
  other arithmetic  9.89 us (3%)
    pallas_call x9, Pallas kernels, call(): pl.pallas_call(body, grid=grid, in_specs=[spec(a.shape, block, index) for...  95.5 us
    all_to_all x4, starting transfers between devices, swap(): lax.all_to_all(x.reshape(count, -1, x.shape[-1]), AXES, 0, 0, tiled=True)  35.6 us
    all_to_all x4, waiting for transfers between devices, swap(): lax.all_to_all(x.reshape(count, -1, x.shape[-1]), AXES, 0, 0, tiled=True)  22.7 us
    ppermute x2, waiting for transfers between devices, edges(): lax.ppermute(field[-1:], AXES, [(i, i + 1) for i in range(count - 1)])  18.9 us
    all_to_all x1, blocking collectives, scatter_sum(): lax.all_to_all(x.reshape(count, -1, x.shape[-1]), AXES, 0, 0, tiled=True)  17.5 us
    all_to_all x1, blocking collectives, gather(): lax.all_to_all(jnp.broadcast_to(x[None], (count,) + x.shape), AXES, 0, 0,...  16.6 us
    unnamed x63, local copies, waits for them, and re-layouts  7.87 us
    ppermute x2, starting transfers between devices, edges(): up = lax.ppermute(field[:1], AXES, [(i + 1, i) for i in range(count - 1)])  7.37 us
  transfers between devices with their start and end apart: 18, of which 10 were waited for; matrix products, arithmetic and copies ran while one was open for 8% of the time, Pallas kernels for 18%

profile of v1, /device:TPU:1, one launch (start us, length us, event | category | flops | bytes accessed | tf_op | source)
XLA Modules:
  0.0 301.8 jit_solution(2939155940324572723)
XLA Ops:
  10.8 5.0 %all-to-all-start = ((bf16[4,5,80,512]{3,2,1,0:T(8,128)(2,1)}), bf16[4,5,80,512]{3,2,1,0:T(8,128)(2,1)S(1)}, u32[]{:S(2)}, u32[]{:S(2)}) async-start(bf16[4,5,80,512]{3,2,1,0:T(8,128)(2,1)} %broadcast_select_fusion), calls=%async_computation | async-start | bytes 3276800 | tf_op jit(solution)/shard_map/all_to_all | solution.py:381
  29.0 7.3 %all-to-all-done.marked = bf16[4,5,80,512]{3,2,1,0:T(8,128)(2,1)S(1)} async-done(((bf16[4,5,80,512]{3,2,1,0:T(8,128)(2,1)}), bf16[4,5,80,512]{3,2,1,0:T(8,128)(2,1)S(1)}, u32[]{:S(2)}, u32[]{:S(2)}) %all-to-all-start) | async-done | bytes 1638432 | tf_op jit(solution)/shard_map/all_to_all | solution.py:381
  37.5 9.5 %head.1 = (bf16[5,320,512]{2,1,0:T(8,128)(2,1)}, bf16[5,320,256]{2,1,0:T(8,128)(2,1)}, bf16[1024,384]{1,0:T(8,128)(2,1)}) custom-call(bf16[4,5,80,512]{3,2,1,0:T(8,128)(2,1)} %copy-done, bf16[384,256]{1,0:T(8,128)(2,1)} %pad_maximum_fusion.1.w_in, bf16[5,1024,320]{2,1,0:T(8,128)(2,1)} %constant.115.clone.tc, bf16[5,1024,320]{2,1,0:T(8,128)(2,1)} %constant.116.clone.ts), custom_call_target="tpu_custom_call" | custom-call | flops 1677721600 | bytes 12582912 | tf_op jit(solution)/shard_map/head/pallas_call | solution.py:96
  47.0 9.5 %all-to-all-start.1 = ((bf16[64,16,384]{2,1,0:T(8,128)(2,1)}), bf16[64,16,384]{2,1,0:T(8,128)(2,1)S(1)}, u32[]{:S(2)}, u32[]{:S(2)}) async-start(bf16[64,16,384]{2,1,0:T(8,128)(2,1)} %bitcast.69), calls=%async_computation.1 | async-start | bytes 1572864 | tf_op jit(solution)/shard_map/all_to_all | solution.py:376
  72.0 4.0 %collective-permute-done.above = bf16[1,320,512]{2,1,0:T(8,128)(2,1)} collective-permute-done((bf16[1,320,512]{2,1,0:T(8,128)(2,1)}, bf16[1,320,512]{2,1,0:T(8,128)(2,1)}, u32[]{:S(2)}, u32[]{:S(2)}) %collective-permute-start) | collective-permute-done | bytes 327712 | tf_op jit(solution)/shard_map/ppermute | solution.py:423
  76.8 11.2 %frequency.1 = (bf16[1024,384]{1,0:T(8,128)(2,1)}, bf16[1024,384]{1,0:T(8,128)(2,1)}) custom-call(bf16[1024,384]{1,0:T(8,128)(2,1)} %bitcast.68, bf16[1024,1024]{1,0:T(8,128)(2,1)} %constant.117.clone.tc, bf16[1024,1024]{1,0:T(8,128)(2,1)} %constant.118.clone.ts, bf16[384,384]{1,0:T(8,128)(2,1)} %copy.46.w_freq, f32[1024,1]{1,0:T(8,128)} %copy.47.weight, ...), custom_call_target="tpu_custom_call" | custom-call | flops 3221225472 | bytes 7340032 | tf_op jit(solution)/shard_map/frequency/pallas_call | solution.py:96
  88.1 5.0 %collective-permute-done.3.refs_2_ = bf16[5,80,512]{2,1,0:T(8,128)(2,1)S(1)} collective-permute-done((bf16[5,80,512]{2,1,0:T(8,128)(2,1)}, bf16[5,80,512]{2,1,0:T(8,128)(2,1)S(1)}, u32[]{:S(2)}, u32[]{:S(2)}) %collective-permute-start.3) | collective-permute-done | bytes 409632 | tf_op jit(solution)/shard_map/ppermute | solution.py:391
  93.8 12.3 %all-to-all-start.2 = ((bf16[64,16,384]{2,1,0:T(8,128)(2,1)}), bf16[64,16,384]{2,1,0:T(8,128)(2,1)S(1)}, u32[]{:S(2)}, u32[]{:S(2)}) async-start(bf16[64,16,384]{2,1,0:T(8,128)(2,1)} %bitcast.70), calls=%async_computation.2 | async-start | bytes 1572864 | tf_op jit(solution)/shard_map/all_to_all | solution.py:376
  107.6 8.7 %conv.1.pre = f32[5,320,512]{2,1,0:T(8,128)} custom-call(bf16[1,320,512]{2,1,0:T(8,128)(2,1)} %collective-permute-done.above, bf16[5,320,512]{2,1,0:T(8,128)(2,1)} %get-tuple-element.48.masked, bf16[1,320,512]{2,1,0:T(8,128)(2,1)} %collective-permute-done.1.below, bf16[3,512,384]{2,1,0:T(8,128)(2,1)} %copy.48.w_local, bf16[384,1152]{1,0:T(8,128)(2,1)} %bitcast.67), custom_call_target="tpu_custom_call" | custom-call | flops 3303014400 | bytes 9437184 | tf_op jit(solution)/shard_map/conv/pallas_call | solution.py:96
  116.3 5.2 %all-to-all-done.2 = bf16[64,16,384]{2,1,0:T(8,128)(2,1)S(1)} async-done(((bf16[64,16,384]{2,1,0:T(8,128)(2,1)}), bf16[64,16,384]{2,1,0:T(8,128)(2,1)S(1)}, u32[]{:S(2)}, u32[]{:S(2)}) %all-to-all-start.2) | async-done | bytes 786464 | tf_op jit(solution)/shard_map/all_to_all | solution.py:376
  122.4 15.8 %middle.1 = (bf16[5,320,512]{2,1,0:T(8,128)(2,1)}, bf16[5,320,512]{2,1,0:T(8,128)(2,1)}, bf16[5,320,256]{2,1,0:T(8,128)(2,1)}, bf16[1024,384]{1,0:T(8,128)(2,1)}, bf16[192,384]{1,0:T(8,128)(2,1)}) custom-call(bf16[1024,384]{1,0:T(8,128)(2,1)} %bitcast.59, bf16[5,320,1024]{2,1,0:T(8,128)(2,1)} %constant.113.clone.tct, ...), custom_call_target="tpu_custom_call" | custom-call | flops 3355443200 | bytes 25165824 | tf_op jit(solution)/shard_map/middle/pallas_call | solution.py:96
  138.2 11.1 %conv_grad.1 = bf16[2,1536,384]{2,1,0:T(8,128)(2,1)} custom-call(bf16[1,320,512]{2,1,0:T(8,128)(2,1)} %collective-permute-done.above, bf16[5,320,512]{2,1,0:T(8,128)(2,1)} %get-tuple-element.48.masked, bf16[1,320,512]{2,1,0:T(8,128)(2,1)} %collective-permute-done.1.below, bf16[5,320,512]{2,1,0:T(8,128)(2,1)} %get-tuple-element.66.d_out, ...), custom_call_target="tpu_custom_call" | custom-call | flops 3303014400 | bytes 7340032 | tf_op jit(solution)/shard_map/conv_grad/pallas_call | solution.py:96
  151.5 5.0 %all-to-all-start.3 = ((bf16[64,16,384]{2,1,0:T(8,128)(2,1)}), bf16[64,16,384]{2,1,0:T(8,128)(2,1)}, u32[]{:S(2)}, u32[]{:S(2)}) async-start(bf16[64,16,384]{2,1,0:T(8,128)(2,1)} %bitcast.71), calls=%async_computation.3 | async-start | bytes 1572864 | tf_op jit(solution)/shard_map/all_to_all | solution.py:376
  159.2 12.7 %all-to-all-done.3 = bf16[64,16,384]{2,1,0:T(8,128)(2,1)} async-done(((bf16[64,16,384]{2,1,0:T(8,128)(2,1)}), bf16[64,16,384]{2,1,0:T(8,128)(2,1)}, u32[]{:S(2)}, u32[]{:S(2)}) %all-to-all-start.3) | async-done | bytes 786464 | tf_op jit(solution)/shard_map/all_to_all | solution.py:376
  171.8 3.9 %all-to-all-start.4 = ((bf16[32,48,384]{2,1,0:T(8,128)(2,1)}), bf16[32,48,384]{2,1,0:T(8,128)(2,1)S(1)}, u32[]{:S(2)}, u32[]{:S(2)}) async-start(bf16[32,48,384]{2,1,0:T(8,128)(2,1)} %bitcast.27), calls=%async_computation.4 | async-start | bytes 2359296 | tf_op jit(solution)/shard_map/all_to_all | solution.py:404
  180.0 3.9 %collective-permute-start.6 = (bf16[1,320,512]{2,1,0:T(8,128)(2,1)S(1)}, bf16[1,320,512]{2,1,0:T(8,128)(2,1)S(1)}, u32[]{:S(2)}, u32[]{:S(2)}) collective-permute-start(bf16[1,320,512]{2,1,0:T(8,128)(2,1)S(1)} %get-tuple-element.85), channel_id=1, source_target_pairs={{1,0},{2,1},{3,2},{4,3},{5,4},{6,5},{7,6},{8,7},{9,8},{10,9},{11,1... | collective-permute-start | bytes 983048 | tf_op jit(solution)/shard_map/ppermute | solution.py:424
  183.9 14.9 %collective-permute-done.5.above = bf16[1,320,512]{2,1,0:T(8,128)(2,1)S(1)} collective-permute-done((bf16[1,320,512]{2,1,0:T(8,128)(2,1)S(1)}, bf16[1,320,512]{2,1,0:T(8,128)(2,1)S(1)}, u32[]{:S(2)}, u32[]{:S(2)}) %collective-permute-start.5) | collective-permute-done | bytes 327712 | tf_op jit(solution)/shard_map/ppermute | solution.py:423
  198.8 13.7 %frequency_back.1 = (bf16[1024,384]{1,0:T(8,128)(2,1)}, bf16[384,384]{1,0:T(8,128)(2,1)}) custom-call(bf16[1024,384]{1,0:T(8,128)(2,1)} %bitcast.24.got, bf16[1024,1024]{1,0:T(8,128)(2,1)} %constant.117.clone.tc, bf16[1024,1024]{1,0:T(8,128)(2,1)} %constant.118.clone.ts, bf16[384,384]{1,0:T(8,128)(2,1)} %copy.46.w_freq, bf16[384,384]{1,0:T(8,128)(2,1)} %bitcast.64, ...), custom_call_target="tpu_custom_call" | custom-call | flops 3221225472 | bytes 8388608 | tf_op jit(solution)/shard_map/frequency_back/pallas_call | solution.py:96
  219.1 8.7 %all-to-all-start.5 = ((bf16[64,16,384]{2,1,0:T(8,128)(2,1)}), bf16[64,16,384]{2,1,0:T(8,128)(2,1)S(1)}, u32[]{:S(2)}, u32[]{:S(2)}) async-start(bf16[64,16,384]{2,1,0:T(8,128)(2,1)} %bitcast.28), calls=%async_computation.5 | async-start | bytes 1572864 | tf_op jit(solution)/shard_map/all_to_all | solution.py:376
  227.9 10.6 %conv_back.1.d_conv = f32[5,320,512]{2,1,0:T(8,128)} custom-call(bf16[1,320,512]{2,1,0:T(8,128)(2,1)} %copy-done.23, bf16[5,320,512]{2,1,0:T(8,128)(2,1)} %get-tuple-element.66.d_out, bf16[1,320,512]{2,1,0:T(8,128)(2,1)} %copy-done.24, bf16[3,384,512]{2,1,0:T(8,128)(2,1)} %bitcast.65, bf16[3,1152,128]{2,1,0:T(8,128)(2,1)} %bitcast.66), custom_call_target="tpu_custom_call" | custom-call | flops 3303014400 | bytes 9437184 | tf_op jit(solution)/shard_map/conv_back/pallas_call | solution.py:96
  238.5 4.8 %all-to-all-done.5 = bf16[64,16,384]{2,1,0:T(8,128)(2,1)S(1)} async-done(((bf16[64,16,384]{2,1,0:T(8,128)(2,1)}), bf16[64,16,384]{2,1,0:T(8,128)(2,1)S(1)}, u32[]{:S(2)}, u32[]{:S(2)}) %all-to-all-start.5) | async-done | bytes 786464 | tf_op jit(solution)/shard_map/all_to_all | solution.py:376
  244.2 11.0 %tail.1 = (bf16[5,320,512]{2,1,0:T(8,128)(2,1)}, bf16[2048,128]{1,0:T(8,128)(2,1)}) custom-call(bf16[1024,384]{1,0:T(8,128)(2,1)} %bitcast.60, bf16[5,320,1024]{2,1,0:T(8,128)(2,1)} %constant.113.clone.tct, bf16[5,320,1024]{2,1,0:T(8,128)(2,1)} %constant.114.clone.tst, bf16[5,320,512]{2,1,0:T(8,128)(2,1)} %get-tuple-element.48.masked, ...), custom_call_target="tpu_custom_call" | custom-call | flops 1677721600 | bytes 16777216 | tf_op jit(solution)/shard_map/tail/pallas_call | solution.py:96
  255.2 17.5 %all_to_all.40 = bf16[64,32,128]{2,1,0:T(8,128)(2,1)S(1)} all-to-all(bf16[64,32,128]{2,1,0:T(8,128)(2,1)} %bitcast.73), channel_id=1, replica_groups=mesh['dp'=2,'row'=16,'col'=4] {'row','col'}, dimensions={0} | all-to-all | bytes 1048576 | tf_op jit(solution)/shard_map/all_to_all | solution.py:429
  272.9 16.6 %all_to_all.41 = bf16[64,32,128]{2,1,0:T(8,128)(2,1)S(1)} all-to-all(bf16[64,32,128]{2,1,0:T(8,128)(2,1)S(1)} %broadcast_in_dim.43), channel_id=1, replica_groups=mesh['dp'=2,'row'=16,'col'=4] {'row','col'}, dimensions={0} | all-to-all | bytes 1048576 | tf_op jit(solution)/shard_map/all_to_all | solution.py:434
  (130 shorter events, 59.3 us)
Async XLA Ops:
  10.8 25.5 %all-to-all-start = ((bf16[4,5,80,512]{3,2,1,0:T(8,128)(2,1)}), bf16[4,5,80,512]{3,2,1,0:T(8,128)(2,1)S(1)}, u32[]{:S(2)}, u32[]{:S(2)}) async-start(bf16[4,5,80,512]{3,2,1,0:T(8,128)(2,1)} %broadcast_select_fusion), calls=%async_computation | async-start | bytes 3276800 | tf_op jit(solution)/shard_map/all_to_all | solution.py:381
  29.0 42.1 %copy-start.11 = (bf16[384,384]{0,1:T(8,128)(2,1)}, bf16[384,384]{0,1:T(8,128)(2,1)S(1)}, u32[]{:S(2)}) copy-start(bf16[384,384]{0,1:T(8,128)(2,1)S(1)} %fusion.11) | copy-start | bytes 884740
  47.0 18.3 %copy-start.6 = (bf16[1,20,80,512]{3,2,1,0:T(8,128)(2,1)S(1)}, bf16[1,20,80,512]{3,2,1,0:T(8,128)(2,1)}, u32[]{:S(2)}) copy-start(bf16[1,20,80,512]{3,2,1,0:T(8,128)(2,1)} %param.17) | copy-start | bytes 4915204
  47.0 28.9 %all-to-all-start.1 = ((bf16[64,16,384]{2,1,0:T(8,128)(2,1)}), bf16[64,16,384]{2,1,0:T(8,128)(2,1)S(1)}, u32[]{:S(2)}, u32[]{:S(2)}) async-start(bf16[64,16,384]{2,1,0:T(8,128)(2,1)} %bitcast.69), calls=%async_computation.1 | async-start | bytes 1572864 | tf_op jit(solution)/shard_map/all_to_all | solution.py:376
  58.5 17.4 %collective-permute-start = (bf16[1,320,512]{2,1,0:T(8,128)(2,1)}, bf16[1,320,512]{2,1,0:T(8,128)(2,1)}, u32[]{:S(2)}, u32[]{:S(2)}) collective-permute-start(bf16[1,320,512]{2,1,0:T(8,128)(2,1)} %get-tuple-element.92), channel_id=1, source_target_pairs={{0,1},{1,2},{2,3},{3,4},{4,5},{5,6},{6,7},{7,8},{8,9},{9,10},{10,1... | collective-permute-start | bytes 983048 | tf_op jit(solution)/shard_map/ppermute | solution.py:423
  61.8 14.1 %collective-permute-start.1 = (bf16[1,320,512]{2,1,0:T(8,128)(2,1)}, bf16[1,320,512]{2,1,0:T(8,128)(2,1)}, u32[]{:S(2)}, u32[]{:S(2)}) collective-permute-start(bf16[1,320,512]{2,1,0:T(8,128)(2,1)} %get-tuple-element.91), channel_id=1, source_target_pairs={{1,0},{2,1},{3,2},{4,3},{5,4},{6,5},{7,6},{8,7},{9,8},{10,9},{11,1... | collective-permute-start | bytes 983048 | tf_op jit(solution)/shard_map/ppermute | solution.py:424
  66.6 21.5 %collective-permute-start.2 = (bf16[5,80,512]{2,1,0:T(8,128)(2,1)}, bf16[5,80,512]{2,1,0:T(8,128)(2,1)S(1)}, u32[]{:S(2)}, u32[]{:S(2)}) collective-permute-start(bf16[5,80,512]{2,1,0:T(8,128)(2,1)} %get-tuple-element.89), channel_id=1, source_target_pairs={{0,1},{1,2},{2,3},{3,0},{4,5},{5,6},{6,7},{7,4},{8,9},{9,10},{10,1... | collective-permute-start | bytes 1228808 | tf_op jit(solution)/shard_map/ppermute | solution.py:391
  66.6 26.5 %collective-permute-start.3 = (bf16[5,80,512]{2,1,0:T(8,128)(2,1)}, bf16[5,80,512]{2,1,0:T(8,128)(2,1)S(1)}, u32[]{:S(2)}, u32[]{:S(2)}) collective-permute-start(bf16[5,80,512]{2,1,0:T(8,128)(2,1)} %get-tuple-element.88), channel_id=1, source_target_pairs={{0,2},{1,3},{2,0},{3,1},{4,6},{5,7},{6,4},{7,5},{8,10},{9,11},{10,... | collective-permute-start | bytes 1228808 | tf_op jit(solution)/shard_map/ppermute | solution.py:391
  68.8 24.2 %collective-permute-start.4 = (bf16[5,80,512]{2,1,0:T(8,128)(2,1)}, bf16[5,80,512]{2,1,0:T(8,128)(2,1)S(1)}, u32[]{:S(2)}, u32[]{:S(2)}) collective-permute-start(bf16[5,80,512]{2,1,0:T(8,128)(2,1)} %get-tuple-element.87), channel_id=1, source_target_pairs={{0,3},{1,0},{2,1},{3,2},{4,7},{5,4},{6,5},{7,6},{8,11},{9,8},{10,9... | collective-permute-start | bytes 1228808 | tf_op jit(solution)/shard_map/ppermute | solution.py:391
  88.0 18.1 %copy-start.2 = (bf16[3,3,512,128]{2,3,1,0:T(8,128)(2,1)S(1)}, bf16[3,3,512,128]{2,3,1,0:T(8,128)(2,1)}, u32[]{:S(2)}) copy-start(bf16[3,3,512,128]{2,3,1,0:T(8,128)(2,1)} %copy.42) | copy-start | bytes 3538948
  88.0 19.6 %copy-start.20 = (bf16[5,80,512]{2,1,0:T(8,128)(2,1)}, bf16[5,80,512]{2,1,0:T(8,128)(2,1)S(1)}, u32[]{:S(2)}) copy-start(bf16[5,80,512]{2,1,0:T(8,128)(2,1)S(1)} %collective-permute-done.2.refs_1_) | copy-start | bytes 1228804
  93.0 14.6 %copy-start.21 = (bf16[5,80,512]{2,1,0:T(8,128)(2,1)}, bf16[5,80,512]{2,1,0:T(8,128)(2,1)S(1)}, u32[]{:S(2)}) copy-start(bf16[5,80,512]{2,1,0:T(8,128)(2,1)S(1)} %collective-permute-done.3.refs_2_) | copy-start | bytes 1228804
  93.8 27.7 %all-to-all-start.2 = ((bf16[64,16,384]{2,1,0:T(8,128)(2,1)}), bf16[64,16,384]{2,1,0:T(8,128)(2,1)S(1)}, u32[]{:S(2)}, u32[]{:S(2)}) async-start(bf16[64,16,384]{2,1,0:T(8,128)(2,1)} %bitcast.70), calls=%async_computation.2 | async-start | bytes 1572864 | tf_op jit(solution)/shard_map/all_to_all | solution.py:376
  150.8 5.7 %collective-permute-start.7 = (bf16[1536,384]{1,0:T(8,128)(2,1)S(1)}, bf16[1536,384]{1,0:T(8,128)(2,1)}, u32[]{:S(2)}, u32[]{:S(2)}) collective-permute-start(bf16[1536,384]{1,0:T(8,128)(2,1)S(1)} %dynamic-slice_bitcast_fusion), channel_id=1, source_target_pairs={{0,4},{4,0},{8,12},{12,8},{16,20},{20,16},{24,28},{28,24},{32,36},... | collective-permute-start | bytes 3538952 | tf_op jit(solution)/shard_map/ppermute | solution.py:401
  151.5 20.3 %all-to-all-start.3 = ((bf16[64,16,384]{2,1,0:T(8,128)(2,1)}), bf16[64,16,384]{2,1,0:T(8,128)(2,1)}, u32[]{:S(2)}, u32[]{:S(2)}) async-start(bf16[64,16,384]{2,1,0:T(8,128)(2,1)} %bitcast.71), calls=%async_computation.3 | async-start | bytes 1572864 | tf_op jit(solution)/shard_map/all_to_all | solution.py:376
  171.8 40.7 %all-to-all-start.4 = ((bf16[32,48,384]{2,1,0:T(8,128)(2,1)}), bf16[32,48,384]{2,1,0:T(8,128)(2,1)S(1)}, u32[]{:S(2)}, u32[]{:S(2)}) async-start(bf16[32,48,384]{2,1,0:T(8,128)(2,1)} %bitcast.27), calls=%async_computation.4 | async-start | bytes 2359296 | tf_op jit(solution)/shard_map/all_to_all | solution.py:404
  175.8 115.3 %all-gather.3.cloned.1.call-start = ((), (), s32[]{:S(2)}) async-start(), calls=%async_computation.8 | async-start | bytes 2506752 | tf_op jit(solution)/shard_map/all_gather | solution.py:418
  176.9 21.9 %collective-permute-start.5 = (bf16[1,320,512]{2,1,0:T(8,128)(2,1)S(1)}, bf16[1,320,512]{2,1,0:T(8,128)(2,1)S(1)}, u32[]{:S(2)}, u32[]{:S(2)}) collective-permute-start(bf16[1,320,512]{2,1,0:T(8,128)(2,1)S(1)} %get-tuple-element.86), channel_id=1, source_target_pairs={{0,1},{1,2},{2,3},{3,4},{4,5},{5,6},{6,7},{7,8},{8,9},{9,10},{10,1... | collective-permute-start | bytes 983048 | tf_op jit(solution)/shard_map/ppermute | solution.py:423
  180.0 18.9 %collective-permute-start.6 = (bf16[1,320,512]{2,1,0:T(8,128)(2,1)S(1)}, bf16[1,320,512]{2,1,0:T(8,128)(2,1)S(1)}, u32[]{:S(2)}, u32[]{:S(2)}) collective-permute-start(bf16[1,320,512]{2,1,0:T(8,128)(2,1)S(1)} %get-tuple-element.85), channel_id=1, source_target_pairs={{1,0},{2,1},{3,2},{4,3},{5,4},{6,5},{7,6},{8,7},{9,8},{10,9},{11,1... | collective-permute-start | bytes 983048 | tf_op jit(solution)/shard_map/ppermute | solution.py:424
  198.8 13.7 %copy-start.23 = (bf16[1,320,512]{2,1,0:T(8,128)(2,1)}, bf16[1,320,512]{2,1,0:T(8,128)(2,1)S(1)}, u32[]{:S(2)}) copy-start(bf16[1,320,512]{2,1,0:T(8,128)(2,1)S(1)} %collective-permute-done.5.above) | copy-start | bytes 983044
  212.7 3.2 %collective-permute-start.8 = (bf16[48,384]{1,0:T(8,128)(2,1)S(1)}, bf16[48,384]{1,0:T(8,128)(2,1)S(1)}, u32[]{:S(2)}, u32[]{:S(2)}) collective-permute-start(bf16[48,384]{1,0:T(8,128)(2,1)S(1)} %reduce_sum.24), channel_id=1, source_target_pairs={{1,0},{2,1},{3,2},{0,3},{5,4},{6,5},{7,6},{4,7},{9,8},{10,9},{11,1... | collective-permute-start | bytes 110600 | tf_op jit(solution)/shard_map/ppermute | solution.py:414
  213.8 4.4 %collective-permute-start.9 = (bf16[48,384]{1,0:T(8,128)(2,1)S(1)}, bf16[48,384]{1,0:T(8,128)(2,1)S(1)}, u32[]{:S(2)}, u32[]{:S(2)}) collective-permute-start(bf16[48,384]{1,0:T(8,128)(2,1)S(1)} %reduce_sum.24), channel_id=1, source_target_pairs={{2,0},{3,1},{0,2},{1,3},{6,4},{7,5},{4,6},{5,7},{10,8},{11,9},{8,1... | collective-permute-start | bytes 110600 | tf_op jit(solution)/shard_map/ppermute | solution.py:414
  213.8 4.5 %collective-permute-start.10 = (bf16[48,384]{1,0:T(8,128)(2,1)S(1)}, bf16[48,384]{1,0:T(8,128)(2,1)S(1)}, u32[]{:S(2)}, u32[]{:S(2)}) collective-permute-start(bf16[48,384]{1,0:T(8,128)(2,1)S(1)} %reduce_sum.24), channel_id=1, source_target_pairs={{3,0},{0,1},{1,2},{2,3},{7,4},{4,5},{5,6},{6,7},{11,8},{8,9},{9,10... | collective-permute-start | bytes 110600 | tf_op jit(solution)/shard_map/ppermute | solution.py:414
  219.1 24.2 %all-to-all-start.5 = ((bf16[64,16,384]{2,1,0:T(8,128)(2,1)}), bf16[64,16,384]{2,1,0:T(8,128)(2,1)S(1)}, u32[]{:S(2)}, u32[]{:S(2)}) async-start(bf16[64,16,384]{2,1,0:T(8,128)(2,1)} %bitcast.28), calls=%async_computation.5 | async-start | bytes 1572864 | tf_op jit(solution)/shard_map/all_to_all | solution.py:376
  (24 other events, 89.1 us)
Sparse Core Ops, SparseCore 0:
  219.2 41.8 all-gather.2

commit v2 on v1

--- a/solution.py
+++ b/solution.py
@@ -240,8 +240,7 @@
 
 
 def tail_kernel(
-    norm, cl, got, tct, tst, masked, marked, d_joined, d_conv, w_in, w_in_t, grad_freq,
-    grad_features, late, got_s, acc_g,
+    norm, cl, got, tct, tst, masked, d_joined, w_in, grad_freq, d_unit, late, got_s, acc_g
 ):
     y = pl.program_id(0)
 
@@ -263,9 +262,7 @@
     def _():
         acc_g[...] += g
 
-    keep = marked[...].reshape(-1, marked.shape[-1])[:, :1].astype(F32) < 0.5 * HOLE
-    total = jnp.concatenate([d_conv[0, :, :cl], d_conv[0, :, cl:] + dot(du, w_in_t[...])], 1)
-    grad_features[0] = jnp.where(keep, total, 0.0).astype(BF)
+    d_unit[0] = du
 
     @pl.when(y == pl.num_programs(0) - 1)
     def _():
@@ -275,6 +272,12 @@
                 late[at : at + size, :] = part[0:size, k * 128 : (k + 1) * 128].astype(BF)
                 at += size
         late[at:, :] = jnp.zeros((late.shape[0] - at, 128), BF)
+
+
+def finish_kernel(cl, marked, d_unit, d_conv, w_in_t, grad_features):
+    keep = marked[...].reshape(-1, marked.shape[-1])[:, :1].astype(F32) < 0.5 * HOLE
+    total = jnp.concatenate([d_conv[0, :, :cl], d_conv[0, :, cl:] + dot(d_unit[0], w_in_t[...])], 1)
+    grad_features[0] = jnp.where(keep, total, 0.0).astype(BF)
 
 
 def shifted(x, step):
@@ -392,19 +395,22 @@
     return out
 
 
-def reduce_halves(early, count):
+def core_sum(early):
     pairs = lax.axis_size("row")
-    cols = count // pairs
     core = lax.axis_index("row") % 2
     mine = lax.dynamic_index_in_dim(early, core, 0, keepdims=False)
     other = lax.dynamic_index_in_dim(early, 1 - core, 0, keepdims=False)
     other = lax.ppermute(other, "row", [(i, i ^ 1) for i in range(pairs)])
-    total = (mine.astype(F32) + other.astype(F32)).astype(BF)
+    return (mine.astype(F32) + other.astype(F32)).astype(BF)
+
+
+def scatter_half(total, count):
+    pairs = lax.axis_size("row")
+    cols = count // pairs
     groups = [[cols * r + c for r in range(k, pairs, 2) for c in range(cols)] for k in range(2)]
-    got = lax.all_to_all(
+    return lax.all_to_all(
         total.reshape(count // 2, -1, total.shape[-1]), AXES, 0, 0, axis_index_groups=groups, tiled=True
     )
-    return total, got
 
 
 def gather_halves(x, cols):
@@ -554,8 +560,9 @@
         [vm((rows + 2, width, ch), BF), vm((3, ch, 3 * cl), F32), vm((3, cl, 3 * cg), F32)],
         flops=18 * pix * (ch * cl + cl * cg), bytes_=7 << 20,
     )
-    total, early = reduce_halves(early, count)
-    got = tied(got, d_above, d_below, total)[0]
+    got, early = tied(got, early)
+    got, total, d_above, d_below = tied(got, core_sum(early), d_above, d_below)
+    early = scatter_half(total, count)
     sent, grad_freq = call(
         functools.partial(frequency_back_kernel, norm_h, tile),
         "frequency_back",
@@ -568,10 +575,8 @@
         [vm((n, 384), BF), vm((256, 384), F32), vm((256, 384), F32)],
         flops=8 * n * n * 384, bytes_=8 << 20,
     )
-    early = early.astype(F32).sum(0).astype(BF)
     sent, early = tied(sent, early)
     got = swap(sent, count)
-    early = gather_halves(early, cols)
     (d_conv,) = call(
         functools.partial(conv_back_kernel, cl),
         "conv_back",
@@ -581,22 +586,34 @@
         [vm((rows + 2, width, 3 * cl), BF), vm((rows + 2, width, 3 * cg), BF)],
         flops=18 * pix * (ch * cl + cl * cg), bytes_=9 << 20,
     )
-    got = tie(got, d_conv)
+    got, d_conv, early = tied(got, d_conv, early)
+    early = gather_halves(early.astype(F32).sum(0).astype(BF), cols)
     late_rows = -(-(3 * 384 + 3 * cs) // (16 * count)) * 16 * count
-    grad_features, late = call(
+    d_unit, late = call(
         functools.partial(tail_kernel, norm_w, cl),
         "tail",
         (rows,),
         [
             (got, None, None), (tct, back_table, at_y), (tst, back_table, at_y), (masked, one_row(ch), at_y),
-            (marked, blocks(128), at_blocks), (d_joined, one_row(256), at_y), (d_conv, one_row(ch), at_y),
-            (w_in_d, None, None), (w_in_t, None, None), (grad_freq, None, None),
+            (d_joined, one_row(256), at_y), (w_in_d, None, None), (grad_freq, None, None),
         ],
-        [(wide, BF, one_row(ch), at_y), ((late_rows, 128), BF, None, None)],
+        [((rows, width, 256), BF, one_row(256), at_y), ((late_rows, 128), BF, None, None)],
         [vm((n, 256), BF), vm((256, cg), F32)],
         flops=4 * n * pix * 256, bytes_=16 << 20,
     )
     late = scatter_sum(late, count)
+    (grad_features,) = call(
+        functools.partial(finish_kernel, cl),
+        "finish",
+        (rows,),
+        [
+            (marked, blocks(128), at_blocks), (d_unit, one_row(256), at_y), (d_conv, one_row(ch), at_y),
+            (w_in_t, None, None),
+        ],
+        [(wide, BF, one_row(ch), at_y)],
+        flops=2 * pix * 256 * cg, bytes_=7 << 20,
+    )
+    late, grad_features = tied(late, grad_features)
     grad_local, grad_cross, grad_out = call(
         functools.partial(unpack_kernel, cl),
         "unpack",
@@ -606,6 +623,7 @@
         flops=1, bytes_=7 << 20,
     )
     late = gather(late, count)
+    late, grad_local, grad_cross, grad_out = tied(late, grad_local, grad_cross, grad_out)
     grad_freq = jnp.concatenate([late[k * 384 : (k + 1) * 384] for k in range(3)], 1).astype(F32)
     at = 3 * 384
     grad_in = jnp.concatenate([late[at + k * cs : at + (k + 1) * cs] for k in range(3)], 1).astype(F32).T

time: 303 us -> 286 us (0.944)
  blocking collectives: 34.1 us -> 0 us
  starting transfers between devices: 64.2 us -> 75.4 us
  Pallas kernels: 95.5 us -> 99.3 us
    all_to_all x2 -> x0, blocking collectives: 34.1 us -> none  [the longest x1 17.5 us: scatter_sum(): lax.all_to_all(x.reshape(count, -1, x.shape[-1]), AXES, 0, 0, tiled=True)]
    all_to_all x1 -> x3, waiting for transfers between devices: 0.01 us -> 16.8 us  [the longest x1 7.16 us: scatter_sum(): lax.all_to_all(x.reshape(count, -1, x.shape[-1]), AXES, 0, 0, tiled=True)]
    all_to_all x1 -> x3, starting transfers between devices: 3.94 us -> 19 us  [the longest x1 7.82 us: scatter_half(): lax.all_to_all(total.reshape(count // 2, -1, total.shape[-1]), AXES, 0, 0...]
    ppermute x2, waiting for transfers between devices: 18.9 us -> 6.94 us  [edges(): lax.ppermute(field[-1:], AXES, [(i, i + 1) for i in range(count - 1)])]
    all_to_all x4, waiting for transfers between devices: 22.7 us -> 14.2 us  [swap(): lax.all_to_all(x.reshape(count, -1, x.shape[-1]), AXES, 0, 0, tiled=True)]
    all_to_all x4, starting transfers between devices: 35.6 us -> 31.4 us  [swap(): lax.all_to_all(x.reshape(count, -1, x.shape[-1]), AXES, 0, 0, tiled=True)]
    pallas_call x9 -> x10, Pallas kernels: 95.5 us -> 99.3 us  [call(): pl.pallas_call(body, grid=grid, in_specs=[spec(a.shape, block, index) for...]
    all_gather x1, waiting for transfers between devices: 0.01 us -> 3.31 us  [gather_halves(): x = lax.all_gather(x, 'row', axis=0)]
  transfers between devices with their start and end apart: 18 -> 20, of which waited for: 10 -> 15; matrix products, arithmetic and copies ran while one was open for 8% -> 8% of each run, Pallas kernels for 18% -> 26%
where the time goes in v2:
time: 286 us; the launch traced here: 285 us
  Pallas kernels  99.3 us (35%)
  starting transfers between devices  75.4 us (26%)
  waiting for transfers between devices  58.3 us (20%)
  local copies, waits for them, and re-layouts  27.5 us (10%)
  between operations  14.5 us (5%)
  other arithmetic  9.86 us (3%)
    pallas_call x10, Pallas kernels, call(): pl.pallas_call(body, grid=grid, in_specs=[spec(a.shape, block, index) for...  99.3 us
    all_to_all x4, starting transfers between devices, swap(): lax.all_to_all(x.reshape(count, -1, x.shape[-1]), AXES, 0, 0, tiled=True)  31.4 us
    all_to_all x4, waiting for transfers between devices, swap(): lax.all_to_all(x.reshape(count, -1, x.shape[-1]), AXES, 0, 0, tiled=True)  14.2 us
    unnamed x65, local copies, waits for them, and re-layouts  8.64 us
    ppermute x2, starting transfers between devices, edges(): up = lax.ppermute(field[:1], AXES, [(i + 1, i) for i in range(count - 1)])  7.99 us
    all_to_all x1, starting transfers between devices, scatter_half(): lax.all_to_all(total.reshape(count // 2, -1, total.shape[-1]), AXES, 0, 0...  7.82 us
    all_to_all x1, waiting for transfers between devices, to_rows(): lax.all_to_all(field.reshape(cols, h // cols, w, c), 'col', 0, 0, tiled=T...  7.36 us
    all_to_all x1, waiting for transfers between devices, scatter_sum(): lax.all_to_all(x.reshape(count, -1, x.shape[-1]), AXES, 0, 0, tiled=True)  7.16 us
  transfers between devices with their start and end apart: 20, of which 15 were waited for; matrix products, arithmetic and copies ran while one was open for 8% of the time, Pallas kernels for 26%

profile of v2, /device:TPU:1, one launch (start us, length us, event | category | flops | bytes accessed | tf_op | source)
XLA Modules:
  0.0 284.9 jit_solution(9410879416910493833)
XLA Ops:
  10.8 5.0 %all-to-all-start = ((bf16[4,5,80,512]{3,2,1,0:T(8,128)(2,1)}), bf16[4,5,80,512]{3,2,1,0:T(8,128)(2,1)S(1)}, u32[]{:S(2)}, u32[]{:S(2)}) async-start(bf16[4,5,80,512]{3,2,1,0:T(8,128)(2,1)} %broadcast_select_fusion), calls=%async_computation | async-start | bytes 3276800 | tf_op jit(solution)/shard_map/all_to_all | solution.py:384
  28.9 7.4 %all-to-all-done.marked = bf16[4,5,80,512]{3,2,1,0:T(8,128)(2,1)S(1)} async-done(((bf16[4,5,80,512]{3,2,1,0:T(8,128)(2,1)}), bf16[4,5,80,512]{3,2,1,0:T(8,128)(2,1)S(1)}, u32[]{:S(2)}, u32[]{:S(2)}) %all-to-all-start) | async-done | bytes 1638432 | tf_op jit(solution)/shard_map/all_to_all | solution.py:384
  37.5 9.6 %head.1 = (bf16[5,320,512]{2,1,0:T(8,128)(2,1)}, bf16[5,320,256]{2,1,0:T(8,128)(2,1)}, bf16[1024,384]{1,0:T(8,128)(2,1)}) custom-call(bf16[4,5,80,512]{3,2,1,0:T(8,128)(2,1)} %copy-done, bf16[384,256]{1,0:T(8,128)(2,1)} %pad_maximum_fusion.1.w_in, bf16[5,1024,320]{2,1,0:T(8,128)(2,1)} %constant.115.clone.tc, bf16[5,1024,320]{2,1,0:T(8,128)(2,1)} %constant.116.clone.ts), custom_call_target="tpu_custom_call" | custom-call | flops 1677721600 | bytes 12582912 | tf_op jit(solution)/shard_map/head/pallas_call | solution.py:96
  47.1 9.5 %all-to-all-start.1 = ((bf16[64,16,384]{2,1,0:T(8,128)(2,1)}), bf16[64,16,384]{2,1,0:T(8,128)(2,1)S(1)}, u32[]{:S(2)}, u32[]{:S(2)}) async-start(bf16[64,16,384]{2,1,0:T(8,128)(2,1)} %bitcast.67), calls=%async_computation.1 | async-start | bytes 1572864 | tf_op jit(solution)/shard_map/all_to_all | solution.py:379
  76.9 11.3 %frequency.1 = (bf16[1024,384]{1,0:T(8,128)(2,1)}, bf16[1024,384]{1,0:T(8,128)(2,1)}) custom-call(bf16[1024,384]{1,0:T(8,128)(2,1)} %bitcast.66, bf16[1024,1024]{1,0:T(8,128)(2,1)} %constant.117.clone.tc, bf16[1024,1024]{1,0:T(8,128)(2,1)} %constant.118.clone.ts, bf16[384,384]{1,0:T(8,128)(2,1)} %copy.46.w_freq, f32[1024,1]{1,0:T(8,128)} %copy.47.weight, ...), custom_call_target="tpu_custom_call" | custom-call | flops 3221225472 | bytes 7340032 | tf_op jit(solution)/shard_map/frequency/pallas_call | solution.py:96
  88.2 4.9 %collective-permute-done.3.refs_2_ = bf16[5,80,512]{2,1,0:T(8,128)(2,1)S(1)} collective-permute-done((bf16[5,80,512]{2,1,0:T(8,128)(2,1)}, bf16[5,80,512]{2,1,0:T(8,128)(2,1)S(1)}, u32[]{:S(2)}, u32[]{:S(2)}) %collective-permute-start.3) | collective-permute-done | bytes 409632 | tf_op jit(solution)/shard_map/ppermute | solution.py:394
  93.9 12.4 %all-to-all-start.2 = ((bf16[64,16,384]{2,1,0:T(8,128)(2,1)}), bf16[64,16,384]{2,1,0:T(8,128)(2,1)S(1)}, u32[]{:S(2)}, u32[]{:S(2)}) async-start(bf16[64,16,384]{2,1,0:T(8,128)(2,1)} %bitcast.71), calls=%async_computation.2 | async-start | bytes 1572864 | tf_op jit(solution)/shard_map/all_to_all | solution.py:379
  107.7 8.7 %conv.1.pre = f32[5,320,512]{2,1,0:T(8,128)} custom-call(bf16[1,320,512]{2,1,0:T(8,128)(2,1)} %collective-permute-done.above, bf16[5,320,512]{2,1,0:T(8,128)(2,1)} %get-tuple-element.61.masked, bf16[1,320,512]{2,1,0:T(8,128)(2,1)} %collective-permute-done.1.below, bf16[3,512,384]{2,1,0:T(8,128)(2,1)} %copy.48.w_local, bf16[384,1152]{1,0:T(8,128)(2,1)} %bitcast.65), custom_call_target="tpu_custom_call" | custom-call | flops 3303014400 | bytes 9437184 | tf_op jit(solution)/shard_map/conv/pallas_call | solution.py:96
  116.5 5.2 %all-to-all-done.2 = bf16[64,16,384]{2,1,0:T(8,128)(2,1)S(1)} async-done(((bf16[64,16,384]{2,1,0:T(8,128)(2,1)}), bf16[64,16,384]{2,1,0:T(8,128)(2,1)S(1)}, u32[]{:S(2)}, u32[]{:S(2)}) %all-to-all-start.2) | async-done | bytes 786464 | tf_op jit(solution)/shard_map/all_to_all | solution.py:379
  122.6 15.8 %middle.1 = (bf16[5,320,512]{2,1,0:T(8,128)(2,1)}, bf16[5,320,512]{2,1,0:T(8,128)(2,1)}, bf16[5,320,256]{2,1,0:T(8,128)(2,1)}, bf16[1024,384]{1,0:T(8,128)(2,1)}, bf16[192,384]{1,0:T(8,128)(2,1)}) custom-call(bf16[1024,384]{1,0:T(8,128)(2,1)} %bitcast.54, bf16[5,320,1024]{2,1,0:T(8,128)(2,1)} %constant.113.clone.tct, ...), custom_call_target="tpu_custom_call" | custom-call | flops 3355443200 | bytes 25165824 | tf_op jit(solution)/shard_map/middle/pallas_call | solution.py:96
  138.4 4.7 %all-to-all-start.3 = ((bf16[64,16,384]{2,1,0:T(8,128)(2,1)}), bf16[64,16,384]{2,1,0:T(8,128)(2,1)S(1)}, u32[]{:S(2)}, u32[]{:S(2)}) async-start(bf16[64,16,384]{2,1,0:T(8,128)(2,1)} %bitcast.70), calls=%async_computation.3 | async-start | bytes 1572864 | tf_op jit(solution)/shard_map/all_to_all | solution.py:379
  143.1 11.1 %conv_grad.1 = bf16[2,1536,384]{2,1,0:T(8,128)(2,1)} custom-call(bf16[1,320,512]{2,1,0:T(8,128)(2,1)} %collective-permute-done.above, bf16[5,320,512]{2,1,0:T(8,128)(2,1)} %get-tuple-element.61.masked, bf16[1,320,512]{2,1,0:T(8,128)(2,1)} %collective-permute-done.1.below, bf16[5,320,512]{2,1,0:T(8,128)(2,1)} %get-tuple-element.79.d_out, ...), custom_call_target="tpu_custom_call" | custom-call | flops 3303014400 | bytes 7340032 | tf_op jit(solution)/shard_map/conv_grad/pallas_call | solution.py:96
  165.0 4.5 %collective-permute-start.7 = (bf16[1,320,512]{2,1,0:T(8,128)(2,1)S(1)}, bf16[1,320,512]{2,1,0:T(8,128)(2,1)S(1)}, u32[]{:S(2)}, u32[]{:S(2)}) collective-permute-start(bf16[1,320,512]{2,1,0:T(8,128)(2,1)S(1)} %get-tuple-element.111), channel_id=1, source_target_pairs={{1,0},{2,1},{3,2},{4,3},{5,4},{6,5},{7,6},{8,7},{9,8},{10,9},{11,1... | collective-permute-start | bytes 983048 | tf_op jit(solution)/shard_map/ppermute | solution.py:430
  176.6 7.8 %all-to-all-start.4 = ((bf16[32,48,384]{2,1,0:T(8,128)(2,1)}), bf16[32,48,384]{2,1,0:T(8,128)(2,1)S(1)}, u32[]{:S(2)}, u32[]{:S(2)}) async-start(bf16[32,48,384]{2,1,0:T(8,128)(2,1)} %bitcast.27), calls=%async_computation.4 | async-start | bytes 2359296 | tf_op jit(solution)/shard_map/all_to_all | solution.py:411
  184.5 13.5 %frequency_back.1 = (bf16[1024,384]{1,0:T(8,128)(2,1)}, bf16[384,384]{1,0:T(8,128)(2,1)}) custom-call(bf16[1024,384]{1,0:T(8,128)(2,1)} %bitcast.68, bf16[1024,1024]{1,0:T(8,128)(2,1)} %constant.117.clone.tc, bf16[1024,1024]{1,0:T(8,128)(2,1)} %constant.118.clone.ts, bf16[384,384]{1,0:T(8,128)(2,1)} %copy.46.w_freq, bf16[384,384]{1,0:T(8,128)(2,1)} %bitcast.62, ...), custom_call_target="tpu_custom_call" | custom-call | flops 3221225472 | bytes 8388608 | tf_op jit(solution)/shard_map/frequency_back/pallas_call | solution.py:96
  202.0 4.8 %all-to-all-start.5 = ((bf16[64,16,384]{2,1,0:T(8,128)(2,1)}), bf16[64,16,384]{2,1,0:T(8,128)(2,1)S(1)}, u32[]{:S(2)}, u32[]{:S(2)}) async-start(bf16[64,16,384]{2,1,0:T(8,128)(2,1)} %bitcast.69), calls=%async_computation.5 | async-start | bytes 1572864 | tf_op jit(solution)/shard_map/all_to_all | solution.py:379
  207.2 10.5 %conv_back.1.d_conv = f32[5,320,512]{2,1,0:T(8,128)} custom-call(bf16[1,320,512]{2,1,0:T(8,128)(2,1)} %copy-done.24, bf16[5,320,512]{2,1,0:T(8,128)(2,1)} %get-tuple-element.79.d_out, bf16[1,320,512]{2,1,0:T(8,128)(2,1)} %copy-done.25, bf16[3,384,512]{2,1,0:T(8,128)(2,1)} %bitcast.63, bf16[3,1152,128]{2,1,0:T(8,128)(2,1)} %bitcast.64), custom_call_target="tpu_custom_call" | custom-call | flops 3303014400 | bytes 9437184 | tf_op jit(solution)/shard_map/conv_back/pallas_call | solution.py:96
  217.7 4.6 %all-to-all-done.5 = bf16[64,16,384]{2,1,0:T(8,128)(2,1)S(1)} async-done(((bf16[64,16,384]{2,1,0:T(8,128)(2,1)}), bf16[64,16,384]{2,1,0:T(8,128)(2,1)S(1)}, u32[]{:S(2)}, u32[]{:S(2)}) %all-to-all-start.5) | async-done | bytes 786464 | tf_op jit(solution)/shard_map/all_to_all | solution.py:379
  229.3 9.4 %tail.1 = (bf16[5,320,256]{2,1,0:T(8,128)(2,1)}, bf16[2048,128]{1,0:T(8,128)(2,1)}) custom-call(bf16[1024,384]{1,0:T(8,128)(2,1)} %bitcast.55, bf16[5,320,1024]{2,1,0:T(8,128)(2,1)} %constant.113.clone.tct, bf16[5,320,1024]{2,1,0:T(8,128)(2,1)} %constant.114.clone.tst, bf16[5,320,512]{2,1,0:T(8,128)(2,1)} %get-tuple-element.61.masked, ...), custom_call_target="tpu_custom_call" | custom-call | flops 1677721600 | bytes 16777216 | tf_op jit(solution)/shard_map/tail/pallas_call | solution.py:96
  238.7 6.5 %all-to-all-start.6 = ((bf16[64,32,128]{2,1,0:T(8,128)(2,1)}), bf16[64,32,128]{2,1,0:T(8,128)(2,1)S(1)}, u32[]{:S(2)}, u32[]{:S(2)}) async-start(bf16[64,32,128]{2,1,0:T(8,128)(2,1)} %bitcast.73), calls=%async_computation.6 | async-start | bytes 1048576 | tf_op jit(solution)/shard_map/all_to_all | solution.py:435
  245.3 5.6 %finish.1 = bf16[5,320,512]{2,1,0:T(8,128)(2,1)} custom-call(bf16[4,5,80,512]{3,2,1,0:T(8,128)(2,1)} %copy-done, bf16[5,320,256]{2,1,0:T(8,128)(2,1)} %get-tuple-element.98.d_unit, f32[5,320,512]{2,1,0:T(8,128)} %conv_back.1.d_conv, bf16[256,384]{1,0:T(8,128)(2,1)} %pad.7.w_in_t), custom_call_target="tpu_custom_call" | custom-call | flops 314572800 | bytes 7340032 | tf_op jit(solution)/shard_map/finish/pallas_call | solution.py:96
  250.9 7.2 %all-to-all-done.6 = bf16[64,32,128]{2,1,0:T(8,128)(2,1)S(1)} async-done(((bf16[64,32,128]{2,1,0:T(8,128)(2,1)}), bf16[64,32,128]{2,1,0:T(8,128)(2,1)S(1)}, u32[]{:S(2)}, u32[]{:S(2)}) %all-to-all-start.6) | async-done | bytes 524320 | tf_op jit(solution)/shard_map/all_to_all | solution.py:435
  259.0 4.6 %all-to-all-start.7 = ((bf16[64,32,128]{2,1,0:T(8,128)(2,1)}), bf16[64,32,128]{2,1,0:T(8,128)(2,1)S(1)}, u32[]{:S(2)}, u32[]{:S(2)}) async-start(bf16[64,32,128]{2,1,0:T(8,128)(2,1)} %broadcast_in_dim.43), calls=%async_computation.7 | async-start | bytes 1048576 | tf_op jit(solution)/shard_map/all_to_all | solution.py:440
  270.8 5.6 %all-to-all-done.7 = bf16[64,32,128]{2,1,0:T(8,128)(2,1)S(1)} async-done(((bf16[64,32,128]{2,1,0:T(8,128)(2,1)}), bf16[64,32,128]{2,1,0:T(8,128)(2,1)S(1)}, u32[]{:S(2)}, u32[]{:S(2)}) %all-to-all-start.7) | async-done | bytes 524320 | tf_op jit(solution)/shard_map/all_to_all | solution.py:440
  (135 shorter events, 80.2 us)
Async XLA Ops:
  10.8 25.5 %all-to-all-start = ((bf16[4,5,80,512]{3,2,1,0:T(8,128)(2,1)}), bf16[4,5,80,512]{3,2,1,0:T(8,128)(2,1)S(1)}, u32[]{:S(2)}, u32[]{:S(2)}) async-start(bf16[4,5,80,512]{3,2,1,0:T(8,128)(2,1)} %broadcast_select_fusion), calls=%async_computation | async-start | bytes 3276800 | tf_op jit(solution)/shard_map/all_to_all | solution.py:384
  28.9 42.2 %copy-start.11 = (bf16[384,384]{0,1:T(8,128)(2,1)}, bf16[384,384]{0,1:T(8,128)(2,1)S(1)}, u32[]{:S(2)}) copy-start(bf16[384,384]{0,1:T(8,128)(2,1)S(1)} %fusion.11) | copy-start | bytes 884740
  47.1 18.3 %copy-start.6 = (bf16[1,20,80,512]{3,2,1,0:T(8,128)(2,1)S(1)}, bf16[1,20,80,512]{3,2,1,0:T(8,128)(2,1)}, u32[]{:S(2)}) copy-start(bf16[1,20,80,512]{3,2,1,0:T(8,128)(2,1)} %param.17) | copy-start | bytes 4915204
  47.1 28.9 %all-to-all-start.1 = ((bf16[64,16,384]{2,1,0:T(8,128)(2,1)}), bf16[64,16,384]{2,1,0:T(8,128)(2,1)S(1)}, u32[]{:S(2)}, u32[]{:S(2)}) async-start(bf16[64,16,384]{2,1,0:T(8,128)(2,1)} %bitcast.67), calls=%async_computation.1 | async-start | bytes 1572864 | tf_op jit(solution)/shard_map/all_to_all | solution.py:379
  58.6 17.4 %collective-permute-start = (bf16[1,320,512]{2,1,0:T(8,128)(2,1)}, bf16[1,320,512]{2,1,0:T(8,128)(2,1)}, u32[]{:S(2)}, u32[]{:S(2)}) collective-permute-start(bf16[1,320,512]{2,1,0:T(8,128)(2,1)} %get-tuple-element.118), channel_id=1, source_target_pairs={{0,1},{1,2},{2,3},{3,4},{4,5},{5,6},{6,7},{7,8},{8,9},{9,10},{10,1... | collective-permute-start | bytes 983048 | tf_op jit(solution)/shard_map/ppermute | solution.py:429
  61.9 14.1 %collective-permute-start.1 = (bf16[1,320,512]{2,1,0:T(8,128)(2,1)}, bf16[1,320,512]{2,1,0:T(8,128)(2,1)}, u32[]{:S(2)}, u32[]{:S(2)}) collective-permute-start(bf16[1,320,512]{2,1,0:T(8,128)(2,1)} %get-tuple-element.117), channel_id=1, source_target_pairs={{1,0},{2,1},{3,2},{4,3},{5,4},{6,5},{7,6},{8,7},{9,8},{10,9},{11,1... | collective-permute-start | bytes 983048 | tf_op jit(solution)/shard_map/ppermute | solution.py:430
  66.7 21.6 %collective-permute-start.2 = (bf16[5,80,512]{2,1,0:T(8,128)(2,1)}, bf16[5,80,512]{2,1,0:T(8,128)(2,1)S(1)}, u32[]{:S(2)}, u32[]{:S(2)}) collective-permute-start(bf16[5,80,512]{2,1,0:T(8,128)(2,1)} %get-tuple-element.115), channel_id=1, source_target_pairs={{0,1},{1,2},{2,3},{3,0},{4,5},{5,6},{6,7},{7,4},{8,9},{9,10},{10,1... | collective-permute-start | bytes 1228808 | tf_op jit(solution)/shard_map/ppermute | solution.py:394
  66.7 26.4 %collective-permute-start.3 = (bf16[5,80,512]{2,1,0:T(8,128)(2,1)}, bf16[5,80,512]{2,1,0:T(8,128)(2,1)S(1)}, u32[]{:S(2)}, u32[]{:S(2)}) collective-permute-start(bf16[5,80,512]{2,1,0:T(8,128)(2,1)} %get-tuple-element.114), channel_id=1, source_target_pairs={{0,2},{1,3},{2,0},{3,1},{4,6},{5,7},{6,4},{7,5},{8,10},{9,11},{10,... | collective-permute-start | bytes 1228808 | tf_op jit(solution)/shard_map/ppermute | solution.py:394
  68.9 24.2 %collective-permute-start.4 = (bf16[5,80,512]{2,1,0:T(8,128)(2,1)}, bf16[5,80,512]{2,1,0:T(8,128)(2,1)S(1)}, u32[]{:S(2)}, u32[]{:S(2)}) collective-permute-start(bf16[5,80,512]{2,1,0:T(8,128)(2,1)} %get-tuple-element.113), channel_id=1, source_target_pairs={{0,3},{1,0},{2,1},{3,2},{4,7},{5,4},{6,5},{7,6},{8,11},{9,8},{10,9... | collective-permute-start | bytes 1228808 | tf_op jit(solution)/shard_map/ppermute | solution.py:394
  88.2 18.1 %copy-start.2 = (bf16[3,3,512,128]{2,3,1,0:T(8,128)(2,1)S(1)}, bf16[3,3,512,128]{2,3,1,0:T(8,128)(2,1)}, u32[]{:S(2)}) copy-start(bf16[3,3,512,128]{2,3,1,0:T(8,128)(2,1)} %copy.42) | copy-start | bytes 3538948
  88.2 19.5 %copy-start.21 = (bf16[5,80,512]{2,1,0:T(8,128)(2,1)}, bf16[5,80,512]{2,1,0:T(8,128)(2,1)S(1)}, u32[]{:S(2)}) copy-start(bf16[5,80,512]{2,1,0:T(8,128)(2,1)S(1)} %collective-permute-done.2.refs_1_) | copy-start | bytes 1228804
  93.9 27.8 %all-to-all-start.2 = ((bf16[64,16,384]{2,1,0:T(8,128)(2,1)}), bf16[64,16,384]{2,1,0:T(8,128)(2,1)S(1)}, u32[]{:S(2)}, u32[]{:S(2)}) async-start(bf16[64,16,384]{2,1,0:T(8,128)(2,1)} %bitcast.71), calls=%async_computation.2 | async-start | bytes 1572864 | tf_op jit(solution)/shard_map/all_to_all | solution.py:379
  138.4 20.2 %all-to-all-start.3 = ((bf16[64,16,384]{2,1,0:T(8,128)(2,1)}), bf16[64,16,384]{2,1,0:T(8,128)(2,1)S(1)}, u32[]{:S(2)}, u32[]{:S(2)}) async-start(bf16[64,16,384]{2,1,0:T(8,128)(2,1)} %bitcast.70), calls=%async_computation.3 | async-start | bytes 1572864 | tf_op jit(solution)/shard_map/all_to_all | solution.py:379
  161.0 8.6 %collective-permute-start.5 = (bf16[1536,384]{1,0:T(8,128)(2,1)S(1)}, bf16[1536,384]{1,0:T(8,128)(2,1)}, u32[]{:S(2)}, u32[]{:S(2)}) collective-permute-start(bf16[1536,384]{1,0:T(8,128)(2,1)S(1)} %dynamic-slice_bitcast_fusion), channel_id=1, source_target_pairs={{0,4},{4,0},{8,12},{12,8},{16,20},{20,16},{24,28},{28,24},{32,36},... | collective-permute-start | bytes 3538952 | tf_op jit(solution)/shard_map/ppermute | solution.py:403
  162.8 12.4 %collective-permute-start.6 = (bf16[1,320,512]{2,1,0:T(8,128)(2,1)S(1)}, bf16[1,320,512]{2,1,0:T(8,128)(2,1)S(1)}, u32[]{:S(2)}, u32[]{:S(2)}) collective-permute-start(bf16[1,320,512]{2,1,0:T(8,128)(2,1)S(1)} %get-tuple-element.112), channel_id=1, source_target_pairs={{0,1},{1,2},{2,3},{3,4},{4,5},{5,6},{6,7},{7,8},{8,9},{9,10},{10,1... | collective-permute-start | bytes 983048 | tf_op jit(solution)/shard_map/ppermute | solution.py:429
  165.0 10.9 %collective-permute-start.7 = (bf16[1,320,512]{2,1,0:T(8,128)(2,1)S(1)}, bf16[1,320,512]{2,1,0:T(8,128)(2,1)S(1)}, u32[]{:S(2)}, u32[]{:S(2)}) collective-permute-start(bf16[1,320,512]{2,1,0:T(8,128)(2,1)S(1)} %get-tuple-element.111), channel_id=1, source_target_pairs={{1,0},{2,1},{3,2},{4,3},{5,4},{6,5},{7,6},{8,7},{9,8},{10,9},{11,1... | collective-permute-start | bytes 983048 | tf_op jit(solution)/shard_map/ppermute | solution.py:430
  176.6 25.4 %all-to-all-start.4 = ((bf16[32,48,384]{2,1,0:T(8,128)(2,1)}), bf16[32,48,384]{2,1,0:T(8,128)(2,1)S(1)}, u32[]{:S(2)}, u32[]{:S(2)}) async-start(bf16[32,48,384]{2,1,0:T(8,128)(2,1)} %bitcast.27), calls=%async_computation.4 | async-start | bytes 2359296 | tf_op jit(solution)/shard_map/all_to_all | solution.py:411
  202.0 20.3 %all-to-all-start.5 = ((bf16[64,16,384]{2,1,0:T(8,128)(2,1)}), bf16[64,16,384]{2,1,0:T(8,128)(2,1)S(1)}, u32[]{:S(2)}, u32[]{:S(2)}) async-start(bf16[64,16,384]{2,1,0:T(8,128)(2,1)} %bitcast.69), calls=%async_computation.5 | async-start | bytes 1572864 | tf_op jit(solution)/shard_map/all_to_all | solution.py:379
  206.9 60.1 %all-gather.3.cloned.1.call-start = ((), (), s32[]{:S(2)}) async-start(), calls=%async_computation.8 | async-start | bytes 2506752 | tf_op jit(solution)/shard_map/all_gather | solution.py:424
  222.4 2.9 %collective-permute-start.8 = (bf16[48,384]{1,0:T(8,128)(2,1)S(1)}, bf16[48,384]{1,0:T(8,128)(2,1)S(1)}, u32[]{:S(2)}, u32[]{:S(2)}) collective-permute-start(bf16[48,384]{1,0:T(8,128)(2,1)S(1)} %reduce_sum.25), channel_id=1, source_target_pairs={{1,0},{2,1},{3,2},{0,3},{5,4},{6,5},{7,6},{4,7},{9,8},{10,9},{11,1... | collective-permute-start | bytes 110600 | tf_op jit(solution)/shard_map/ppermute | solution.py:420
  222.5 4.4 %collective-permute-start.9 = (bf16[48,384]{1,0:T(8,128)(2,1)S(1)}, bf16[48,384]{1,0:T(8,128)(2,1)S(1)}, u32[]{:S(2)}, u32[]{:S(2)}) collective-permute-start(bf16[48,384]{1,0:T(8,128)(2,1)S(1)} %reduce_sum.25), channel_id=1, source_target_pairs={{2,0},{3,1},{0,2},{1,3},{6,4},{7,5},{4,6},{5,7},{10,8},{11,9},{8,1... | collective-permute-start | bytes 110600 | tf_op jit(solution)/shard_map/ppermute | solution.py:420
  224.5 4.0 %collective-permute-start.10 = (bf16[48,384]{1,0:T(8,128)(2,1)S(1)}, bf16[48,384]{1,0:T(8,128)(2,1)S(1)}, u32[]{:S(2)}, u32[]{:S(2)}) collective-permute-start(bf16[48,384]{1,0:T(8,128)(2,1)S(1)} %reduce_sum.25), channel_id=1, source_target_pairs={{3,0},{0,1},{1,2},{2,3},{7,4},{4,5},{5,6},{6,7},{11,8},{8,9},{9,10... | collective-permute-start | bytes 110600 | tf_op jit(solution)/shard_map/ppermute | solution.py:420
  238.7 19.3 %all-to-all-start.6 = ((bf16[64,32,128]{2,1,0:T(8,128)(2,1)}), bf16[64,32,128]{2,1,0:T(8,128)(2,1)S(1)}, u32[]{:S(2)}, u32[]{:S(2)}) async-start(bf16[64,32,128]{2,1,0:T(8,128)(2,1)} %bitcast.73), calls=%async_computation.6 | async-start | bytes 1048576 | tf_op jit(solution)/shard_map/all_to_all | solution.py:435
  259.0 17.4 %all-to-all-start.7 = ((bf16[64,32,128]{2,1,0:T(8,128)(2,1)}), bf16[64,32,128]{2,1,0:T(8,128)(2,1)S(1)}, u32[]{:S(2)}, u32[]{:S(2)}) async-start(bf16[64,32,128]{2,1,0:T(8,128)(2,1)} %broadcast_in_dim.43), calls=%async_computation.7 | async-start | bytes 1048576 | tf_op jit(solution)/shard_map/all_to_all | solution.py:440
  (27 other events, 101.5 us)
Sparse Core Ops, SparseCore 0:
  229.4 37.4 all-gather.2

commit v3 on v2

--- a/solution.py
+++ b/solution.py
@@ -344,18 +344,24 @@
         early[1, at + size :, :] = jnp.zeros((early.shape[1] - at - size, g), BF)
 
 
-def unpack_kernel(cl, got, g_local, g_cross, g_out):
-    rows, ch = got.shape[2], g_local.shape[2]
-    for at in range(0, 3 * ch, 64):
-        block = got[at // rows, 0, at % rows : at % rows + 64, :].astype(F32)
-        for j in range(3):
-            g_local[at // ch, j, at % ch : at % ch + 64, :] = block[:, j * cl : (j + 1) * cl]
-    for at in range(0, 9 * cl + g_out.shape[0], 64):
-        block = got[at // rows, 1, at % rows : at % rows + 64, :].astype(F32)
-        if at < 9 * cl:
-            g_cross[at : at + 64, :] = block
-        else:
-            g_out[at - 9 * cl : at - 9 * cl + 64, :] = block
+def unpack_kernel(cl, mine, other, core, g_local, g_cross, g_out):
+    ch = g_local.shape[2]
+
+    def write(local, rest):
+        for at in range(0, 3 * ch, 64):
+            block = local[at : at + 64, :].astype(F32)
+            for j in range(3):
+                g_local[at // ch, j, at % ch : at % ch + 64, :] = block[:, j * cl : (j + 1) * cl]
+        g_cross[...] = rest[0 : 9 * cl, :].astype(F32)
+        g_out[...] = rest[9 * cl : 9 * cl + g_out.shape[0], :].astype(F32)
+
+    @pl.when(core[0, 0] == 0)
+    def _():
+        write(mine, other)
+
+    @pl.when(core[0, 0] == 1)
+    def _():
+        write(other, mine)
 
 
 def conv_back_kernel(cl, above, d_out, below, w_local, w_cross, d_conv, pad_l, pad_g):
@@ -404,25 +410,12 @@
     return (mine.astype(F32) + other.astype(F32)).astype(BF)
 
 
-def scatter_half(total, count):
+def core_exchange(x, count):
     pairs = lax.axis_size("row")
     cols = count // pairs
     groups = [[cols * r + c for r in range(k, pairs, 2) for c in range(cols)] for k in range(2)]
-    return lax.all_to_all(
-        total.reshape(count // 2, -1, total.shape[-1]), AXES, 0, 0, axis_index_groups=groups, tiled=True
-    )
-
-
-def gather_halves(x, cols):
-    me = lax.axis_index("col")
-    parts = [x]
-    for k in range(1, cols):
-        parts.append(lax.ppermute(x, "col", [((i + k) % cols, i) for i in range(cols)]))
-    both = jnp.concatenate(parts + parts[:-1], 0)
-    size = x.shape[0]
-    x = lax.dynamic_slice_in_dim(both, (cols - me) % cols * size, cols * size, 0)
-    x = lax.all_gather(x, "row", axis=0)
-    return x.reshape(x.shape[0] // 2, 2, *x.shape[1:])
+    x = x.reshape(count // 2, -1, x.shape[-1])
+    return lax.all_to_all(x, AXES, 0, 0, axis_index_groups=groups, tiled=True)
 
 
 def edges(field, count):
@@ -562,7 +555,7 @@
     )
     got, early = tied(got, early)
     got, total, d_above, d_below = tied(got, core_sum(early), d_above, d_below)
-    early = scatter_half(total, count)
+    early = core_exchange(total, count)
     sent, grad_freq = call(
         functools.partial(frequency_back_kernel, norm_h, tile),
         "frequency_back",
@@ -587,7 +580,8 @@
         flops=18 * pix * (ch * cl + cl * cg), bytes_=9 << 20,
     )
     got, d_conv, early = tied(got, d_conv, early)
-    early = gather_halves(early.astype(F32).sum(0).astype(BF), cols)
+    early = early.astype(F32).sum(0).astype(BF)
+    early = core_exchange(jnp.tile(early, (count // 2, 1)), count).reshape(-1, 384)
     late_rows = -(-(3 * 384 + 3 * cs) // (16 * count)) * 16 * count
     d_unit, late = call(
         functools.partial(tail_kernel, norm_w, cl),
@@ -601,6 +595,10 @@
         [vm((n, 256), BF), vm((256, cg), F32)],
         flops=4 * n * pix * 256, bytes_=16 << 20,
     )
+    late, early = tied(late, early)
+    pairs = lax.axis_size("row")
+    other = lax.ppermute(early, "row", [(i, i ^ 1) for i in range(pairs)])
+    my_core = (lax.axis_index("row") % 2).astype(jnp.int32).reshape(1, 1)
     late = scatter_sum(late, count)
     (grad_features,) = call(
         functools.partial(finish_kernel, cl),
@@ -618,7 +616,7 @@
         functools.partial(unpack_kernel, cl),
         "unpack",
         (1,),
-        [(early, None, None)],
+        [(early, None, None), (other, None, None), (my_core, None, None)],
         [((3, 3, ch, cl), F32, None, None), ((9 * cl, cg), F32, None, None), ((cs, cg), F32, None, None)],
         flops=1, bytes_=7 << 20,
     )

time: 286 us -> 279 us (0.976)
  between operations: 14.5 us -> 1.08 us
  waiting for transfers between devices: 58.3 us -> 61.5 us
    all_to_all x1 -> x2, waiting for transfers between devices: 4.08 us -> 12.2 us  [core_exchange(): return lax.all_to_all(x, AXES, 0, 0, axis_index_groups=groups, tiled=True)]
    ppermute x3 -> x1, waiting for transfers between devices: 3.99 us -> 0.01 us  [shards(): other = lax.ppermute(early, 'row', [(i, i ^ 1) for i in range(pairs)])]
    all_to_all x1 -> x2, starting transfers between devices: 7.82 us -> 11.8 us  [core_exchange(): return lax.all_to_all(x, AXES, 0, 0, axis_index_groups=groups, tiled=True)]
    all_gather x1 -> x0, waiting for transfers between devices: 3.31 us -> none  [gather_halves(): x = lax.all_gather(x, 'row', axis=0)]
    unnamed x65 -> x63, local copies, waits for them, and re-layouts: 8.64 us -> 9.61 us
  transfers between devices with their start and end apart: 20 -> 18, of which waited for: 15 -> 12; matrix products, arithmetic and copies ran while one was open for 8% -> 9% of each run, Pallas kernels for 26% -> 27%
where the time goes in v3:
time: 279 us; the launch traced here: 278 us
  Pallas kernels  99.5 us (36%)
  starting transfers between devices  77 us (28%)
  waiting for transfers between devices  61.5 us (22%)
  local copies, waits for them, and re-layouts  28.8 us (10%)
  other arithmetic  9.87 us (4%)
    pallas_call x10, Pallas kernels, call(): pl.pallas_call(body, grid=grid, in_specs=[spec(a.shape, block, index) for...  99.5 us
    all_to_all x4, starting transfers between devices, swap(): lax.all_to_all(x.reshape(count, -1, x.shape[-1]), AXES, 0, 0, tiled=True)  31.5 us
    all_to_all x4, waiting for transfers between devices, swap(): lax.all_to_all(x.reshape(count, -1, x.shape[-1]), AXES, 0, 0, tiled=True)  14.5 us
    all_to_all x2, waiting for transfers between devices, core_exchange(): return lax.all_to_all(x, AXES, 0, 0, axis_index_groups=groups, tiled=True)  12.2 us
    all_to_all x2, starting transfers between devices, core_exchange(): return lax.all_to_all(x, AXES, 0, 0, axis_index_groups=groups, tiled=True)  11.8 us
    unnamed x63, local copies, waits for them, and re-layouts  9.61 us
    ppermute x2, starting transfers between devices, edges(): up = lax.ppermute(field[:1], AXES, [(i + 1, i) for i in range(count - 1)])  7.99 us
    all_to_all x1, waiting for transfers between devices, gather(): lax.all_to_all(jnp.broadcast_to(x[None], (count,) + x.shape), AXES, 0, 0,...  7.7 us
  transfers between devices with their start and end apart: 18, of which 12 were waited for; matrix products, arithmetic and copies ran while one was open for 9% of the time, Pallas kernels for 27%

profile of v3, /device:TPU:1, one launch (start us, length us, event | category | flops | bytes accessed | tf_op | source)
XLA Modules:
  0.0 277.7 jit_solution(10142144820326069485)
XLA Ops:
  4.3 5.0 %all-to-all-start = ((bf16[4,5,80,512]{3,2,1,0:T(8,128)(2,1)}), bf16[4,5,80,512]{3,2,1,0:T(8,128)(2,1)S(1)}, u32[]{:S(2)}, u32[]{:S(2)}) async-start(bf16[4,5,80,512]{3,2,1,0:T(8,128)(2,1)} %broadcast_select_fusion), calls=%async_computation | async-start | bytes 3276800 | tf_op jit(solution)/shard_map/all_to_all | solution.py:390
  22.4 7.4 %all-to-all-done.marked = bf16[4,5,80,512]{3,2,1,0:T(8,128)(2,1)S(1)} async-done(((bf16[4,5,80,512]{3,2,1,0:T(8,128)(2,1)}), bf16[4,5,80,512]{3,2,1,0:T(8,128)(2,1)S(1)}, u32[]{:S(2)}, u32[]{:S(2)}) %all-to-all-start) | async-done | bytes 1638432 | tf_op jit(solution)/shard_map/all_to_all | solution.py:390
  30.9 9.6 %head.1 = (bf16[5,320,512]{2,1,0:T(8,128)(2,1)}, bf16[5,320,256]{2,1,0:T(8,128)(2,1)}, bf16[1024,384]{1,0:T(8,128)(2,1)}) custom-call(bf16[4,5,80,512]{3,2,1,0:T(8,128)(2,1)} %copy-done, bf16[384,256]{1,0:T(8,128)(2,1)} %pad_maximum_fusion.1.w_in, bf16[5,1024,320]{2,1,0:T(8,128)(2,1)} %constant.109.clone.tc, bf16[5,1024,320]{2,1,0:T(8,128)(2,1)} %constant.110.clone.ts), custom_call_target="tpu_custom_call" | custom-call | flops 1677721600 | bytes 12582912 | tf_op jit(solution)/shard_map/head/pallas_call | solution.py:96
  40.6 9.5 %all-to-all-start.1 = ((bf16[64,16,384]{2,1,0:T(8,128)(2,1)}), bf16[64,16,384]{2,1,0:T(8,128)(2,1)S(1)}, u32[]{:S(2)}, u32[]{:S(2)}) async-start(bf16[64,16,384]{2,1,0:T(8,128)(2,1)} %bitcast.69), calls=%async_computation.1 | async-start | bytes 1572864 | tf_op jit(solution)/shard_map/all_to_all | solution.py:385
  70.4 11.3 %frequency.1 = (bf16[1024,384]{1,0:T(8,128)(2,1)}, bf16[1024,384]{1,0:T(8,128)(2,1)}) custom-call(bf16[1024,384]{1,0:T(8,128)(2,1)} %bitcast.68, bf16[1024,1024]{1,0:T(8,128)(2,1)} %constant.111.clone.tc, bf16[1024,1024]{1,0:T(8,128)(2,1)} %constant.112.clone.ts, bf16[384,384]{1,0:T(8,128)(2,1)} %copy.46.w_freq, f32[1024,1]{1,0:T(8,128)} %copy.47.weight, ...), custom_call_target="tpu_custom_call" | custom-call | flops 3221225472 | bytes 7340032 | tf_op jit(solution)/shard_map/frequency/pallas_call | solution.py:96
  81.7 4.9 %collective-permute-done.3.refs_2_ = bf16[5,80,512]{2,1,0:T(8,128)(2,1)S(1)} collective-permute-done((bf16[5,80,512]{2,1,0:T(8,128)(2,1)}, bf16[5,80,512]{2,1,0:T(8,128)(2,1)S(1)}, u32[]{:S(2)}, u32[]{:S(2)}) %collective-permute-start.3) | collective-permute-done | bytes 409632 | tf_op jit(solution)/shard_map/ppermute | solution.py:400
  87.4 12.4 %all-to-all-start.2 = ((bf16[64,16,384]{2,1,0:T(8,128)(2,1)}), bf16[64,16,384]{2,1,0:T(8,128)(2,1)S(1)}, u32[]{:S(2)}, u32[]{:S(2)}) async-start(bf16[64,16,384]{2,1,0:T(8,128)(2,1)} %bitcast.72), calls=%async_computation.2 | async-start | bytes 1572864 | tf_op jit(solution)/shard_map/all_to_all | solution.py:385
  101.2 8.7 %conv.1.pre = f32[5,320,512]{2,1,0:T(8,128)} custom-call(bf16[1,320,512]{2,1,0:T(8,128)(2,1)} %collective-permute-done.above, bf16[5,320,512]{2,1,0:T(8,128)(2,1)} %get-tuple-element.63.masked, bf16[1,320,512]{2,1,0:T(8,128)(2,1)} %collective-permute-done.1.below, bf16[3,512,384]{2,1,0:T(8,128)(2,1)} %copy.48.w_local, bf16[384,1152]{1,0:T(8,128)(2,1)} %bitcast.67), custom_call_target="tpu_custom_call" | custom-call | flops 3303014400 | bytes 9437184 | tf_op jit(solution)/shard_map/conv/pallas_call | solution.py:96
  110.0 5.2 %all-to-all-done.2 = bf16[64,16,384]{2,1,0:T(8,128)(2,1)S(1)} async-done(((bf16[64,16,384]{2,1,0:T(8,128)(2,1)}), bf16[64,16,384]{2,1,0:T(8,128)(2,1)S(1)}, u32[]{:S(2)}, u32[]{:S(2)}) %all-to-all-start.2) | async-done | bytes 786464 | tf_op jit(solution)/shard_map/all_to_all | solution.py:385
  116.1 15.8 %middle.1 = (bf16[5,320,512]{2,1,0:T(8,128)(2,1)}, bf16[5,320,512]{2,1,0:T(8,128)(2,1)}, bf16[5,320,256]{2,1,0:T(8,128)(2,1)}, bf16[1024,384]{1,0:T(8,128)(2,1)}, bf16[192,384]{1,0:T(8,128)(2,1)}) custom-call(bf16[1024,384]{1,0:T(8,128)(2,1)} %bitcast.57, bf16[5,320,1024]{2,1,0:T(8,128)(2,1)} %constant.107.clone.tct, ...), custom_call_target="tpu_custom_call" | custom-call | flops 3355443200 | bytes 25165824 | tf_op jit(solution)/shard_map/middle/pallas_call | solution.py:96
  131.9 4.7 %all-to-all-start.3 = ((bf16[64,16,384]{2,1,0:T(8,128)(2,1)}), bf16[64,16,384]{2,1,0:T(8,128)(2,1)S(1)}, u32[]{:S(2)}, u32[]{:S(2)}) async-start(bf16[64,16,384]{2,1,0:T(8,128)(2,1)} %bitcast.71), calls=%async_computation.3 | async-start | bytes 1572864 | tf_op jit(solution)/shard_map/all_to_all | solution.py:385
  136.6 11.1 %conv_grad.1 = bf16[2,1536,384]{2,1,0:T(8,128)(2,1)} custom-call(bf16[1,320,512]{2,1,0:T(8,128)(2,1)} %collective-permute-done.above, bf16[5,320,512]{2,1,0:T(8,128)(2,1)} %get-tuple-element.63.masked, bf16[1,320,512]{2,1,0:T(8,128)(2,1)} %collective-permute-done.1.below, bf16[5,320,512]{2,1,0:T(8,128)(2,1)} %get-tuple-element.81.d_out, ...), custom_call_target="tpu_custom_call" | custom-call | flops 3303014400 | bytes 7340032 | tf_op jit(solution)/shard_map/conv_grad/pallas_call | solution.py:96
  170.1 7.8 %all-to-all-start.4 = ((bf16[32,48,384]{2,1,0:T(8,128)(2,1)}), bf16[32,48,384]{2,1,0:T(8,128)(2,1)S(1)}, u32[]{:S(2)}, u32[]{:S(2)}) async-start(bf16[32,48,384]{2,1,0:T(8,128)(2,1)} %bitcast.27), calls=%async_computation.4 | async-start | bytes 2359296 | tf_op jit(solution)/shard_map/all_to_all | solution.py:418
  178.0 13.5 %frequency_back.1 = (bf16[1024,384]{1,0:T(8,128)(2,1)}, bf16[384,384]{1,0:T(8,128)(2,1)}) custom-call(bf16[1024,384]{1,0:T(8,128)(2,1)} %bitcast.70, bf16[1024,1024]{1,0:T(8,128)(2,1)} %constant.111.clone.tc, bf16[1024,1024]{1,0:T(8,128)(2,1)} %constant.112.clone.ts, bf16[384,384]{1,0:T(8,128)(2,1)} %copy.46.w_freq, bf16[384,384]{1,0:T(8,128)(2,1)} %bitcast.64, ...), custom_call_target="tpu_custom_call" | custom-call | flops 3221225472 | bytes 8388608 | tf_op jit(solution)/shard_map/frequency_back/pallas_call | solution.py:96
  195.5 4.9 %all-to-all-start.5 = ((bf16[64,16,384]{2,1,0:T(8,128)(2,1)}), bf16[64,16,384]{2,1,0:T(8,128)(2,1)S(1)}, u32[]{:S(2)}, u32[]{:S(2)}) async-start(bf16[64,16,384]{2,1,0:T(8,128)(2,1)} %bitcast.73), calls=%async_computation.5 | async-start | bytes 1572864 | tf_op jit(solution)/shard_map/all_to_all | solution.py:385
  200.4 10.5 %conv_back.1.d_conv = f32[5,320,512]{2,1,0:T(8,128)} custom-call(bf16[1,320,512]{2,1,0:T(8,128)(2,1)} %copy-done.26, bf16[5,320,512]{2,1,0:T(8,128)(2,1)} %get-tuple-element.81.d_out, bf16[1,320,512]{2,1,0:T(8,128)(2,1)} %copy-done.27, bf16[3,384,512]{2,1,0:T(8,128)(2,1)} %bitcast.65, bf16[3,1152,128]{2,1,0:T(8,128)(2,1)} %bitcast.66), custom_call_target="tpu_custom_call" | custom-call | flops 3303014400 | bytes 9437184 | tf_op jit(solution)/shard_map/conv_back/pallas_call | solution.py:96
  210.9 4.9 %all-to-all-done.5 = bf16[64,16,384]{2,1,0:T(8,128)(2,1)S(1)} async-done(((bf16[64,16,384]{2,1,0:T(8,128)(2,1)}), bf16[64,16,384]{2,1,0:T(8,128)(2,1)S(1)}, u32[]{:S(2)}, u32[]{:S(2)}) %all-to-all-start.5) | async-done | bytes 786464 | tf_op jit(solution)/shard_map/all_to_all | solution.py:385
  221.0 9.4 %tail.1 = (bf16[5,320,256]{2,1,0:T(8,128)(2,1)}, bf16[2048,128]{1,0:T(8,128)(2,1)}) custom-call(bf16[1024,384]{1,0:T(8,128)(2,1)} %bitcast.58, bf16[5,320,1024]{2,1,0:T(8,128)(2,1)} %constant.107.clone.tct, bf16[5,320,1024]{2,1,0:T(8,128)(2,1)} %constant.108.clone.tst, bf16[5,320,512]{2,1,0:T(8,128)(2,1)} %get-tuple-element.63.masked, ...), custom_call_target="tpu_custom_call" | custom-call | flops 1677721600 | bytes 16777216 | tf_op jit(solution)/shard_map/tail/pallas_call | solution.py:96
  230.4 8.1 %all-to-all-done.6 = bf16[32,48,384]{2,1,0:T(8,128)(2,1)S(1)} async-done(((bf16[32,48,384]{2,1,0:T(8,128)(2,1)}), bf16[32,48,384]{2,1,0:T(8,128)(2,1)S(1)}, u32[]{:S(2)}, u32[]{:S(2)}) %all-to-all-start.6) | async-done | bytes 1179680 | tf_op jit(solution)/shard_map/all_to_all | solution.py:418
  240.2 4.8 %all-to-all-start.7 = ((bf16[64,32,128]{2,1,0:T(8,128)(2,1)}), bf16[64,32,128]{2,1,0:T(8,128)(2,1)S(1)}, u32[]{:S(2)}, u32[]{:S(2)}) async-start(bf16[64,32,128]{2,1,0:T(8,128)(2,1)} %bitcast.75), calls=%async_computation.7 | async-start | bytes 1048576 | tf_op jit(solution)/shard_map/all_to_all | solution.py:428
  245.0 5.5 %finish.1 = bf16[5,320,512]{2,1,0:T(8,128)(2,1)} custom-call(bf16[4,5,80,512]{3,2,1,0:T(8,128)(2,1)} %copy-done, bf16[5,320,256]{2,1,0:T(8,128)(2,1)} %get-tuple-element.102.d_unit, f32[5,320,512]{2,1,0:T(8,128)} %conv_back.1.d_conv, bf16[256,384]{1,0:T(8,128)(2,1)} %pad.7.w_in_t), custom_call_target="tpu_custom_call" | custom-call | flops 314572800 | bytes 7340032 | tf_op jit(solution)/shard_map/finish/pallas_call | solution.py:96
  250.6 7.1 %all-to-all-done.7 = bf16[64,32,128]{2,1,0:T(8,128)(2,1)S(1)} async-done(((bf16[64,32,128]{2,1,0:T(8,128)(2,1)}), bf16[64,32,128]{2,1,0:T(8,128)(2,1)S(1)}, u32[]{:S(2)}, u32[]{:S(2)}) %all-to-all-start.7) | async-done | bytes 524320 | tf_op jit(solution)/shard_map/all_to_all | solution.py:428
  258.6 4.6 %all-to-all-start.8 = ((bf16[64,32,128]{2,1,0:T(8,128)(2,1)}), bf16[64,32,128]{2,1,0:T(8,128)(2,1)S(1)}, u32[]{:S(2)}, u32[]{:S(2)}) async-start(bf16[64,32,128]{2,1,0:T(8,128)(2,1)} %broadcast_in_dim.43), calls=%async_computation.8 | async-start | bytes 1048576 | tf_op jit(solution)/shard_map/all_to_all | solution.py:433
  268.3 7.7 %all-to-all-done.8 = bf16[64,32,128]{2,1,0:T(8,128)(2,1)S(1)} async-done(((bf16[64,32,128]{2,1,0:T(8,128)(2,1)}), bf16[64,32,128]{2,1,0:T(8,128)(2,1)S(1)}, u32[]{:S(2)}, u32[]{:S(2)}) %all-to-all-start.8) | async-done | bytes 524320 | tf_op jit(solution)/shard_map/all_to_all | solution.py:433
  (127 shorter events, 82.2 us)
Async XLA Ops:
  4.3 25.5 %all-to-all-start = ((bf16[4,5,80,512]{3,2,1,0:T(8,128)(2,1)}), bf16[4,5,80,512]{3,2,1,0:T(8,128)(2,1)S(1)}, u32[]{:S(2)}, u32[]{:S(2)}) async-start(bf16[4,5,80,512]{3,2,1,0:T(8,128)(2,1)} %broadcast_select_fusion), calls=%async_computation | async-start | bytes 3276800 | tf_op jit(solution)/shard_map/all_to_all | solution.py:390
  22.4 42.2 %copy-start.13 = (bf16[384,384]{0,1:T(8,128)(2,1)}, bf16[384,384]{0,1:T(8,128)(2,1)S(1)}, u32[]{:S(2)}) copy-start(bf16[384,384]{0,1:T(8,128)(2,1)S(1)} %fusion.11) | copy-start | bytes 884740
  40.6 18.3 %copy-start.7 = (bf16[1,20,80,512]{3,2,1,0:T(8,128)(2,1)S(1)}, bf16[1,20,80,512]{3,2,1,0:T(8,128)(2,1)}, u32[]{:S(2)}) copy-start(bf16[1,20,80,512]{3,2,1,0:T(8,128)(2,1)} %param.17) | copy-start | bytes 4915204
  40.6 28.9 %all-to-all-start.1 = ((bf16[64,16,384]{2,1,0:T(8,128)(2,1)}), bf16[64,16,384]{2,1,0:T(8,128)(2,1)S(1)}, u32[]{:S(2)}, u32[]{:S(2)}) async-start(bf16[64,16,384]{2,1,0:T(8,128)(2,1)} %bitcast.69), calls=%async_computation.1 | async-start | bytes 1572864 | tf_op jit(solution)/shard_map/all_to_all | solution.py:385
  52.0 17.4 %collective-permute-start = (bf16[1,320,512]{2,1,0:T(8,128)(2,1)}, bf16[1,320,512]{2,1,0:T(8,128)(2,1)}, u32[]{:S(2)}, u32[]{:S(2)}) collective-permute-start(bf16[1,320,512]{2,1,0:T(8,128)(2,1)} %get-tuple-element.122), channel_id=1, source_target_pairs={{0,1},{1,2},{2,3},{3,4},{4,5},{5,6},{6,7},{7,8},{8,9},{9,10},{10,1... | collective-permute-start | bytes 983048 | tf_op jit(solution)/shard_map/ppermute | solution.py:422
  55.3 14.2 %collective-permute-start.1 = (bf16[1,320,512]{2,1,0:T(8,128)(2,1)}, bf16[1,320,512]{2,1,0:T(8,128)(2,1)}, u32[]{:S(2)}, u32[]{:S(2)}) collective-permute-start(bf16[1,320,512]{2,1,0:T(8,128)(2,1)} %get-tuple-element.121), channel_id=1, source_target_pairs={{1,0},{2,1},{3,2},{4,3},{5,4},{6,5},{7,6},{8,7},{9,8},{10,9},{11,1... | collective-permute-start | bytes 983048 | tf_op jit(solution)/shard_map/ppermute | solution.py:423
  60.1 21.6 %collective-permute-start.2 = (bf16[5,80,512]{2,1,0:T(8,128)(2,1)}, bf16[5,80,512]{2,1,0:T(8,128)(2,1)S(1)}, u32[]{:S(2)}, u32[]{:S(2)}) collective-permute-start(bf16[5,80,512]{2,1,0:T(8,128)(2,1)} %get-tuple-element.119), channel_id=1, source_target_pairs={{0,1},{1,2},{2,3},{3,0},{4,5},{5,6},{6,7},{7,4},{8,9},{9,10},{10,1... | collective-permute-start | bytes 1228808 | tf_op jit(solution)/shard_map/ppermute | solution.py:400
  60.1 26.5 %collective-permute-start.3 = (bf16[5,80,512]{2,1,0:T(8,128)(2,1)}, bf16[5,80,512]{2,1,0:T(8,128)(2,1)S(1)}, u32[]{:S(2)}, u32[]{:S(2)}) collective-permute-start(bf16[5,80,512]{2,1,0:T(8,128)(2,1)} %get-tuple-element.118), channel_id=1, source_target_pairs={{0,2},{1,3},{2,0},{3,1},{4,6},{5,7},{6,4},{7,5},{8,10},{9,11},{10,... | collective-permute-start | bytes 1228808 | tf_op jit(solution)/shard_map/ppermute | solution.py:400
  62.4 24.2 %collective-permute-start.4 = (bf16[5,80,512]{2,1,0:T(8,128)(2,1)}, bf16[5,80,512]{2,1,0:T(8,128)(2,1)S(1)}, u32[]{:S(2)}, u32[]{:S(2)}) collective-permute-start(bf16[5,80,512]{2,1,0:T(8,128)(2,1)} %get-tuple-element.117), channel_id=1, source_target_pairs={{0,3},{1,0},{2,1},{3,2},{4,7},{5,4},{6,5},{7,6},{8,11},{9,8},{10,9... | collective-permute-start | bytes 1228808 | tf_op jit(solution)/shard_map/ppermute | solution.py:400
  81.7 18.1 %copy-start.3 = (bf16[3,3,512,128]{2,3,1,0:T(8,128)(2,1)S(1)}, bf16[3,3,512,128]{2,3,1,0:T(8,128)(2,1)}, u32[]{:S(2)}) copy-start(bf16[3,3,512,128]{2,3,1,0:T(8,128)(2,1)} %copy.42) | copy-start | bytes 3538948
  81.7 19.5 %copy-start.23 = (bf16[5,80,512]{2,1,0:T(8,128)(2,1)}, bf16[5,80,512]{2,1,0:T(8,128)(2,1)S(1)}, u32[]{:S(2)}) copy-start(bf16[5,80,512]{2,1,0:T(8,128)(2,1)S(1)} %collective-permute-done.2.refs_1_) | copy-start | bytes 1228804
  86.6 14.7 %copy-start.24 = (bf16[5,80,512]{2,1,0:T(8,128)(2,1)}, bf16[5,80,512]{2,1,0:T(8,128)(2,1)S(1)}, u32[]{:S(2)}) copy-start(bf16[5,80,512]{2,1,0:T(8,128)(2,1)S(1)} %collective-permute-done.3.refs_2_) | copy-start | bytes 1228804
  87.4 27.8 %all-to-all-start.2 = ((bf16[64,16,384]{2,1,0:T(8,128)(2,1)}), bf16[64,16,384]{2,1,0:T(8,128)(2,1)S(1)}, u32[]{:S(2)}, u32[]{:S(2)}) async-start(bf16[64,16,384]{2,1,0:T(8,128)(2,1)} %bitcast.72), calls=%async_computation.2 | async-start | bytes 1572864 | tf_op jit(solution)/shard_map/all_to_all | solution.py:385
  131.9 20.2 %all-to-all-start.3 = ((bf16[64,16,384]{2,1,0:T(8,128)(2,1)}), bf16[64,16,384]{2,1,0:T(8,128)(2,1)S(1)}, u32[]{:S(2)}, u32[]{:S(2)}) async-start(bf16[64,16,384]{2,1,0:T(8,128)(2,1)} %bitcast.71), calls=%async_computation.3 | async-start | bytes 1572864 | tf_op jit(solution)/shard_map/all_to_all | solution.py:385
  154.5 8.6 %collective-permute-start.5 = (bf16[1536,384]{1,0:T(8,128)(2,1)S(1)}, bf16[1536,384]{1,0:T(8,128)(2,1)}, u32[]{:S(2)}, u32[]{:S(2)}) collective-permute-start(bf16[1536,384]{1,0:T(8,128)(2,1)S(1)} %dynamic-slice_bitcast_fusion), channel_id=1, source_target_pairs={{0,4},{4,0},{8,12},{12,8},{16,20},{20,16},{24,28},{28,24},{32,36},... | collective-permute-start | bytes 3538952 | tf_op jit(solution)/shard_map/ppermute | solution.py:409
  156.3 12.4 %collective-permute-start.6 = (bf16[1,320,512]{2,1,0:T(8,128)(2,1)S(1)}, bf16[1,320,512]{2,1,0:T(8,128)(2,1)S(1)}, u32[]{:S(2)}, u32[]{:S(2)}) collective-permute-start(bf16[1,320,512]{2,1,0:T(8,128)(2,1)S(1)} %get-tuple-element.116), channel_id=1, source_target_pairs={{0,1},{1,2},{2,3},{3,4},{4,5},{5,6},{6,7},{7,8},{8,9},{9,10},{10,1... | collective-permute-start | bytes 983048 | tf_op jit(solution)/shard_map/ppermute | solution.py:422
  158.5 10.9 %collective-permute-start.7 = (bf16[1,320,512]{2,1,0:T(8,128)(2,1)S(1)}, bf16[1,320,512]{2,1,0:T(8,128)(2,1)S(1)}, u32[]{:S(2)}, u32[]{:S(2)}) collective-permute-start(bf16[1,320,512]{2,1,0:T(8,128)(2,1)S(1)} %get-tuple-element.115), channel_id=1, source_target_pairs={{1,0},{2,1},{3,2},{4,3},{5,4},{6,5},{7,6},{8,7},{9,8},{10,9},{11,1... | collective-permute-start | bytes 983048 | tf_op jit(solution)/shard_map/ppermute | solution.py:423
  170.1 25.4 %all-to-all-start.4 = ((bf16[32,48,384]{2,1,0:T(8,128)(2,1)}), bf16[32,48,384]{2,1,0:T(8,128)(2,1)S(1)}, u32[]{:S(2)}, u32[]{:S(2)}) async-start(bf16[32,48,384]{2,1,0:T(8,128)(2,1)} %bitcast.27), calls=%async_computation.4 | async-start | bytes 2359296 | tf_op jit(solution)/shard_map/all_to_all | solution.py:418
  195.5 20.3 %all-to-all-start.5 = ((bf16[64,16,384]{2,1,0:T(8,128)(2,1)}), bf16[64,16,384]{2,1,0:T(8,128)(2,1)S(1)}, u32[]{:S(2)}, u32[]{:S(2)}) async-start(bf16[64,16,384]{2,1,0:T(8,128)(2,1)} %bitcast.73), calls=%async_computation.5 | async-start | bytes 1572864 | tf_op jit(solution)/shard_map/all_to_all | solution.py:385
  217.1 21.4 %all-to-all-start.6 = ((bf16[32,48,384]{2,1,0:T(8,128)(2,1)}), bf16[32,48,384]{2,1,0:T(8,128)(2,1)S(1)}, u32[]{:S(2)}, u32[]{:S(2)}) async-start(bf16[32,48,384]{2,1,0:T(8,128)(2,1)} %reshape_tile.3), calls=%async_computation.6 | async-start | bytes 2359296 | tf_op jit(solution)/shard_map/all_to_all | solution.py:418
  238.5 12.1 %copy-start.1 = (bf16[32,48,384]{2,1,0:T(8,128)(2,1)}, bf16[32,48,384]{2,1,0:T(8,128)(2,1)S(1)}, u32[]{:S(2)}) copy-start(bf16[32,48,384]{2,1,0:T(8,128)(2,1)S(1)} %all-to-all-done.6) | copy-start | bytes 3538948
  238.5 24.8 %collective-permute-start.8 = (bf16[1536,384]{1,0:T(8,128)(2,1)S(1)}, bf16[1536,384]{1,0:T(8,128)(2,1)S(1)}, u32[]{:S(2)}, u32[]{:S(2)}) collective-permute-start(bf16[1536,384]{1,0:T(8,128)(2,1)S(1)} %bitcast.50), channel_id=1, source_target_pairs={{0,4},{4,0},{8,12},{12,8},{16,20},{20,16},{24,28},{28,24},{32,36},... | collective-permute-start | bytes 3538952 | tf_op jit(solution)/shard_map/ppermute | solution.py:600
  240.2 17.5 %all-to-all-start.7 = ((bf16[64,32,128]{2,1,0:T(8,128)(2,1)}), bf16[64,32,128]{2,1,0:T(8,128)(2,1)S(1)}, u32[]{:S(2)}, u32[]{:S(2)}) async-start(bf16[64,32,128]{2,1,0:T(8,128)(2,1)} %bitcast.75), calls=%async_computation.7 | async-start | bytes 1048576 | tf_op jit(solution)/shard_map/all_to_all | solution.py:428
  258.6 17.4 %all-to-all-start.8 = ((bf16[64,32,128]{2,1,0:T(8,128)(2,1)}), bf16[64,32,128]{2,1,0:T(8,128)(2,1)S(1)}, u32[]{:S(2)}, u32[]{:S(2)}) async-start(bf16[64,32,128]{2,1,0:T(8,128)(2,1)} %broadcast_in_dim.43), calls=%async_computation.8 | async-start | bytes 1048576 | tf_op jit(solution)/shard_map/all_to_all | solution.py:433
  (27 other events, 81.9 us)

commit v4 on v3

--- a/solution.py
+++ b/solution.py
@@ -20,32 +20,17 @@
     return lax.dot_general(a, b, (dims, ((), ())), preferred_element_type=F32)
 
 
-def line_tables(rows, width, count, lines, slots):
-    cos = np.zeros((rows, count, slots, width), np.float32)
-    sin = np.zeros((rows, count, slots, width), np.float32)
-    freq = lines * np.arange(count)[:, None] + np.arange(lines)[None]
-    angle = 2.0 * np.pi * (freq[..., None] * np.arange(width) % width) / width
-    valid = (freq <= width // 2)[..., None]
-    for y in range(rows):
-        cos[y, :, y * lines : (y + 1) * lines] = np.cos(angle) * valid
-        sin[y, :, y * lines : (y + 1) * lines] = np.sin(angle) * valid
-    shape = (rows, count * slots, width)
-    return cos.reshape(shape).astype(BF), sin.reshape(shape).astype(BF)
-
-
-def column_tables(rows, count, lines, slots):
-    height = rows * count
-    cos = np.zeros((count, slots, count, slots), np.float32)
-    sin = np.zeros((count, slots, count, slots), np.float32)
-    h = np.arange(height).reshape(count, rows)
-    angle = 2.0 * np.pi * (h[:, :, None, None] * h[None, None] % height) / height
-    for y in range(rows):
-        for z in range(rows):
-            for j in range(lines):
-                cos[:, y * lines + j, :, z * lines + j] = np.cos(angle[:, y, :, z])
-                sin[:, y * lines + j, :, z * lines + j] = np.sin(angle[:, y, :, z])
-    shape = (count * slots, count * slots)
-    return cos.reshape(shape).astype(BF), sin.reshape(shape).astype(BF)
+def line_tables(width, count, lines):
+    freq = (lines * np.arange(count)[None] + np.arange(lines)[:, None]).reshape(-1, 1)
+    angle = 2.0 * np.pi * (freq * np.arange(width) % width) / width
+    valid = freq <= width // 2
+    return (np.cos(angle) * valid).astype(BF), (np.sin(angle) * valid).astype(BF)
+
+
+def column_tables(rows, count):
+    h = (rows * np.arange(count)[None] + np.arange(rows)[:, None]).reshape(-1)
+    angle = 2.0 * np.pi * (h[:, None] * h[None] % (rows * count)) / (rows * count)
+    return np.cos(angle).astype(BF), np.sin(angle).astype(BF)
 
 
 def slope_and_silu(value):
@@ -86,7 +71,7 @@
 
 def call(body, name, grid, ins, outs, scratch=(), flops=0, bytes_=0):
     def spec(shape, block, index):
-        if shape == (1, 1):
+        if shape[0] == 1 and shape[-1] < 8:
             return pl.BlockSpec(memory_space=pltpu.SMEM)
         if block is None:
             zeros = (0,) * len(shape)
@@ -106,7 +91,34 @@
     )(*[a for a, _, _ in ins])
 
 
-def head_kernel(norm, cl, marked, w_in, tc, ts, masked, unit, sent, acc_c, acc_s):
+def put_slots(sizes, z, value_of, sent):
+    rows, lines, count, slots = sizes
+    for q in range(slots):
+        value = value_of(q // lines, q % lines) if q < rows * lines else jnp.zeros((count, 384), F32)
+        for k in range(3):
+            z[k, pl.ds(q, count, stride=slots), :] = value[:, k * 128 : (k + 1) * 128]
+    for k in range(3):
+        sent[:, k * 128 : (k + 1) * 128] = z[k].astype(BF)
+
+
+def spread(got, z):
+    for k in range(3):
+        z[k] = got[:, k * 128 : (k + 1) * 128].astype(F32)
+
+
+def slot(sizes, z, q):
+    _, _, count, slots = sizes
+    return jnp.concatenate([z[k, pl.ds(q, count, stride=slots), :] for k in range(3)], 1)
+
+
+def take_slots(sizes, got, z, x):
+    rows, lines, count, slots = sizes
+    spread(got, z)
+    for q in range(rows * lines):
+        x[q * count : (q + 1) * count, :] = slot(sizes, z, q).astype(BF)
+
+
+def head_kernel(norm, sizes, cl, marked, w_in, tc, ts, masked, unit, sent, v, z):
     y = pl.program_id(0)
     x = marked[...].reshape(-1, marked.shape[-1])
     keep = x[:, :1].astype(F32) < 0.5 * HOLE
@@ -114,80 +126,63 @@
     masked[0] = x
     u = slope_and_silu(dot(x[:, cl:], w_in[...]))[1].astype(BF)
     unit[0] = u
-    transform_out(y, norm, u, tc, ts, sent, acc_c, acc_s)
-
-
-def transform_out(y, norm, u, tc, ts, sent, acc_c, acc_s):
-    re, im = dot(tc[0], u), dot(ts[0], u)
-
-    @pl.when(y == 0)
-    def _():
-        acc_c[...] = re
-        acc_s[...] = im
-
-    @pl.when(y > 0)
-    def _():
-        acc_c[...] += re
-        acc_s[...] += im
+    transform_out(y, norm, sizes, u, tc, ts, sent, v, z)
+
+
+def transform_out(y, norm, sizes, u, tc, ts, sent, v, z):
+    count = sizes[2]
+    v[y] = packed(dot(tc[...], u) * norm, dot(ts[...], u) * -norm)
 
     @pl.when(y == pl.num_programs(0) - 1)
     def _():
-        sent[...] = packed(acc_c[...] * norm, acc_s[...] * -norm).astype(BF)
-
-
-def frequency_kernel(norm, tile, got, tc, ts, w_freq, weight, sign, stacked, sent, z):
-    def first(k, carry):
-        rows = pl.ds(pl.multiple_of(k * tile, tile), tile)
-        spec = turned(dot(tc[rows, :], got[...]), dot(ts[rows, :], got[...]), 1.0) * norm
-        st = spec.astype(BF)
-        stacked[rows, :] = st
+        put_slots(sizes, z, lambda row, j: v[row, j * count : (j + 1) * count, :], sent)
+
+
+def column_line(sizes, z, j):
+    rows, lines, count, slots = sizes
+    parts = [slot(sizes, z, row * lines + j) for row in range(rows)]
+    return jnp.concatenate(parts, 0).astype(BF)
+
+
+def frequency_kernel(norm, sizes, got, hc, hs, w_freq, weight, sign, stacked, sent, z, v):
+    count = sizes[2]
+    spread(got, z)
+    for j in range(sizes[1]):
+        x = column_line(sizes, z, j)
+        st = (turned(dot(hc[...], x), dot(hs[...], x), 1.0) * norm).astype(BF)
+        stacked[j] = st
         pos = slope_and_silu(dot(st, w_freq[...]))[1]
         neg = slope_and_silu(dot((st.astype(F32) * sign[...]).astype(BF), w_freq[...]))[1]
-        z[rows, :] = (weight[rows, :] * (pos + sign[...] * neg)).astype(BF)
-        return carry
-
-    def second(k, carry):
-        rows = pl.ds(pl.multiple_of(k * tile, tile), tile)
-        sent[rows, :] = (turned(dot(tc[rows, :], z[...]), dot(ts[rows, :], z[...]), -1.0) * norm).astype(BF)
-        return carry
-
-    steps = got.shape[0] // tile
-    lax.fori_loop(0, steps, first, 0)
-    lax.fori_loop(0, steps, second, 0)
+        x = (weight[0, j] * (pos + sign[...] * neg)).astype(BF)
+        v[j] = turned(dot(hc[...], x), dot(hs[...], x), -1.0) * norm
+    put_slots(sizes, z, lambda row, j: v[j, row * count : (row + 1) * count, :], sent)
 
 
 def frequency_back_kernel(
-    norm, tile, got, tc, ts, w_freq, w_freq_t, weight, sign, stacked, sent, grad, z, acc_p, acc_m
+    norm, sizes, got, hc, hs, w_freq, w_freq_t, weight, sign, stacked, sent, grad, z, v, acc_p, acc_m
 ):
-    acc_p[...] = jnp.zeros_like(acc_p)
-    acc_m[...] = jnp.zeros_like(acc_m)
-
-    def first(k, carry):
-        rows = pl.ds(pl.multiple_of(k * tile, tile), tile)
-        dz = turned(dot(tc[rows, :], got[...]), dot(ts[rows, :], got[...]), 1.0) * norm
-        st = stacked[rows, :]
+    count = sizes[2]
+    spread(got, z)
+    for j in range(sizes[1]):
+        x = column_line(sizes, z, j)
+        dz = turned(dot(hc[...], x), dot(hs[...], x), 1.0) * norm
+        st = stacked[j]
         pos = slope_and_silu(dot(st, w_freq[...]))[0]
         neg = slope_and_silu(dot((st.astype(F32) * sign[...]).astype(BF), w_freq[...]))[0]
         pos = (dz * pos).astype(BF).astype(F32)
         neg = (dz * sign[...] * neg).astype(BF).astype(F32)
-        total = (weight[rows, :] * (pos + neg)).astype(BF)
-        delta = (weight[rows, :] * (pos - neg)).astype(BF)
-        acc_p[...] += dot(st[:, :256], total, ROWS_OF)
-        acc_m[...] += dot(st[:, 128:], delta, ROWS_OF)
+        total = (weight[0, j] * (pos + neg)).astype(BF)
+        delta = (weight[0, j] * (pos - neg)).astype(BF)
+        g_p = dot(st[:, :256], total, ROWS_OF)
+        g_m = dot(st[:, 128:], delta, ROWS_OF)
+        acc_p[...] = g_p if j == 0 else acc_p[...] + g_p
+        acc_m[...] = g_m if j == 0 else acc_m[...] + g_m
         re = dot(total, w_freq_t[:, :256])
         im = dot(delta, w_freq_t[:, 128:])
-        mid = jnp.where(lanes_below((tile, 128), 64), re[:, 128:], im[:, :128])
-        z[rows, :] = jnp.concatenate([re[:, :128], mid, im[:, 128:]], 1).astype(BF)
-        return carry
-
-    def second(k, carry):
-        rows = pl.ds(pl.multiple_of(k * tile, tile), tile)
-        sent[rows, :] = (turned(dot(tc[rows, :], z[...]), dot(ts[rows, :], z[...]), -1.0) * norm).astype(BF)
-        return carry
-
-    steps = got.shape[0] // tile
-    lax.fori_loop(0, steps, first, 0)
-    lax.fori_loop(0, steps, second, 0)
+        mid = jnp.where(lanes_below((re.shape[0], 128), 64), re[:, 128:], im[:, :128])
+        x = jnp.concatenate([re[:, :128], mid, im[:, 128:]], 1).astype(BF)
+        v[j] = turned(dot(hc[...], x), dot(hs[...], x), -1.0) * norm
+    put_slots(sizes, z, lambda row, j: v[j, row * count : (row + 1) * count, :], sent)
     grad[0:192, :] = natural_lanes(acc_p[0:192, :]).astype(BF)
     grad[192:320, :] = natural_lanes(acc_m[128:256, :]).astype(BF)
     grad[320:384, :] = natural_lanes(acc_m[64:128, :]).astype(BF)
@@ -198,22 +193,29 @@
     return jnp.concatenate([got[:, 256:], mid], 1)
 
 
+def line_back(y, norm, sizes, got, tct, tst, z, got_x, got_s):
+    @pl.when(y == 0)
+    def _():
+        take_slots(sizes, got, z, got_x)
+        got_s[...] = imag_first(got_x[...])
+
+    size = sizes[1] * sizes[2]
+    at = pl.ds(pl.multiple_of(y * size, size), size)
+    return ((dot(tct[...], got_x[at, :256]) - dot(tst[...], got_s[at, :])) * norm).astype(BF)
+
+
 def middle_kernel(
-    norm, cl, cols, got, tct, tst, tc, ts, unit, pre, w_out, w_out_t, my_col, *refs,
+    norm, sizes, cl, cols, got, tct, tst, tc, ts, unit, pre, w_out, w_out_t, my_col, *refs,
 ):
     cots = refs[:cols]
-    output, d_out, d_joined, sent, grad, got_s, cot, acc_c, acc_s, acc_g = refs[cols:]
+    output, d_out, d_joined, sent, grad, got_x, got_s, cot, v, z, acc_g = refs[cols:]
     y = pl.program_id(0)
     w = cots[0].shape[1]
     for k in range(cols):
         at = lax.rem(my_col[0, 0] + (cols - k), cols)
         cot[pl.ds(pl.multiple_of(at * w, w), w), :] = cots[k][0]
 
-    @pl.when(y == 0)
-    def _():
-        got_s[...] = imag_first(got[...])
-
-    back = ((dot(tct[0], got[:, :256]) - dot(tst[0], got_s[...])) * norm).astype(BF)
+    back = line_back(y, norm, sizes, got, tct, tst, z, got_x, got_s)
     joined = (unit[0].astype(F32) + back.astype(F32)).astype(BF)
     pre_all = jnp.concatenate([pre[0, :, :cl], pre[0, :, cl:] + dot(joined, w_out[...])], 1)
     slope, silu = slope_and_silu(pre_all)
@@ -232,7 +234,7 @@
     def _():
         acc_g[...] += g
 
-    transform_out(y, norm, dj, tc, ts, sent, acc_c, acc_s)
+    transform_out(y, norm, sizes, dj, tc, ts, sent, v, z)
 
     @pl.when(y == pl.num_programs(0) - 1)
     def _():
@@ -240,15 +242,11 @@
 
 
 def tail_kernel(
-    norm, cl, got, tct, tst, masked, d_joined, w_in, grad_freq, d_unit, late, got_s, acc_g
+    norm, sizes, cl, got, tct, tst, masked, d_joined, w_in, grad_freq, d_unit, late, got_x, got_s, z, acc_g
 ):
     y = pl.program_id(0)
 
-    @pl.when(y == 0)
-    def _():
-        got_s[...] = imag_first(got[...])
-
-    back = ((dot(tct[0], got[:, :256]) - dot(tst[0], got_s[...])) * norm).astype(BF)
+    back = line_back(y, norm, sizes, got, tct, tst, z, got_x, got_s)
     x = masked[0, :, cl:]
     slope = slope_and_silu(dot(x, w_in[...]))[0]
     du = ((d_joined[0].astype(F32) + back.astype(F32)) * slope).astype(BF)
@@ -453,15 +451,15 @@
     lines = -(-(width // 2 + 1) // count)
     slots = -(-(rows * lines) // 16) * 16
     n = count * slots
-    tile = min(256, n)
-    tc, ts = line_tables(rows, width, count, lines, slots)
-    tct, tst = jnp.asarray(tc.transpose(0, 2, 1)), jnp.asarray(ts.transpose(0, 2, 1))
+    sizes = (rows, lines, count, slots)
+    tc, ts = line_tables(width, count, lines)
+    tct, tst = jnp.asarray(tc.T), jnp.asarray(ts.T)
     tc, ts = jnp.asarray(tc), jnp.asarray(ts)
-    hc, hs = (jnp.asarray(t) for t in column_tables(rows, count, lines, slots))
+    hc, hs = (jnp.asarray(t) for t in column_tables(rows, count))
     norm_w, norm_h = 1.0 / math.sqrt(width), 1.0 / math.sqrt(height)
-    freq = lines * me + jnp.arange(slots) % lines
+    freq = lines * me + jnp.arange(lines)
     weight = jnp.where((freq == 0) | (freq * 2 == width), 0.5, jnp.where(freq * 2 < width, 1.0, 0.0))
-    weight = jnp.tile(weight.astype(F32), count)[:, None]
+    weight = weight.astype(F32)[None]
     sign = np.where((np.arange(384) < 192), 1.0, -1.0).astype(np.float32)
     sign = jnp.asarray(sign[None])
 
@@ -480,11 +478,12 @@
     one_row = lambda c: (1, width, c)
     blocks = lambda c: (cols, 1, w, c)
     at_blocks = lambda y: (0, y, 0, 0)
-    line_table = (1, n, width)
-    back_table = (1, width, n)
     wide = (rows, width, ch)
     pix = rows * width
     vm = pltpu.VMEM
+    lined = (rows, lines * count, 384)
+    spectral = (lines, height, 384)
+    used = rows * lines * count
 
     marked = jnp.where(hole_mask[0][..., None] == 1, HOLE, features[0]).astype(BF)
     marked = to_rows(marked, cols)
@@ -495,13 +494,13 @@
     my_col = lax.axis_index("col").astype(jnp.int32).reshape(1, 1)
 
     masked, unit, sent = call(
-        functools.partial(head_kernel, norm_w, cl),
+        functools.partial(head_kernel, norm_w, sizes, cl),
         "head",
         (rows,),
-        [(marked, blocks(ch), at_blocks), (w_in_d, None, None), (tc, line_table, at_y), (ts, line_table, at_y)],
+        [(marked, blocks(ch), at_blocks), (w_in_d, None, None), (tc, None, None), (ts, None, None)],
         [(wide, BF, one_row(ch), at_y), ((rows, width, 256), BF, one_row(256), at_y), ((n, 384), BF, None, None)],
-        [vm((n, 256), F32), vm((n, 256), F32)],
-        flops=4 * n * pix * 256, bytes_=12 << 20,
+        [vm(lined, F32), vm((3, n, 128), F32)],
+        flops=1 << 30, bytes_=6 << 20,
     )
     above, below = edges(masked, count)
     got = tie(swap(sent, count), above, below)
@@ -515,23 +514,23 @@
         flops=18 * pix * (ch * cl + cl * cg), bytes_=9 << 20,
     )
     stacked, sent = call(
-        functools.partial(frequency_kernel, norm_h, tile),
+        functools.partial(frequency_kernel, norm_h, sizes),
         "frequency",
         (1,),
         [(got, None, None), (hc, None, None), (hs, None, None), (w_freq_p, None, None), (weight, None, None), (sign, None, None)],
-        [((n, 384), BF, None, None), ((n, 384), BF, None, None)],
-        [vm((n, 384), BF)],
-        flops=8 * n * n * 384, bytes_=7 << 20,
+        [(spectral, BF, None, None), ((n, 384), BF, None, None)],
+        [vm((3, n, 128), F32), vm(spectral, F32)],
+        flops=3 << 30, bytes_=7 << 20,
     )
     sent, *cots = tied(sent, *cots)
     got = swap(sent, count)
     output, d_out, d_joined, sent, grad_out = call(
-        functools.partial(middle_kernel, norm_w, cl, cols),
+        functools.partial(middle_kernel, norm_w, sizes, cl, cols),
         "middle",
         (rows,),
         [
-            (got, None, None), (tct, back_table, at_y), (tst, back_table, at_y), (tc, line_table, at_y),
-            (ts, line_table, at_y), (unit, one_row(256), at_y), (pre, one_row(ch), at_y),
+            (got, None, None), (tct, None, None), (tst, None, None), (tc, None, None),
+            (ts, None, None), (unit, one_row(256), at_y), (pre, one_row(ch), at_y),
             (w_out_z, None, None), (w_out_t, None, None), (my_col, None, None),
         ]
         + [(c, (1, w, ch), at_y) for c in cots],
@@ -539,8 +538,8 @@
             (wide, BF, one_row(ch), at_y), (wide, BF, one_row(ch), at_y), ((rows, width, 256), BF, one_row(256), at_y),
             ((n, 384), BF, None, None), ((cs, cg), BF, None, None),
         ],
-        [vm((n, 256), BF), vm((width, ch), BF), vm((n, 256), F32), vm((n, 256), F32), vm((256, cg), F32)],
-        flops=8 * n * pix * 256, bytes_=24 << 20,
+        [vm((used, 384), BF), vm((used, 256), BF), vm((width, ch), BF), vm(lined, F32), vm((3, n, 128), F32), vm((256, cg), F32)],
+        flops=3 << 30, bytes_=12 << 20,
     )
     got = swap(sent, count)
     d_above, d_below = edges(d_out, count)
@@ -553,11 +552,11 @@
         [vm((rows + 2, width, ch), BF), vm((3, ch, 3 * cl), F32), vm((3, cl, 3 * cg), F32)],
         flops=18 * pix * (ch * cl + cl * cg), bytes_=7 << 20,
     )
-    got, early = tied(got, early)
-    got, total, d_above, d_below = tied(got, core_sum(early), d_above, d_below)
+    got, early, d_above, d_below = tied(got, early, d_above, d_below)
+    got, total = tied(got, core_sum(early))
     early = core_exchange(total, count)
     sent, grad_freq = call(
-        functools.partial(frequency_back_kernel, norm_h, tile),
+        functools.partial(frequency_back_kernel, norm_h, sizes),
         "frequency_back",
         (1,),
         [
@@ -565,8 +564,8 @@
             (weight, None, None), (sign, None, None), (stacked, None, None),
         ],
         [((n, 384), BF, None, None), ((384, 384), BF, None, None)],
-        [vm((n, 384), BF), vm((256, 384), F32), vm((256, 384), F32)],
-        flops=8 * n * n * 384, bytes_=8 << 20,
+        [vm((3, n, 128), F32), vm(spectral, F32), vm((256, 384), F32), vm((256, 384), F32)],
+        flops=3 << 30, bytes_=8 << 20,
     )
     sent, early = tied(sent, early)
     got = swap(sent, count)
@@ -584,16 +583,16 @@
     early = core_exchange(jnp.tile(early, (count // 2, 1)), count).reshape(-1, 384)
     late_rows = -(-(3 * 384 + 3 * cs) // (16 * count)) * 16 * count
     d_unit, late = call(
-        functools.partial(tail_kernel, norm_w, cl),
+        functools.partial(tail_kernel, norm_w, sizes, cl),
         "tail",
         (rows,),
         [
-            (got, None, None), (tct, back_table, at_y), (tst, back_table, at_y), (masked, one_row(ch), at_y),
+            (got, None, None), (tct, None, None), (tst, None, None), (masked, one_row(ch), at_y),
             (d_joined, one_row(256), at_y), (w_in_d, None, None), (grad_freq, None, None),
         ],
         [((rows, width, 256), BF, one_row(256), at_y), ((late_rows, 128), BF, None, None)],
-        [vm((n, 256), BF), vm((256, cg), F32)],
-        flops=4 * n * pix * 256, bytes_=16 << 20,
+        [vm((used, 384), BF), vm((used, 256), BF), vm((3, n, 128), F32), vm((256, cg), F32)],
+        flops=1 << 30, bytes_=5 << 20,
     )
     late, early = tied(late, early)
     pairs = lax.axis_size("row")

time: 279 us -> 265 us (0.950)
  Pallas kernels: 99.5 us -> 83.7 us
  waiting for transfers between devices: 61.5 us -> 66.2 us
    pallas_call x10, Pallas kernels: 99.5 us -> 83.7 us  [call(): pl.pallas_call(body, grid=grid, in_specs=[spec(a.shape, block, index) for...]
    all_to_all x2, waiting for transfers between devices: 12.2 us -> 17.2 us  [core_exchange(): return lax.all_to_all(x, AXES, 0, 0, axis_index_groups=groups, tiled=True)]
    all_to_all x4, waiting for transfers between devices: 14.5 us -> 10.2 us  [swap(): lax.all_to_all(x.reshape(count, -1, x.shape[-1]), AXES, 0, 0, tiled=True)]
    ppermute x3, waiting for transfers between devices: 4.87 us -> 8.99 us  [turn(): lax.ppermute(part, 'col', [(i, (i + k) % cols) for i in range(cols)])]
    ppermute x1, waiting for transfers between devices: 0.01 us -> 2.96 us  [core_sum(): other = lax.ppermute(other, 'row', [(i, i ^ 1) for i in range(pairs)])]
    unnamed x63 -> x55, local copies, waits for them, and re-layouts: 9.61 us -> 8.1 us
  transfers between devices with their start and end apart: 18 -> 18, of which waited for: 12 -> 10; matrix products, arithmetic and copies ran while one was open for 9% -> 8% of each run, Pallas kernels for 27% -> 25%
where the time goes in v4:
time: 265 us; the launch traced here: 263 us
  Pallas kernels  83.7 us (32%)
  starting transfers between devices  75 us (28%)
  waiting for transfers between devices  66.2 us (25%)
  local copies, waits for them, and re-layouts  26.6 us (10%)
  other arithmetic  10.5 us (4%)
    pallas_call x10, Pallas kernels, call(): pl.pallas_call(body, grid=grid, in_specs=[spec(a.shape, block, index) for...  83.7 us
    all_to_all x4, starting transfers between devices, swap(): lax.all_to_all(x.reshape(count, -1, x.shape[-1]), AXES, 0, 0, tiled=True)  30.2 us
    all_to_all x2, waiting for transfers between devices, core_exchange(): return lax.all_to_all(x, AXES, 0, 0, axis_index_groups=groups, tiled=True)  17.2 us
    all_to_all x2, starting transfers between devices, core_exchange(): return lax.all_to_all(x, AXES, 0, 0, axis_index_groups=groups, tiled=True)  11.4 us
    all_to_all x4, waiting for transfers between devices, swap(): lax.all_to_all(x.reshape(count, -1, x.shape[-1]), AXES, 0, 0, tiled=True)  10.2 us
    ppermute x3, waiting for transfers between devices, turn(): lax.ppermute(part, 'col', [(i, (i + k) % cols) for i in range(cols)])  8.99 us
    unnamed x55, local copies, waits for them, and re-layouts  8.1 us
    all_to_all x1, waiting for transfers between devices, gather(): lax.all_to_all(jnp.broadcast_to(x[None], (count,) + x.shape), AXES, 0, 0,...  7.68 us
  transfers between devices with their start and end apart: 18, of which 10 were waited for; matrix products, arithmetic and copies ran while one was open for 8% of the time, Pallas kernels for 25%

profile of v4, /device:TPU:1, one launch (start us, length us, event | category | flops | bytes accessed | tf_op | source)
XLA Modules:
  0.0 263.0 jit_solution(13690290180542241844)
XLA Ops:
  4.3 5.0 %all-to-all-start = ((bf16[4,5,80,512]{3,2,1,0:T(8,128)(2,1)}), bf16[4,5,80,512]{3,2,1,0:T(8,128)(2,1)S(1)}, u32[]{:S(2)}, u32[]{:S(2)}) async-start(bf16[4,5,80,512]{3,2,1,0:T(8,128)(2,1)} %broadcast_select_fusion), calls=%async_computation | async-start | bytes 3276800 | tf_op jit(solution)/shard_map/all_to_all | solution.py:388
  22.9 6.9 %all-to-all-done.marked = bf16[4,5,80,512]{3,2,1,0:T(8,128)(2,1)S(1)} async-done(((bf16[4,5,80,512]{3,2,1,0:T(8,128)(2,1)}), bf16[4,5,80,512]{3,2,1,0:T(8,128)(2,1)S(1)}, u32[]{:S(2)}, u32[]{:S(2)}) %all-to-all-start) | async-done | bytes 1638432 | tf_op jit(solution)/shard_map/all_to_all | solution.py:388
  30.9 7.6 %head.1 = (bf16[5,320,512]{2,1,0:T(8,128)(2,1)}, bf16[5,320,256]{2,1,0:T(8,128)(2,1)}, bf16[1024,384]{1,0:T(8,128)(2,1)}) custom-call(bf16[4,5,80,512]{3,2,1,0:T(8,128)(2,1)} %copy-done, bf16[384,256]{1,0:T(8,128)(2,1)} %pad_maximum_fusion.1.w_in, bf16[192,320]{1,0:T(8,128)(2,1)} %constant.100.clone.tc, bf16[192,320]{1,0:T(8,128)(2,1)} %constant.101.clone.ts), custom_call_target="tpu_custom_call" | custom-call | flops 1073741824 | bytes 6291456 | tf_op jit(solution)/shard_map/head/pallas_call | solution.py:81
  38.6 9.5 %all-to-all-start.1 = ((bf16[64,16,384]{2,1,0:T(8,128)(2,1)}), bf16[64,16,384]{2,1,0:T(8,128)(2,1)S(1)}, u32[]{:S(2)}, u32[]{:S(2)}) async-start(bf16[64,16,384]{2,1,0:T(8,128)(2,1)} %bitcast.68), calls=%async_computation.1 | async-start | bytes 1572864 | tf_op jit(solution)/shard_map/all_to_all | solution.py:383
  62.2 5.2 %collective-permute-done.above = bf16[1,320,512]{2,1,0:T(8,128)(2,1)} collective-permute-done((bf16[1,320,512]{2,1,0:T(8,128)(2,1)}, bf16[1,320,512]{2,1,0:T(8,128)(2,1)}, u32[]{:S(2)}, u32[]{:S(2)}) %collective-permute-start) | collective-permute-done | bytes 327712 | tf_op jit(solution)/shard_map/ppermute | solution.py:420
  68.4 7.3 %frequency.1 = (bf16[3,320,384]{2,1,0:T(8,128)(2,1)}, bf16[1024,384]{1,0:T(8,128)(2,1)}) custom-call(bf16[1024,384]{1,0:T(8,128)(2,1)} %bitcast.67, bf16[320,320]{1,0:T(8,128)(2,1)} %constant.102.clone.hc, bf16[320,320]{1,0:T(8,128)(2,1)} %constant.103.clone.hs, bf16[384,384]{1,0:T(8,128)(2,1)} %copy.46.w_freq, f32[1,3]{1,0:T(1,128)} %or_select_fusion.weight, ...), custom_call_target="tpu_custom_call" | custom-call | flops 3221225472 | bytes 7340032 | tf_op jit(solution)/shard_map/frequency/pallas_call | solution.py:81
  75.7 9.0 %collective-permute-done.3.refs_2_ = bf16[5,80,512]{2,1,0:T(8,128)(2,1)} collective-permute-done((bf16[5,80,512]{2,1,0:T(8,128)(2,1)S(1)}, bf16[5,80,512]{2,1,0:T(8,128)(2,1)}, u32[]{:S(2)}, u32[]{:S(2)}) %collective-permute-start.3) | collective-permute-done | bytes 409632 | tf_op jit(solution)/shard_map/ppermute | solution.py:398
  84.7 9.5 %all-to-all-start.2 = ((bf16[64,16,384]{2,1,0:T(8,128)(2,1)}), bf16[64,16,384]{2,1,0:T(8,128)(2,1)S(1)}, u32[]{:S(2)}, u32[]{:S(2)}) async-start(bf16[64,16,384]{2,1,0:T(8,128)(2,1)} %bitcast.72), calls=%async_computation.2 | async-start | bytes 1572864 | tf_op jit(solution)/shard_map/all_to_all | solution.py:383
  95.6 8.7 %conv.1.pre = f32[5,320,512]{2,1,0:T(8,128)} custom-call(bf16[1,320,512]{2,1,0:T(8,128)(2,1)} %collective-permute-done.above, bf16[5,320,512]{2,1,0:T(8,128)(2,1)} %get-tuple-element.63.masked, bf16[1,320,512]{2,1,0:T(8,128)(2,1)} %collective-permute-done.1.below, bf16[3,512,384]{2,1,0:T(8,128)(2,1)} %copy.47.w_local, bf16[384,1152]{1,0:T(8,128)(2,1)} %bitcast.66), custom_call_target="tpu_custom_call" | custom-call | flops 3303014400 | bytes 9437184 | tf_op jit(solution)/shard_map/conv/pallas_call | solution.py:81
  104.3 5.3 %all-to-all-done.2 = bf16[64,16,384]{2,1,0:T(8,128)(2,1)S(1)} async-done(((bf16[64,16,384]{2,1,0:T(8,128)(2,1)}), bf16[64,16,384]{2,1,0:T(8,128)(2,1)S(1)}, u32[]{:S(2)}, u32[]{:S(2)}) %all-to-all-start.2) | async-done | bytes 786464 | tf_op jit(solution)/shard_map/all_to_all | solution.py:383
  110.5 11.5 %middle.1 = (bf16[5,320,512]{2,1,0:T(8,128)(2,1)}, bf16[5,320,512]{2,1,0:T(8,128)(2,1)}, bf16[5,320,256]{2,1,0:T(8,128)(2,1)}, bf16[1024,384]{1,0:T(8,128)(2,1)}, bf16[192,384]{1,0:T(8,128)(2,1)}) custom-call(bf16[1024,384]{1,0:T(8,128)(2,1)} %bitcast.71, bf16[320,192]{1,0:T(8,128)(2,1)} %constant.98.clone.tct, bf16[320,192]{1,0:T(8,128)(2,1)} %constant.99.clone.tst, ...), custom_call_target="tpu_custom_call" | custom-call | flops 3221225472 | bytes 12582912 | tf_op jit(solution)/shard_map/middle/pallas_call | solution.py:81
  135.3 11.1 %conv_grad.1 = bf16[2,1536,384]{2,1,0:T(8,128)(2,1)} custom-call(bf16[1,320,512]{2,1,0:T(8,128)(2,1)} %collective-permute-done.above, bf16[5,320,512]{2,1,0:T(8,128)(2,1)} %get-tuple-element.63.masked, bf16[1,320,512]{2,1,0:T(8,128)(2,1)} %collective-permute-done.1.below, bf16[5,320,512]{2,1,0:T(8,128)(2,1)} %get-tuple-element.81.d_out, ...), custom_call_target="tpu_custom_call" | custom-call | flops 3303014400 | bytes 7340032 | tf_op jit(solution)/shard_map/conv_grad/pallas_call | solution.py:81
  154.4 7.5 %all-to-all-start.4 = ((bf16[32,48,384]{2,1,0:T(8,128)(2,1)}), bf16[32,48,384]{2,1,0:T(8,128)(2,1)S(1)}, u32[]{:S(2)}, u32[]{:S(2)}) async-start(bf16[32,48,384]{2,1,0:T(8,128)(2,1)} %bitcast.27), calls=%async_computation.4 | async-start | bytes 2359296 | tf_op jit(solution)/shard_map/all_to_all | solution.py:416
  161.9 9.5 %frequency_back.1 = (bf16[1024,384]{1,0:T(8,128)(2,1)}, bf16[384,384]{1,0:T(8,128)(2,1)}) custom-call(bf16[1024,384]{1,0:T(8,128)(2,1)} %bitcast.69, bf16[320,320]{1,0:T(8,128)(2,1)} %constant.102.clone.hc, bf16[320,320]{1,0:T(8,128)(2,1)} %constant.103.clone.hs, bf16[384,384]{1,0:T(8,128)(2,1)} %copy.46.w_freq, bf16[384,384]{1,0:T(8,128)(2,1)} %bitcast.63, ...), custom_call_target="tpu_custom_call" | custom-call | flops 3221225472 | bytes 8388608 | tf_op jit(solution)/shard_map/frequency_back/pallas_call | solution.py:81
  171.4 7.6 %all-to-all-done.4 = bf16[32,48,384]{2,1,0:T(8,128)(2,1)S(1)} async-done(((bf16[32,48,384]{2,1,0:T(8,128)(2,1)}), bf16[32,48,384]{2,1,0:T(8,128)(2,1)S(1)}, u32[]{:S(2)}, u32[]{:S(2)}) %all-to-all-start.4) | async-done | bytes 1179680 | tf_op jit(solution)/shard_map/all_to_all | solution.py:416
  179.0 6.5 %all-to-all-start.5 = ((bf16[64,16,384]{2,1,0:T(8,128)(2,1)}), bf16[64,16,384]{2,1,0:T(8,128)(2,1)S(1)}, u32[]{:S(2)}, u32[]{:S(2)}) async-start(bf16[64,16,384]{2,1,0:T(8,128)(2,1)} %bitcast.73), calls=%async_computation.5 | async-start | bytes 1572864 | tf_op jit(solution)/shard_map/all_to_all | solution.py:383
  185.5 10.5 %conv_back.1.d_conv = f32[5,320,512]{2,1,0:T(8,128)} custom-call(bf16[1,320,512]{2,1,0:T(8,128)(2,1)} %collective-permute-done.5.above, bf16[5,320,512]{2,1,0:T(8,128)(2,1)} %get-tuple-element.81.d_out, bf16[1,320,512]{2,1,0:T(8,128)(2,1)} %collective-permute-done.6.below, bf16[3,384,512]{2,1,0:T(8,128)(2,1)} %bitcast.64, bf16[3,1152,128]{2,1,0:T(8,128)(2,1)} %bitcast.65), custom_call_target="tpu_custom_call" | custom-call | flops 3303014400 | bytes 9437184 | tf_op jit(solution)/shard_map/conv_back/pallas_call | solution.py:81
  196.0 4.9 %all-to-all-done.5 = bf16[64,16,384]{2,1,0:T(8,128)(2,1)S(1)} async-done(((bf16[64,16,384]{2,1,0:T(8,128)(2,1)}), bf16[64,16,384]{2,1,0:T(8,128)(2,1)S(1)}, u32[]{:S(2)}, u32[]{:S(2)}) %all-to-all-start.5) | async-done | bytes 786464 | tf_op jit(solution)/shard_map/all_to_all | solution.py:383
  206.1 8.0 %tail.1 = (bf16[5,320,256]{2,1,0:T(8,128)(2,1)}, bf16[2048,128]{1,0:T(8,128)(2,1)}) custom-call(bf16[1024,384]{1,0:T(8,128)(2,1)} %bitcast.57, bf16[320,192]{1,0:T(8,128)(2,1)} %constant.98.clone.tct, bf16[320,192]{1,0:T(8,128)(2,1)} %constant.99.clone.tst, bf16[5,320,512]{2,1,0:T(8,128)(2,1)} %get-tuple-element.63.masked, ...), custom_call_target="tpu_custom_call" | custom-call | flops 1073741824 | bytes 5242880 | tf_op jit(solution)/shard_map/tail/pallas_call | solution.py:81
  214.1 9.5 %all-to-all-done.6 = bf16[32,48,384]{2,1,0:T(8,128)(2,1)S(1)} async-done(((bf16[32,48,384]{2,1,0:T(8,128)(2,1)}), bf16[32,48,384]{2,1,0:T(8,128)(2,1)S(1)}, u32[]{:S(2)}, u32[]{:S(2)}) %all-to-all-start.6) | async-done | bytes 1179680 | tf_op jit(solution)/shard_map/all_to_all | solution.py:416
  225.3 5.0 %all-to-all-start.7 = ((bf16[64,32,128]{2,1,0:T(8,128)(2,1)}), bf16[64,32,128]{2,1,0:T(8,128)(2,1)S(1)}, u32[]{:S(2)}, u32[]{:S(2)}) async-start(bf16[64,32,128]{2,1,0:T(8,128)(2,1)} %bitcast.75), calls=%async_computation.7 | async-start | bytes 1048576 | tf_op jit(solution)/shard_map/all_to_all | solution.py:426
  230.4 5.5 %finish.1 = bf16[5,320,512]{2,1,0:T(8,128)(2,1)} custom-call(bf16[4,5,80,512]{3,2,1,0:T(8,128)(2,1)} %copy-done, bf16[5,320,256]{2,1,0:T(8,128)(2,1)} %get-tuple-element.102.d_unit, f32[5,320,512]{2,1,0:T(8,128)} %conv_back.1.d_conv, bf16[256,384]{1,0:T(8,128)(2,1)} %pad.7.w_in_t), custom_call_target="tpu_custom_call" | custom-call | flops 314572800 | bytes 7340032 | tf_op jit(solution)/shard_map/finish/pallas_call | solution.py:81
  235.9 7.1 %all-to-all-done.7 = bf16[64,32,128]{2,1,0:T(8,128)(2,1)S(1)} async-done(((bf16[64,32,128]{2,1,0:T(8,128)(2,1)}), bf16[64,32,128]{2,1,0:T(8,128)(2,1)S(1)}, u32[]{:S(2)}, u32[]{:S(2)}) %all-to-all-start.7) | async-done | bytes 524320 | tf_op jit(solution)/shard_map/all_to_all | solution.py:426
  253.7 7.7 %all-to-all-done.8 = bf16[64,32,128]{2,1,0:T(8,128)(2,1)S(1)} async-done(((bf16[64,32,128]{2,1,0:T(8,128)(2,1)}), bf16[64,32,128]{2,1,0:T(8,128)(2,1)S(1)}, u32[]{:S(2)}, u32[]{:S(2)}) %all-to-all-start.8) | async-done | bytes 524320 | tf_op jit(solution)/shard_map/all_to_all | solution.py:431
  (116 shorter events, 76.1 us)
Async XLA Ops:
  4.3 25.5 %all-to-all-start = ((bf16[4,5,80,512]{3,2,1,0:T(8,128)(2,1)}), bf16[4,5,80,512]{3,2,1,0:T(8,128)(2,1)S(1)}, u32[]{:S(2)}, u32[]{:S(2)}) async-start(bf16[4,5,80,512]{3,2,1,0:T(8,128)(2,1)} %broadcast_select_fusion), calls=%async_computation | async-start | bytes 3276800 | tf_op jit(solution)/shard_map/all_to_all | solution.py:388
  16.8 6.0 %copy-start.14 = (bf16[64,384]{0,1:T(8,128)(2,1)S(1)}, bf16[64,384]{0,1:T(8,128)(2,1)}, u32[]{:S(2)}) copy-start(bf16[64,384]{0,1:T(8,128)(2,1)} %copy-done.13) | copy-start | bytes 147460
  22.9 38.5 %copy-start.12 = (bf16[384,384]{0,1:T(8,128)(2,1)}, bf16[384,384]{0,1:T(8,128)(2,1)S(1)}, u32[]{:S(2)}) copy-start(bf16[384,384]{0,1:T(8,128)(2,1)S(1)} %fusion.11) | copy-start | bytes 884740
  38.5 18.3 %copy-start.6 = (bf16[1,20,80,512]{3,2,1,0:T(8,128)(2,1)S(1)}, bf16[1,20,80,512]{3,2,1,0:T(8,128)(2,1)}, u32[]{:S(2)}) copy-start(bf16[1,20,80,512]{3,2,1,0:T(8,128)(2,1)} %param.17) | copy-start | bytes 4915204
  38.6 28.9 %all-to-all-start.1 = ((bf16[64,16,384]{2,1,0:T(8,128)(2,1)}), bf16[64,16,384]{2,1,0:T(8,128)(2,1)S(1)}, u32[]{:S(2)}, u32[]{:S(2)}) async-start(bf16[64,16,384]{2,1,0:T(8,128)(2,1)} %bitcast.68), calls=%async_computation.1 | async-start | bytes 1572864 | tf_op jit(solution)/shard_map/all_to_all | solution.py:383
  50.0 17.4 %collective-permute-start = (bf16[1,320,512]{2,1,0:T(8,128)(2,1)}, bf16[1,320,512]{2,1,0:T(8,128)(2,1)}, u32[]{:S(2)}, u32[]{:S(2)}) collective-permute-start(bf16[1,320,512]{2,1,0:T(8,128)(2,1)} %get-tuple-element.122), channel_id=1, source_target_pairs={{0,1},{1,2},{2,3},{3,4},{4,5},{5,6},{6,7},{7,8},{8,9},{9,10},{10,1... | collective-permute-start | bytes 983048 | tf_op jit(solution)/shard_map/ppermute | solution.py:420
  53.3 14.2 %collective-permute-start.1 = (bf16[1,320,512]{2,1,0:T(8,128)(2,1)}, bf16[1,320,512]{2,1,0:T(8,128)(2,1)}, u32[]{:S(2)}, u32[]{:S(2)}) collective-permute-start(bf16[1,320,512]{2,1,0:T(8,128)(2,1)} %get-tuple-element.121), channel_id=1, source_target_pairs={{1,0},{2,1},{3,2},{4,3},{5,4},{6,5},{7,6},{8,7},{9,8},{10,9},{11,1... | collective-permute-start | bytes 983048 | tf_op jit(solution)/shard_map/ppermute | solution.py:421
  57.9 17.8 %collective-permute-start.2 = (bf16[5,80,512]{2,1,0:T(8,128)(2,1)}, bf16[5,80,512]{2,1,0:T(8,128)(2,1)S(1)}, u32[]{:S(2)}, u32[]{:S(2)}) collective-permute-start(bf16[5,80,512]{2,1,0:T(8,128)(2,1)} %get-tuple-element.119), channel_id=1, source_target_pairs={{0,1},{1,2},{2,3},{3,0},{4,5},{5,6},{6,7},{7,4},{8,9},{9,10},{10,1... | collective-permute-start | bytes 1228808 | tf_op jit(solution)/shard_map/ppermute | solution.py:398
  57.9 26.8 %collective-permute-start.3 = (bf16[5,80,512]{2,1,0:T(8,128)(2,1)S(1)}, bf16[5,80,512]{2,1,0:T(8,128)(2,1)}, u32[]{:S(2)}, u32[]{:S(2)}) collective-permute-start(bf16[5,80,512]{2,1,0:T(8,128)(2,1)S(1)} %get-tuple-element.118), channel_id=1, source_target_pairs={{0,2},{1,3},{2,0},{3,1},{4,6},{5,7},{6,4},{7,5},{8,10},{9,11},{10,... | collective-permute-start | bytes 1228808 | tf_op jit(solution)/shard_map/ppermute | solution.py:398
  60.2 24.5 %collective-permute-start.4 = (bf16[5,80,512]{2,1,0:T(8,128)(2,1)S(1)}, bf16[5,80,512]{2,1,0:T(8,128)(2,1)}, u32[]{:S(2)}, u32[]{:S(2)}) collective-permute-start(bf16[5,80,512]{2,1,0:T(8,128)(2,1)S(1)} %get-tuple-element.117), channel_id=1, source_target_pairs={{0,3},{1,0},{2,1},{3,2},{4,7},{5,4},{6,5},{7,6},{8,11},{9,8},{10,9... | collective-permute-start | bytes 1228808 | tf_op jit(solution)/shard_map/ppermute | solution.py:398
  75.7 18.5 %copy-start.3 = (bf16[3,3,512,128]{2,3,1,0:T(8,128)(2,1)S(1)}, bf16[3,3,512,128]{2,3,1,0:T(8,128)(2,1)}, u32[]{:S(2)}) copy-start(bf16[3,3,512,128]{2,3,1,0:T(8,128)(2,1)} %copy.42) | copy-start | bytes 3538948
  75.7 9.0 %copy-start.23 = (bf16[5,80,512]{2,1,0:T(8,128)(2,1)}, bf16[5,80,512]{2,1,0:T(8,128)(2,1)S(1)}, u32[]{:S(2)}) copy-start(bf16[5,80,512]{2,1,0:T(8,128)(2,1)S(1)} %collective-permute-done.2.refs_1_) | copy-start | bytes 1228804
  84.7 24.9 %all-to-all-start.2 = ((bf16[64,16,384]{2,1,0:T(8,128)(2,1)}), bf16[64,16,384]{2,1,0:T(8,128)(2,1)S(1)}, u32[]{:S(2)}, u32[]{:S(2)}) async-start(bf16[64,16,384]{2,1,0:T(8,128)(2,1)} %bitcast.72), calls=%async_computation.2 | async-start | bytes 1572864 | tf_op jit(solution)/shard_map/all_to_all | solution.py:383
  122.0 24.4 %all-to-all-start.3 = ((bf16[64,16,384]{2,1,0:T(8,128)(2,1)}), bf16[64,16,384]{2,1,0:T(8,128)(2,1)S(1)}, u32[]{:S(2)}, u32[]{:S(2)}) async-start(bf16[64,16,384]{2,1,0:T(8,128)(2,1)} %bitcast.70), calls=%async_computation.3 | async-start | bytes 1572864 | tf_op jit(solution)/shard_map/all_to_all | solution.py:383
  128.5 17.9 %collective-permute-start.5 = (bf16[1,320,512]{2,1,0:T(8,128)(2,1)}, bf16[1,320,512]{2,1,0:T(8,128)(2,1)}, u32[]{:S(2)}, u32[]{:S(2)}) collective-permute-start(bf16[1,320,512]{2,1,0:T(8,128)(2,1)} %get-tuple-element.116), channel_id=1, source_target_pairs={{0,1},{1,2},{2,3},{3,4},{4,5},{5,6},{6,7},{7,8},{8,9},{9,10},{10,1... | collective-permute-start | bytes 983048 | tf_op jit(solution)/shard_map/ppermute | solution.py:420
  131.8 14.6 %collective-permute-start.6 = (bf16[1,320,512]{2,1,0:T(8,128)(2,1)S(1)}, bf16[1,320,512]{2,1,0:T(8,128)(2,1)}, u32[]{:S(2)}, u32[]{:S(2)}) collective-permute-start(bf16[1,320,512]{2,1,0:T(8,128)(2,1)S(1)} %get-tuple-element.115), channel_id=1, source_target_pairs={{1,0},{2,1},{3,2},{4,3},{5,4},{6,5},{7,6},{8,7},{9,8},{10,9},{11,1... | collective-permute-start | bytes 983048 | tf_op jit(solution)/shard_map/ppermute | solution.py:421
  148.7 3.1 %collective-permute-start.7 = (bf16[1536,384]{1,0:T(8,128)(2,1)S(1)}, bf16[1536,384]{1,0:T(8,128)(2,1)}, u32[]{:S(2)}, u32[]{:S(2)}) collective-permute-start(bf16[1536,384]{1,0:T(8,128)(2,1)S(1)} %dynamic-slice_bitcast_fusion), channel_id=1, source_target_pairs={{0,4},{4,0},{8,12},{12,8},{16,20},{20,16},{24,28},{28,24},{32,36},... | collective-permute-start | bytes 3538952 | tf_op jit(solution)/shard_map/ppermute | solution.py:407
  154.4 24.6 %all-to-all-start.4 = ((bf16[32,48,384]{2,1,0:T(8,128)(2,1)}), bf16[32,48,384]{2,1,0:T(8,128)(2,1)S(1)}, u32[]{:S(2)}, u32[]{:S(2)}) async-start(bf16[32,48,384]{2,1,0:T(8,128)(2,1)} %bitcast.27), calls=%async_computation.4 | async-start | bytes 2359296 | tf_op jit(solution)/shard_map/all_to_all | solution.py:416
  179.0 21.9 %all-to-all-start.5 = ((bf16[64,16,384]{2,1,0:T(8,128)(2,1)}), bf16[64,16,384]{2,1,0:T(8,128)(2,1)S(1)}, u32[]{:S(2)}, u32[]{:S(2)}) async-start(bf16[64,16,384]{2,1,0:T(8,128)(2,1)} %bitcast.73), calls=%async_computation.5 | async-start | bytes 1572864 | tf_op jit(solution)/shard_map/all_to_all | solution.py:383
  202.2 21.4 %all-to-all-start.6 = ((bf16[32,48,384]{2,1,0:T(8,128)(2,1)}), bf16[32,48,384]{2,1,0:T(8,128)(2,1)S(1)}, u32[]{:S(2)}, u32[]{:S(2)}) async-start(bf16[32,48,384]{2,1,0:T(8,128)(2,1)} %reshape_tile.3), calls=%async_computation.6 | async-start | bytes 2359296 | tf_op jit(solution)/shard_map/all_to_all | solution.py:416
  223.6 12.3 %copy-start.1 = (bf16[32,48,384]{2,1,0:T(8,128)(2,1)}, bf16[32,48,384]{2,1,0:T(8,128)(2,1)S(1)}, u32[]{:S(2)}) copy-start(bf16[32,48,384]{2,1,0:T(8,128)(2,1)S(1)} %all-to-all-done.6) | copy-start | bytes 3538948
  223.6 25.0 %collective-permute-start.8 = (bf16[1536,384]{1,0:T(8,128)(2,1)S(1)}, bf16[1536,384]{1,0:T(8,128)(2,1)S(1)}, u32[]{:S(2)}, u32[]{:S(2)}) collective-permute-start(bf16[1536,384]{1,0:T(8,128)(2,1)S(1)} %bitcast.50), channel_id=1, source_target_pairs={{0,4},{4,0},{8,12},{12,8},{16,20},{20,16},{24,28},{28,24},{32,36},... | collective-permute-start | bytes 3538952 | tf_op jit(solution)/shard_map/ppermute | solution.py:599
  225.3 17.7 %all-to-all-start.7 = ((bf16[64,32,128]{2,1,0:T(8,128)(2,1)}), bf16[64,32,128]{2,1,0:T(8,128)(2,1)S(1)}, u32[]{:S(2)}, u32[]{:S(2)}) async-start(bf16[64,32,128]{2,1,0:T(8,128)(2,1)} %bitcast.75), calls=%async_computation.7 | async-start | bytes 1048576 | tf_op jit(solution)/shard_map/all_to_all | solution.py:426
  244.0 17.4 %all-to-all-start.8 = ((bf16[64,32,128]{2,1,0:T(8,128)(2,1)}), bf16[64,32,128]{2,1,0:T(8,128)(2,1)S(1)}, u32[]{:S(2)}, u32[]{:S(2)}) async-start(bf16[64,32,128]{2,1,0:T(8,128)(2,1)} %broadcast_in_dim.44), calls=%async_computation.8 | async-start | bytes 1048576 | tf_op jit(solution)/shard_map/all_to_all | solution.py:431
  (23 other events, 72.2 us)

commit v5 on v4

--- a/solution.py
+++ b/solution.py
@@ -502,8 +502,23 @@
         [vm(lined, F32), vm((3, n, 128), F32)],
         flops=1 << 30, bytes_=6 << 20,
     )
+    near = [k for k in range(cols) if k in (0, 1, cols - 1)]
+    sent, *moved = tied(sent, *[cots[k] for k in near])
+    for k, c in zip(near, moved):
+        cots[k] = c
     above, below = edges(masked, count)
-    got = tie(swap(sent, count), above, below)
+    got = swap(sent, count)
+    stacked, sent = call(
+        functools.partial(frequency_kernel, norm_h, sizes),
+        "frequency",
+        (1,),
+        [(got, None, None), (hc, None, None), (hs, None, None), (w_freq_p, None, None), (weight, None, None), (sign, None, None)],
+        [(spectral, BF, None, None), ((n, 384), BF, None, None)],
+        [vm((3, n, 128), F32), vm(spectral, F32)],
+        flops=3 << 30, bytes_=7 << 20,
+    )
+    sent, above, below, *cots = tied(sent, above, below, *cots)
+    got = swap(sent, count)
     (pre,) = call(
         functools.partial(conv_kernel, cl),
         "conv",
@@ -513,17 +528,6 @@
         [vm((rows + 2, width, ch), BF)],
         flops=18 * pix * (ch * cl + cl * cg), bytes_=9 << 20,
     )
-    stacked, sent = call(
-        functools.partial(frequency_kernel, norm_h, sizes),
-        "frequency",
-        (1,),
-        [(got, None, None), (hc, None, None), (hs, None, None), (w_freq_p, None, None), (weight, None, None), (sign, None, None)],
-        [(spectral, BF, None, None), ((n, 384), BF, None, None)],
-        [vm((3, n, 128), F32), vm(spectral, F32)],
-        flops=3 << 30, bytes_=7 << 20,
-    )
-    sent, *cots = tied(sent, *cots)
-    got = swap(sent, count)
     output, d_out, d_joined, sent, grad_out = call(
         functools.partial(middle_kernel, norm_w, sizes, cl, cols),
         "middle",
@@ -552,7 +556,7 @@
         [vm((rows + 2, width, ch), BF), vm((3, ch, 3 * cl), F32), vm((3, cl, 3 * cg), F32)],
         flops=18 * pix * (ch * cl + cl * cg), bytes_=7 << 20,
     )
-    got, early, d_above, d_below = tied(got, early, d_above, d_below)
+    got, early = tied(got, early)
     got, total = tied(got, core_sum(early))
     early = core_exchange(total, count)
     sent, grad_freq = call(
@@ -567,7 +571,7 @@
         [vm((3, n, 128), F32), vm(spectral, F32), vm((256, 384), F32), vm((256, 384), F32)],
         flops=3 << 30, bytes_=8 << 20,
     )
-    sent, early = tied(sent, early)
+    sent, early, d_above, d_below = tied(sent, early, d_above, d_below)
     got = swap(sent, count)
     (d_conv,) = call(
         functools.partial(conv_back_kernel, cl),

time: 265 us -> 260 us (0.981)
  waiting for transfers between devices: 66.2 us -> 57.7 us
    ppermute x3, waiting for transfers between devices: 8.99 us -> 0.01 us  [turn(): lax.ppermute(part, 'col', [(i, (i + k) % cols) for i in range(cols)])]
    all_to_all x4, waiting for transfers between devices: 10.2 us -> 18.3 us  [swap(): lax.all_to_all(x.reshape(count, -1, x.shape[-1]), AXES, 0, 0, tiled=True)]
    all_to_all x2, waiting for transfers between devices: 17.2 us -> 9.53 us  [core_exchange(): return lax.all_to_all(x, AXES, 0, 0, axis_index_groups=groups, tiled=True)]
    ppermute x2, waiting for transfers between devices: 5.23 us -> 9.3 us  [edges(): lax.ppermute(field[-1:], AXES, [(i, i + 1) for i in range(count - 1)])]
    all_to_all x1, waiting for transfers between devices: 6.89 us -> 3.15 us  [to_rows(): lax.all_to_all(field.reshape(cols, h // cols, w, c), 'col', 0, 0, tiled=T...]
    all_to_all x2, starting transfers between devices: 11.4 us -> 7.88 us  [core_exchange(): return lax.all_to_all(x, AXES, 0, 0, axis_index_groups=groups, tiled=True)]
    unnamed x55 -> x63, local copies, waits for them, and re-layouts: 8.1 us -> 9.11 us
  transfers between devices with their start and end apart: 18 -> 18, of which waited for: 10 -> 11; matrix products, arithmetic and copies ran while one was open for 8% -> 9% of each run, Pallas kernels for 25% -> 28%
where the time goes in v5:
time: 260 us; the launch traced here: 258 us
  Pallas kernels  83.8 us (32%)
  starting transfers between devices  75.7 us (29%)
  waiting for transfers between devices  57.7 us (22%)
  local copies, waits for them, and re-layouts  28.5 us (11%)
  other arithmetic  11.4 us (4%)
    pallas_call x10, Pallas kernels, call(): pl.pallas_call(body, grid=grid, in_specs=[spec(a.shape, block, index) for...  83.8 us
    all_to_all x4, starting transfers between devices, swap(): lax.all_to_all(x.reshape(count, -1, x.shape[-1]), AXES, 0, 0, tiled=True)  31.3 us
    all_to_all x4, waiting for transfers between devices, swap(): lax.all_to_all(x.reshape(count, -1, x.shape[-1]), AXES, 0, 0, tiled=True)  18.3 us
    all_to_all x2, waiting for transfers between devices, core_exchange(): return lax.all_to_all(x, AXES, 0, 0, axis_index_groups=groups, tiled=True)  9.53 us
    ppermute x2, waiting for transfers between devices, edges(): lax.ppermute(field[-1:], AXES, [(i, i + 1) for i in range(count - 1)])  9.3 us
    unnamed x63, local copies, waits for them, and re-layouts  9.11 us
    ppermute x2, starting transfers between devices, edges(): up = lax.ppermute(field[:1], AXES, [(i + 1, i) for i in range(count - 1)])  8.57 us
    all_to_all x2, starting transfers between devices, core_exchange(): return lax.all_to_all(x, AXES, 0, 0, axis_index_groups=groups, tiled=True)  7.88 us
  transfers between devices with their start and end apart: 18, of which 11 were waited for; matrix products, arithmetic and copies ran while one was open for 9% of the time, Pallas kernels for 28%

profile of v5, /device:TPU:1, one launch (start us, length us, event | category | flops | bytes accessed | tf_op | source)
XLA Modules:
  0.0 258.3 jit_solution(10164391223970224456)
XLA Ops:
  4.3 5.0 %all-to-all-start = ((bf16[4,5,80,512]{3,2,1,0:T(8,128)(2,1)}), bf16[4,5,80,512]{3,2,1,0:T(8,128)(2,1)S(1)}, u32[]{:S(2)}, u32[]{:S(2)}) async-start(bf16[4,5,80,512]{3,2,1,0:T(8,128)(2,1)} %broadcast_select_fusion), calls=%async_computation | async-start | bytes 3276800 | tf_op jit(solution)/shard_map/all_to_all | solution.py:388
  35.4 7.8 %head.1 = (bf16[5,320,512]{2,1,0:T(8,128)(2,1)}, bf16[5,320,256]{2,1,0:T(8,128)(2,1)}, bf16[1024,384]{1,0:T(8,128)(2,1)}) custom-call(bf16[4,5,80,512]{3,2,1,0:T(8,128)(2,1)} %copy-done, bf16[384,256]{1,0:T(8,128)(2,1)} %pad_maximum_fusion.1.w_in, bf16[192,320]{1,0:T(8,128)(2,1)} %constant.100.clone.tc, bf16[192,320]{1,0:T(8,128)(2,1)} %constant.101.clone.ts), custom_call_target="tpu_custom_call" | custom-call | flops 1073741824 | bytes 6291456 | tf_op jit(solution)/shard_map/head/pallas_call | solution.py:81
  43.2 10.3 %all-to-all-start.1 = ((bf16[64,16,384]{2,1,0:T(8,128)(2,1)}), bf16[64,16,384]{2,1,0:T(8,128)(2,1)S(1)}, u32[]{:S(2)}, u32[]{:S(2)}) async-start(bf16[64,16,384]{2,1,0:T(8,128)(2,1)} %bitcast.69), calls=%async_computation.1 | async-start | bytes 1572864 | tf_op jit(solution)/shard_map/all_to_all | solution.py:383
  59.9 4.6 %collective-permute-start.3 = (bf16[1,320,512]{2,1,0:T(8,128)(2,1)S(1)}, bf16[1,320,512]{2,1,0:T(8,128)(2,1)}, u32[]{:S(2)}, u32[]{:S(2)}) collective-permute-start(bf16[1,320,512]{2,1,0:T(8,128)(2,1)S(1)} %get-tuple-element.131), channel_id=1, source_target_pairs={{1,0},{2,1},{3,2},{4,3},{5,4},{6,5},{7,6},{8,7},{9,8},{10,9},{11,1... | collective-permute-start | bytes 983048 | tf_op jit(solution)/shard_map/ppermute | solution.py:421
  70.1 7.3 %frequency.1 = (bf16[3,320,384]{2,1,0:T(8,128)(2,1)}, bf16[1024,384]{1,0:T(8,128)(2,1)}) custom-call(bf16[1024,384]{1,0:T(8,128)(2,1)} %bitcast.72, bf16[320,320]{1,0:T(8,128)(2,1)} %constant.102.clone.hc, bf16[320,320]{1,0:T(8,128)(2,1)} %constant.103.clone.hs, bf16[384,384]{1,0:T(8,128)(2,1)} %copy.46.w_freq, f32[1,3]{1,0:T(1,128)} %or_select_fusion.weight, ...), custom_call_target="tpu_custom_call" | custom-call | flops 3221225472 | bytes 7340032 | tf_op jit(solution)/shard_map/frequency/pallas_call | solution.py:81
  81.3 8.9 %all-to-all-start.2 = ((bf16[64,16,384]{2,1,0:T(8,128)(2,1)}), bf16[64,16,384]{2,1,0:T(8,128)(2,1)S(1)}, u32[]{:S(2)}, u32[]{:S(2)}) async-start(bf16[64,16,384]{2,1,0:T(8,128)(2,1)} %bitcast.73), calls=%async_computation.2 | async-start | bytes 1572864 | tf_op jit(solution)/shard_map/all_to_all | solution.py:383
  91.6 8.7 %conv.1.pre = f32[5,320,512]{2,1,0:T(8,128)} custom-call(bf16[1,320,512]{2,1,0:T(8,128)(2,1)} %collective-permute-done.2.above, bf16[5,320,512]{2,1,0:T(8,128)(2,1)} %get-tuple-element.73.masked, bf16[1,320,512]{2,1,0:T(8,128)(2,1)} %collective-permute-done.3.below, bf16[3,512,384]{2,1,0:T(8,128)(2,1)} %copy.47.w_local, bf16[384,1152]{1,0:T(8,128)(2,1)} %bitcast.66), custom_call_target="tpu_custom_call" | custom-call | flops 3303014400 | bytes 9437184 | tf_op jit(solution)/shard_map/conv/pallas_call | solution.py:81
  100.3 5.3 %all-to-all-done.2 = bf16[64,16,384]{2,1,0:T(8,128)(2,1)S(1)} async-done(((bf16[64,16,384]{2,1,0:T(8,128)(2,1)}), bf16[64,16,384]{2,1,0:T(8,128)(2,1)S(1)}, u32[]{:S(2)}, u32[]{:S(2)}) %all-to-all-start.2) | async-done | bytes 786464 | tf_op jit(solution)/shard_map/all_to_all | solution.py:383
  106.5 11.5 %middle.1 = (bf16[5,320,512]{2,1,0:T(8,128)(2,1)}, bf16[5,320,512]{2,1,0:T(8,128)(2,1)}, bf16[5,320,256]{2,1,0:T(8,128)(2,1)}, bf16[1024,384]{1,0:T(8,128)(2,1)}, bf16[192,384]{1,0:T(8,128)(2,1)}) custom-call(bf16[1024,384]{1,0:T(8,128)(2,1)} %bitcast.71, bf16[320,192]{1,0:T(8,128)(2,1)} %constant.98.clone.tct, bf16[320,192]{1,0:T(8,128)(2,1)} %constant.99.clone.tst, ...), custom_call_target="tpu_custom_call" | custom-call | flops 3221225472 | bytes 12582912 | tf_op jit(solution)/shard_map/middle/pallas_call | solution.py:81
  118.0 4.7 %all-to-all-start.3 = ((bf16[64,16,384]{2,1,0:T(8,128)(2,1)}), bf16[64,16,384]{2,1,0:T(8,128)(2,1)S(1)}, u32[]{:S(2)}, u32[]{:S(2)}) async-start(bf16[64,16,384]{2,1,0:T(8,128)(2,1)} %bitcast.68), calls=%async_computation.3 | async-start | bytes 1572864 | tf_op jit(solution)/shard_map/all_to_all | solution.py:383
  122.7 11.1 %conv_grad.1 = bf16[2,1536,384]{2,1,0:T(8,128)(2,1)} custom-call(bf16[1,320,512]{2,1,0:T(8,128)(2,1)} %collective-permute-done.2.above, bf16[5,320,512]{2,1,0:T(8,128)(2,1)} %get-tuple-element.73.masked, bf16[1,320,512]{2,1,0:T(8,128)(2,1)} %collective-permute-done.3.below, bf16[5,320,512]{2,1,0:T(8,128)(2,1)} %get-tuple-element.91.d_out, ...), custom_call_target="tpu_custom_call" | custom-call | flops 3303014400 | bytes 7340032 | tf_op jit(solution)/shard_map/conv_grad/pallas_call | solution.py:81
  133.7 4.4 %all-to-all-done.3 = bf16[64,16,384]{2,1,0:T(8,128)(2,1)S(1)} async-done(((bf16[64,16,384]{2,1,0:T(8,128)(2,1)}), bf16[64,16,384]{2,1,0:T(8,128)(2,1)S(1)}, u32[]{:S(2)}, u32[]{:S(2)}) %all-to-all-start.3) | async-done | bytes 786464 | tf_op jit(solution)/shard_map/all_to_all | solution.py:383
  158.4 9.5 %frequency_back.1 = (bf16[1024,384]{1,0:T(8,128)(2,1)}, bf16[384,384]{1,0:T(8,128)(2,1)}) custom-call(bf16[1024,384]{1,0:T(8,128)(2,1)} %bitcast.67, bf16[320,320]{1,0:T(8,128)(2,1)} %constant.102.clone.hc, bf16[320,320]{1,0:T(8,128)(2,1)} %constant.103.clone.hs, bf16[384,384]{1,0:T(8,128)(2,1)} %copy.46.w_freq, bf16[384,384]{1,0:T(8,128)(2,1)} %bitcast.63, ...), custom_call_target="tpu_custom_call" | custom-call | flops 3221225472 | bytes 8388608 | tf_op jit(solution)/shard_map/frequency_back/pallas_call | solution.py:81
  167.9 5.4 %collective-permute-done.6.above = bf16[1,320,512]{2,1,0:T(8,128)(2,1)S(1)} collective-permute-done((bf16[1,320,512]{2,1,0:T(8,128)(2,1)S(1)}, bf16[1,320,512]{2,1,0:T(8,128)(2,1)S(1)}, u32[]{:S(2)}, u32[]{:S(2)}) %collective-permute-start.6) | collective-permute-done | bytes 327712 | tf_op jit(solution)/shard_map/ppermute | solution.py:420
  173.3 7.4 %all-to-all-start.5 = ((bf16[64,16,384]{2,1,0:T(8,128)(2,1)}), bf16[64,16,384]{2,1,0:T(8,128)(2,1)S(1)}, u32[]{:S(2)}, u32[]{:S(2)}) async-start(bf16[64,16,384]{2,1,0:T(8,128)(2,1)} %bitcast.70), calls=%async_computation.5 | async-start | bytes 1572864 | tf_op jit(solution)/shard_map/all_to_all | solution.py:383
  180.8 10.5 %conv_back.1.d_conv = f32[5,320,512]{2,1,0:T(8,128)} custom-call(bf16[1,320,512]{2,1,0:T(8,128)(2,1)} %copy-done.26, bf16[5,320,512]{2,1,0:T(8,128)(2,1)} %get-tuple-element.91.d_out, bf16[1,320,512]{2,1,0:T(8,128)(2,1)} %copy-done.27, bf16[3,384,512]{2,1,0:T(8,128)(2,1)} %bitcast.64, bf16[3,1152,128]{2,1,0:T(8,128)(2,1)} %bitcast.65), custom_call_target="tpu_custom_call" | custom-call | flops 3303014400 | bytes 9437184 | tf_op jit(solution)/shard_map/conv_back/pallas_call | solution.py:81
  191.3 4.9 %all-to-all-done.5 = bf16[64,16,384]{2,1,0:T(8,128)(2,1)S(1)} async-done(((bf16[64,16,384]{2,1,0:T(8,128)(2,1)}), bf16[64,16,384]{2,1,0:T(8,128)(2,1)S(1)}, u32[]{:S(2)}, u32[]{:S(2)}) %all-to-all-start.5) | async-done | bytes 786464 | tf_op jit(solution)/shard_map/all_to_all | solution.py:383
  201.4 8.0 %tail.1 = (bf16[5,320,256]{2,1,0:T(8,128)(2,1)}, bf16[2048,128]{1,0:T(8,128)(2,1)}) custom-call(bf16[1024,384]{1,0:T(8,128)(2,1)} %bitcast.57, bf16[320,192]{1,0:T(8,128)(2,1)} %constant.98.clone.tct, bf16[320,192]{1,0:T(8,128)(2,1)} %constant.99.clone.tst, bf16[5,320,512]{2,1,0:T(8,128)(2,1)} %get-tuple-element.73.masked, ...), custom_call_target="tpu_custom_call" | custom-call | flops 1073741824 | bytes 5242880 | tf_op jit(solution)/shard_map/tail/pallas_call | solution.py:81
  209.3 9.5 %all-to-all-done.6 = bf16[32,48,384]{2,1,0:T(8,128)(2,1)S(1)} async-done(((bf16[32,48,384]{2,1,0:T(8,128)(2,1)}), bf16[32,48,384]{2,1,0:T(8,128)(2,1)S(1)}, u32[]{:S(2)}, u32[]{:S(2)}) %all-to-all-start.6) | async-done | bytes 1179680 | tf_op jit(solution)/shard_map/all_to_all | solution.py:416
  220.6 5.0 %all-to-all-start.7 = ((bf16[64,32,128]{2,1,0:T(8,128)(2,1)}), bf16[64,32,128]{2,1,0:T(8,128)(2,1)S(1)}, u32[]{:S(2)}, u32[]{:S(2)}) async-start(bf16[64,32,128]{2,1,0:T(8,128)(2,1)} %bitcast.75), calls=%async_computation.7 | async-start | bytes 1048576 | tf_op jit(solution)/shard_map/all_to_all | solution.py:426
  225.7 5.5 %finish.1 = bf16[5,320,512]{2,1,0:T(8,128)(2,1)} custom-call(bf16[4,5,80,512]{3,2,1,0:T(8,128)(2,1)} %copy-done, bf16[5,320,256]{2,1,0:T(8,128)(2,1)} %get-tuple-element.112.d_unit, f32[5,320,512]{2,1,0:T(8,128)} %conv_back.1.d_conv, bf16[256,384]{1,0:T(8,128)(2,1)} %pad.7.w_in_t), custom_call_target="tpu_custom_call" | custom-call | flops 314572800 | bytes 7340032 | tf_op jit(solution)/shard_map/finish/pallas_call | solution.py:81
  231.2 7.1 %all-to-all-done.7 = bf16[64,32,128]{2,1,0:T(8,128)(2,1)S(1)} async-done(((bf16[64,32,128]{2,1,0:T(8,128)(2,1)}), bf16[64,32,128]{2,1,0:T(8,128)(2,1)S(1)}, u32[]{:S(2)}, u32[]{:S(2)}) %all-to-all-start.7) | async-done | bytes 524320 | tf_op jit(solution)/shard_map/all_to_all | solution.py:426
  239.3 4.6 %all-to-all-start.8 = ((bf16[64,32,128]{2,1,0:T(8,128)(2,1)}), bf16[64,32,128]{2,1,0:T(8,128)(2,1)S(1)}, u32[]{:S(2)}, u32[]{:S(2)}) async-start(bf16[64,32,128]{2,1,0:T(8,128)(2,1)} %broadcast_in_dim.44), calls=%async_computation.8 | async-start | bytes 1048576 | tf_op jit(solution)/shard_map/all_to_all | solution.py:431
  249.0 7.7 %all-to-all-done.8 = bf16[64,32,128]{2,1,0:T(8,128)(2,1)S(1)} async-done(((bf16[64,32,128]{2,1,0:T(8,128)(2,1)}), bf16[64,32,128]{2,1,0:T(8,128)(2,1)S(1)}, u32[]{:S(2)}, u32[]{:S(2)}) %all-to-all-start.8) | async-done | bytes 524320 | tf_op jit(solution)/shard_map/all_to_all | solution.py:431
  (123 shorter events, 82.6 us)
Async XLA Ops:
  4.3 25.5 %all-to-all-start = ((bf16[4,5,80,512]{3,2,1,0:T(8,128)(2,1)}), bf16[4,5,80,512]{3,2,1,0:T(8,128)(2,1)S(1)}, u32[]{:S(2)}, u32[]{:S(2)}) async-start(bf16[4,5,80,512]{3,2,1,0:T(8,128)(2,1)} %broadcast_select_fusion), calls=%async_computation | async-start | bytes 3276800 | tf_op jit(solution)/shard_map/all_to_all | solution.py:388
  31.2 12.0 %collective-permute-start = (bf16[5,80,512]{2,1,0:T(8,128)(2,1)S(1)}, bf16[5,80,512]{2,1,0:T(8,128)(2,1)S(1)}, u32[]{:S(2)}, u32[]{:S(2)}) collective-permute-start(bf16[5,80,512]{2,1,0:T(8,128)(2,1)S(1)} %get-tuple-element.129), channel_id=1, source_target_pairs={{0,1},{1,2},{2,3},{3,0},{4,5},{5,6},{6,7},{7,4},{8,9},{9,10},{10,1... | collective-permute-start | bytes 1228808 | tf_op jit(solution)/shard_map/ppermute | solution.py:398
  31.5 11.7 %collective-permute-start.1 = (bf16[5,80,512]{2,1,0:T(8,128)(2,1)S(1)}, bf16[5,80,512]{2,1,0:T(8,128)(2,1)S(1)}, u32[]{:S(2)}, u32[]{:S(2)}) collective-permute-start(bf16[5,80,512]{2,1,0:T(8,128)(2,1)S(1)} %get-tuple-element.128), channel_id=1, source_target_pairs={{0,3},{1,0},{2,1},{3,2},{4,7},{5,4},{6,5},{7,6},{8,11},{9,8},{10,9... | collective-permute-start | bytes 1228808 | tf_op jit(solution)/shard_map/ppermute | solution.py:398
  35.4 29.1 %copy-start.11 = (bf16[384,384]{0,1:T(8,128)(2,1)}, bf16[384,384]{0,1:T(8,128)(2,1)S(1)}, u32[]{:S(2)}) copy-start(bf16[384,384]{0,1:T(8,128)(2,1)S(1)} %fusion.11) | copy-start | bytes 884740
  35.4 18.2 %copy-start.22 = (bf16[5,80,512]{2,1,0:T(8,128)(2,1)S(1)}, bf16[5,80,512]{2,1,0:T(8,128)(2,1)}, u32[]{:S(2)}) copy-start(bf16[5,80,512]{2,1,0:T(8,128)(2,1)} %get-tuple-element.127) | copy-start | bytes 1228804
  43.2 22.2 %copy-start.23 = (bf16[5,80,512]{2,1,0:T(8,128)(2,1)}, bf16[5,80,512]{2,1,0:T(8,128)(2,1)S(1)}, u32[]{:S(2)}) copy-start(bf16[5,80,512]{2,1,0:T(8,128)(2,1)S(1)} %collective-permute-done.refs_1_) | copy-start | bytes 1228804
  43.2 22.2 %copy-start.24 = (bf16[5,80,512]{2,1,0:T(8,128)(2,1)}, bf16[5,80,512]{2,1,0:T(8,128)(2,1)S(1)}, u32[]{:S(2)}) copy-start(bf16[5,80,512]{2,1,0:T(8,128)(2,1)S(1)} %collective-permute-done.1.refs_3_) | copy-start | bytes 1228804
  43.2 25.9 %all-to-all-start.1 = ((bf16[64,16,384]{2,1,0:T(8,128)(2,1)}), bf16[64,16,384]{2,1,0:T(8,128)(2,1)S(1)}, u32[]{:S(2)}, u32[]{:S(2)}) async-start(bf16[64,16,384]{2,1,0:T(8,128)(2,1)} %bitcast.69), calls=%async_computation.1 | async-start | bytes 1572864 | tf_op jit(solution)/shard_map/all_to_all | solution.py:383
  53.6 27.7 %collective-permute-start.4 = (bf16[5,80,512]{2,1,0:T(8,128)(2,1)S(1)}, bf16[5,80,512]{2,1,0:T(8,128)(2,1)S(1)}, u32[]{:S(2)}, u32[]{:S(2)}) collective-permute-start(bf16[5,80,512]{2,1,0:T(8,128)(2,1)S(1)} %copy-done.22), channel_id=1, source_target_pairs={{0,2},{1,3},{2,0},{3,1},{4,6},{5,7},{6,4},{7,5},{8,10},{9,11},{10,... | collective-permute-start | bytes 1228808 | tf_op jit(solution)/shard_map/ppermute | solution.py:398
  57.7 23.6 %collective-permute-start.2 = (bf16[1,320,512]{2,1,0:T(8,128)(2,1)S(1)}, bf16[1,320,512]{2,1,0:T(8,128)(2,1)}, u32[]{:S(2)}, u32[]{:S(2)}) collective-permute-start(bf16[1,320,512]{2,1,0:T(8,128)(2,1)S(1)} %get-tuple-element.132), channel_id=1, source_target_pairs={{0,1},{1,2},{2,3},{3,4},{4,5},{5,6},{6,7},{7,8},{8,9},{9,10},{10,1... | collective-permute-start | bytes 983048 | tf_op jit(solution)/shard_map/ppermute | solution.py:420
  59.9 21.4 %collective-permute-start.3 = (bf16[1,320,512]{2,1,0:T(8,128)(2,1)S(1)}, bf16[1,320,512]{2,1,0:T(8,128)(2,1)}, u32[]{:S(2)}, u32[]{:S(2)}) collective-permute-start(bf16[1,320,512]{2,1,0:T(8,128)(2,1)S(1)} %get-tuple-element.131), channel_id=1, source_target_pairs={{1,0},{2,1},{3,2},{4,3},{5,4},{6,5},{7,6},{8,7},{9,8},{10,9},{11,1... | collective-permute-start | bytes 983048 | tf_op jit(solution)/shard_map/ppermute | solution.py:421
  77.4 12.8 %copy-start.3 = (bf16[3,3,512,128]{2,3,1,0:T(8,128)(2,1)S(1)}, bf16[3,3,512,128]{2,3,1,0:T(8,128)(2,1)}, u32[]{:S(2)}) copy-start(bf16[3,3,512,128]{2,3,1,0:T(8,128)(2,1)} %copy.42) | copy-start | bytes 3538948
  81.3 24.3 %all-to-all-start.2 = ((bf16[64,16,384]{2,1,0:T(8,128)(2,1)}), bf16[64,16,384]{2,1,0:T(8,128)(2,1)S(1)}, u32[]{:S(2)}, u32[]{:S(2)}) async-start(bf16[64,16,384]{2,1,0:T(8,128)(2,1)} %bitcast.73), calls=%async_computation.2 | async-start | bytes 1572864 | tf_op jit(solution)/shard_map/all_to_all | solution.py:383
  118.0 20.2 %all-to-all-start.3 = ((bf16[64,16,384]{2,1,0:T(8,128)(2,1)}), bf16[64,16,384]{2,1,0:T(8,128)(2,1)S(1)}, u32[]{:S(2)}, u32[]{:S(2)}) async-start(bf16[64,16,384]{2,1,0:T(8,128)(2,1)} %bitcast.68), calls=%async_computation.3 | async-start | bytes 1572864 | tf_op jit(solution)/shard_map/all_to_all | solution.py:383
  140.4 3.3 %collective-permute-start.5 = (bf16[1536,384]{1,0:T(8,128)(2,1)S(1)}, bf16[1536,384]{1,0:T(8,128)(2,1)}, u32[]{:S(2)}, u32[]{:S(2)}) collective-permute-start(bf16[1536,384]{1,0:T(8,128)(2,1)S(1)} %dynamic-slice_bitcast_fusion), channel_id=1, source_target_pairs={{0,4},{4,0},{8,12},{12,8},{16,20},{20,16},{24,28},{28,24},{32,36},... | collective-permute-start | bytes 3538952 | tf_op jit(solution)/shard_map/ppermute | solution.py:407
  146.3 27.0 %all-to-all-start.4 = ((bf16[32,48,384]{2,1,0:T(8,128)(2,1)}), bf16[32,48,384]{2,1,0:T(8,128)(2,1)S(1)}, u32[]{:S(2)}, u32[]{:S(2)}) async-start(bf16[32,48,384]{2,1,0:T(8,128)(2,1)} %bitcast.27), calls=%async_computation.4 | async-start | bytes 2359296 | tf_op jit(solution)/shard_map/all_to_all | solution.py:416
  151.3 21.9 %collective-permute-start.6 = (bf16[1,320,512]{2,1,0:T(8,128)(2,1)S(1)}, bf16[1,320,512]{2,1,0:T(8,128)(2,1)S(1)}, u32[]{:S(2)}, u32[]{:S(2)}) collective-permute-start(bf16[1,320,512]{2,1,0:T(8,128)(2,1)S(1)} %get-tuple-element.126), channel_id=1, source_target_pairs={{0,1},{1,2},{2,3},{3,4},{4,5},{5,6},{6,7},{7,8},{8,9},{9,10},{10,1... | collective-permute-start | bytes 983048 | tf_op jit(solution)/shard_map/ppermute | solution.py:420
  154.4 18.9 %collective-permute-start.7 = (bf16[1,320,512]{2,1,0:T(8,128)(2,1)S(1)}, bf16[1,320,512]{2,1,0:T(8,128)(2,1)S(1)}, u32[]{:S(2)}, u32[]{:S(2)}) collective-permute-start(bf16[1,320,512]{2,1,0:T(8,128)(2,1)S(1)} %get-tuple-element.125), channel_id=1, source_target_pairs={{1,0},{2,1},{3,2},{4,3},{5,4},{6,5},{7,6},{8,7},{9,8},{10,9},{11,1... | collective-permute-start | bytes 983048 | tf_op jit(solution)/shard_map/ppermute | solution.py:421
  173.3 22.9 %all-to-all-start.5 = ((bf16[64,16,384]{2,1,0:T(8,128)(2,1)}), bf16[64,16,384]{2,1,0:T(8,128)(2,1)S(1)}, u32[]{:S(2)}, u32[]{:S(2)}) async-start(bf16[64,16,384]{2,1,0:T(8,128)(2,1)} %bitcast.70), calls=%async_computation.5 | async-start | bytes 1572864 | tf_op jit(solution)/shard_map/all_to_all | solution.py:383
  197.4 21.4 %all-to-all-start.6 = ((bf16[32,48,384]{2,1,0:T(8,128)(2,1)}), bf16[32,48,384]{2,1,0:T(8,128)(2,1)S(1)}, u32[]{:S(2)}, u32[]{:S(2)}) async-start(bf16[32,48,384]{2,1,0:T(8,128)(2,1)} %reshape_tile.3), calls=%async_computation.6 | async-start | bytes 2359296 | tf_op jit(solution)/shard_map/all_to_all | solution.py:416
  218.9 12.3 %copy-start.1 = (bf16[32,48,384]{2,1,0:T(8,128)(2,1)}, bf16[32,48,384]{2,1,0:T(8,128)(2,1)S(1)}, u32[]{:S(2)}) copy-start(bf16[32,48,384]{2,1,0:T(8,128)(2,1)S(1)} %all-to-all-done.6) | copy-start | bytes 3538948
  218.9 25.0 %collective-permute-start.8 = (bf16[1536,384]{1,0:T(8,128)(2,1)S(1)}, bf16[1536,384]{1,0:T(8,128)(2,1)S(1)}, u32[]{:S(2)}, u32[]{:S(2)}) collective-permute-start(bf16[1536,384]{1,0:T(8,128)(2,1)S(1)} %bitcast.50), channel_id=1, source_target_pairs={{0,4},{4,0},{8,12},{12,8},{16,20},{20,16},{24,28},{28,24},{32,36},... | collective-permute-start | bytes 3538952 | tf_op jit(solution)/shard_map/ppermute | solution.py:603
  220.6 17.7 %all-to-all-start.7 = ((bf16[64,32,128]{2,1,0:T(8,128)(2,1)}), bf16[64,32,128]{2,1,0:T(8,128)(2,1)S(1)}, u32[]{:S(2)}, u32[]{:S(2)}) async-start(bf16[64,32,128]{2,1,0:T(8,128)(2,1)} %bitcast.75), calls=%async_computation.7 | async-start | bytes 1048576 | tf_op jit(solution)/shard_map/all_to_all | solution.py:426
  239.3 17.4 %all-to-all-start.8 = ((bf16[64,32,128]{2,1,0:T(8,128)(2,1)}), bf16[64,32,128]{2,1,0:T(8,128)(2,1)S(1)}, u32[]{:S(2)}, u32[]{:S(2)}) async-start(bf16[64,32,128]{2,1,0:T(8,128)(2,1)} %broadcast_in_dim.44), calls=%async_computation.8 | async-start | bytes 1048576 | tf_op jit(solution)/shard_map/all_to_all | solution.py:431
  (26 other events, 104.2 us)

commit v6 on v5

--- a/solution.py
+++ b/solution.py
@@ -309,7 +309,7 @@
     pre[0, :, cl:] = shifted(cross[:, :g], 1) + cross[:, g : 2 * g] + shifted(cross[:, 2 * g :], -1)
 
 
-def conv_grad_kernel(cl, above, masked, below, d_out, g_out, early, pad, acc_l, acc_c):
+def conv_grad_kernel(cl, above, masked, below, d_out, g_out, core, mine, other, pad, acc_l, acc_c):
     y = pl.program_id(0)
     rows = masked.shape[0]
 
@@ -329,17 +329,26 @@
         acc_l[i] += dot(x, d_local, ROWS_OF)
         acc_c[i] += dot(x[:, :cl], d_global, ROWS_OF)
 
-    @pl.when(y == pl.num_programs(0) - 1)
-    def _():
+    def write(local, rest):
         ch = masked.shape[2]
         for i in range(3):
-            early[0, i * ch : (i + 1) * ch, :] = acc_l[i].astype(BF)
+            local[i * ch : (i + 1) * ch, :] = acc_l[i].astype(BF)
             for j in range(3):
                 at = (3 * i + j) * cl
-                early[1, at : at + cl, :] = acc_c[i, :, j * g : (j + 1) * g].astype(BF)
+                rest[at : at + cl, :] = acc_c[i, :, j * g : (j + 1) * g].astype(BF)
         at, size = 9 * cl, g_out.shape[0]
-        early[1, at : at + size, :] = g_out[...]
-        early[1, at + size :, :] = jnp.zeros((early.shape[1] - at - size, g), BF)
+        rest[at : at + size, :] = g_out[...]
+        rest[at + size :, :] = jnp.zeros((rest.shape[0] - at - size, g), BF)
+
+    last = y == pl.num_programs(0) - 1
+
+    @pl.when(last & (core[0, 0] == 0))
+    def _():
+        write(mine, other)
+
+    @pl.when(last & (core[0, 0] == 1))
+    def _():
+        write(other, mine)
 
 
 def unpack_kernel(cl, mine, other, core, g_local, g_cross, g_out):
@@ -388,24 +397,18 @@
     return lax.all_to_all(field.reshape(cols, h // cols, w, c), "col", 0, 0, tiled=True)
 
 
-def turn(field, cols):
+def turn(field, cols, after):
     h, w, c = field.shape
     blocks = field.reshape(cols, h // cols, w, c)
     me = lax.axis_index("col")
-    out = []
-    for k in range(cols):
-        part = lax.dynamic_index_in_dim(blocks, (me + k) % cols, 0, keepdims=False)
-        out.append(lax.ppermute(part, "col", [(i, (i + k) % cols) for i in range(cols)]) if k else part)
-    return out
-
-
-def core_sum(early):
-    pairs = lax.axis_size("row")
-    core = lax.axis_index("row") % 2
-    mine = lax.dynamic_index_in_dim(early, core, 0, keepdims=False)
-    other = lax.dynamic_index_in_dim(early, 1 - core, 0, keepdims=False)
-    other = lax.ppermute(other, "row", [(i, i ^ 1) for i in range(pairs)])
-    return (mine.astype(F32) + other.astype(F32)).astype(BF)
+    parts = [lax.dynamic_index_in_dim(blocks, (me + k) % cols, 0, keepdims=False) for k in range(cols)]
+    parts = tied(*parts, after)[:-1]
+    moves = [[(i, (i + k) % cols) for i in range(cols)] for k in range(cols)]
+    return [lax.ppermute(part, "col", move) if k else part for k, (part, move) in enumerate(zip(parts, moves))]
+
+
+def core_swap(x):
+    return lax.ppermute(x, "row", [(i, i ^ 1) for i in range(lax.axis_size("row"))])
 
 
 def core_exchange(x, count):
@@ -490,7 +493,7 @@
     w_in_d, w_in_t, w_out_z, w_out_t, w_freq_p, w_freq_t, wl, wc, wl_t, wc_t, weight = tied(
         w_in_d, w_in_t, w_out_z, w_out_t, w_freq_p, w_freq_t, wl, wc, wl_t, wc_t, weight
     )
-    cots = turn(tie(cotangent[0], marked), cols)
+    cots = turn(cotangent[0], cols, marked)
     my_col = lax.axis_index("col").astype(jnp.int32).reshape(1, 1)
 
     masked, unit, sent = call(
@@ -547,17 +550,18 @@
     )
     got = swap(sent, count)
     d_above, d_below = edges(d_out, count)
-    (early,) = call(
+    my_core = (lax.axis_index("row") % 2).astype(jnp.int32).reshape(1, 1)
+    mine, other = call(
         functools.partial(conv_grad_kernel, cl),
         "conv_grad",
         (rows,),
-        [(above, None, None), (masked, None, None), (below, None, None), (d_out, one_row(ch), at_y), (grad_out, None, None)],
-        [((2, 3 * ch, 384), BF, None, None)],
+        [(above, None, None), (masked, None, None), (below, None, None), (d_out, one_row(ch), at_y), (grad_out, None, None), (my_core, None, None)],
+        [((3 * ch, 384), BF, None, None), ((3 * ch, 384), BF, None, None)],
         [vm((rows + 2, width, ch), BF), vm((3, ch, 3 * cl), F32), vm((3, cl, 3 * cg), F32)],
         flops=18 * pix * (ch * cl + cl * cg), bytes_=7 << 20,
     )
-    got, early = tied(got, early)
-    got, total = tied(got, core_sum(early))
+    got, other = tied(got, other)
+    got, total = tied(got, (mine.astype(F32) + core_swap(other).astype(F32)).astype(BF))
     early = core_exchange(total, count)
     sent, grad_freq = call(
         functools.partial(frequency_back_kernel, norm_h, sizes),
@@ -599,9 +603,7 @@
         flops=1 << 30, bytes_=5 << 20,
     )
     late, early = tied(late, early)
-    pairs = lax.axis_size("row")
-    other = lax.ppermute(early, "row", [(i, i ^ 1) for i in range(pairs)])
-    my_core = (lax.axis_index("row") % 2).astype(jnp.int32).reshape(1, 1)
+    other = core_swap(early)
     late = scatter_sum(late, count)
     (grad_features,) = call(
         functools.partial(finish_kernel, cl),

time: 260 us -> 257 us (0.988)
  waiting for transfers between devices: 57.7 us -> 61.4 us
  local copies, waits for them, and re-layouts: 28.5 us -> 25.6 us
  starting transfers between devices: 75.7 us -> 72.9 us
    ppermute x2, waiting for transfers between devices: 0.01 us -> 6.04 us  [edges(): up = lax.ppermute(field[:1], AXES, [(i + 1, i) for i in range(count - 1)])]
    ppermute x2, waiting for transfers between devices: 9.3 us -> 3.65 us  [edges(): lax.ppermute(field[-1:], AXES, [(i, i + 1) for i in range(count - 1)])]
    unnamed x63 -> x59, local copies, waits for them, and re-layouts: 9.11 us -> 7.92 us
  transfers between devices with their start and end apart: 18 -> 18, of which waited for: 11 -> 13; matrix products, arithmetic and copies ran while one was open for 9% -> 9% of each run, Pallas kernels for 28% -> 28%
where the time goes in v6:
time: 257 us; the launch traced here: 255 us
  Pallas kernels  83.8 us (33%)
  starting transfers between devices  72.9 us (28%)
  waiting for transfers between devices  61.4 us (24%)
  local copies, waits for them, and re-layouts  25.6 us (10%)
  other arithmetic  10.5 us (4%)
    pallas_call x10, Pallas kernels, call(): pl.pallas_call(body, grid=grid, in_specs=[spec(a.shape, block, index) for...  83.8 us
    all_to_all x4, starting transfers between devices, swap(): lax.all_to_all(x.reshape(count, -1, x.shape[-1]), AXES, 0, 0, tiled=True)  30.1 us
    all_to_all x4, waiting for transfers between devices, swap(): lax.all_to_all(x.reshape(count, -1, x.shape[-1]), AXES, 0, 0, tiled=True)  19.7 us
    all_to_all x2, waiting for transfers between devices, core_exchange(): return lax.all_to_all(x, AXES, 0, 0, axis_index_groups=groups, tiled=True)  9.53 us
    ppermute x2, starting transfers between devices, edges(): up = lax.ppermute(field[:1], AXES, [(i + 1, i) for i in range(count - 1)])  8.22 us
    unnamed x59, local copies, waits for them, and re-layouts  7.92 us
    all_to_all x2, starting transfers between devices, core_exchange(): return lax.all_to_all(x, AXES, 0, 0, axis_index_groups=groups, tiled=True)  7.89 us
    all_to_all x1, waiting for transfers between devices, gather(): lax.all_to_all(jnp.broadcast_to(x[None], (count,) + x.shape), AXES, 0, 0,...  7.7 us
  transfers between devices with their start and end apart: 18, of which 13 were waited for; matrix products, arithmetic and copies ran while one was open for 9% of the time, Pallas kernels for 28%

profile of v6, /device:TPU:1, one launch (start us, length us, event | category | flops | bytes accessed | tf_op | source)
XLA Modules:
  0.0 255.1 jit_solution(9049266321604370070)
XLA Ops:
  4.3 5.0 %all-to-all-start = ((bf16[4,5,80,512]{3,2,1,0:T(8,128)(2,1)}), bf16[4,5,80,512]{3,2,1,0:T(8,128)(2,1)S(1)}, u32[]{:S(2)}, u32[]{:S(2)}) async-start(bf16[4,5,80,512]{3,2,1,0:T(8,128)(2,1)} %broadcast_select_fusion), calls=%async_computation | async-start | bytes 3276800 | tf_op jit(solution)/shard_map/all_to_all | solution.py:397
  24.8 5.0 %all-to-all-done.marked = bf16[4,5,80,512]{3,2,1,0:T(8,128)(2,1)S(1)} async-done(((bf16[4,5,80,512]{3,2,1,0:T(8,128)(2,1)}), bf16[4,5,80,512]{3,2,1,0:T(8,128)(2,1)S(1)}, u32[]{:S(2)}, u32[]{:S(2)}) %all-to-all-start) | async-done | bytes 1638432 | tf_op jit(solution)/shard_map/all_to_all | solution.py:397
  34.0 7.6 %head.1 = (bf16[5,320,512]{2,1,0:T(8,128)(2,1)}, bf16[5,320,256]{2,1,0:T(8,128)(2,1)}, bf16[1024,384]{1,0:T(8,128)(2,1)}) custom-call(bf16[4,5,80,512]{3,2,1,0:T(8,128)(2,1)} %copy-done, bf16[384,256]{1,0:T(8,128)(2,1)} %pad_maximum_fusion.1.w_in, bf16[192,320]{1,0:T(8,128)(2,1)} %constant.91.clone.tc, bf16[192,320]{1,0:T(8,128)(2,1)} %constant.92.clone.ts), custom_call_target="tpu_custom_call" | custom-call | flops 1073741824 | bytes 6291456 | tf_op jit(solution)/shard_map/head/pallas_call | solution.py:81
  43.1 9.8 %all-to-all-start.1 = ((bf16[64,16,384]{2,1,0:T(8,128)(2,1)}), bf16[64,16,384]{2,1,0:T(8,128)(2,1)S(1)}, u32[]{:S(2)}, u32[]{:S(2)}) async-start(bf16[64,16,384]{2,1,0:T(8,128)(2,1)} %bitcast.64), calls=%async_computation.1 | async-start | bytes 1572864 | tf_op jit(solution)/shard_map/all_to_all | solution.py:392
  63.2 5.3 %all-to-all-done.1 = bf16[64,16,384]{2,1,0:T(8,128)(2,1)S(1)} async-done(((bf16[64,16,384]{2,1,0:T(8,128)(2,1)}), bf16[64,16,384]{2,1,0:T(8,128)(2,1)S(1)}, u32[]{:S(2)}, u32[]{:S(2)}) %all-to-all-start.1) | async-done | bytes 786464 | tf_op jit(solution)/shard_map/all_to_all | solution.py:392
  69.4 7.2 %frequency.1 = (bf16[3,320,384]{2,1,0:T(8,128)(2,1)}, bf16[1024,384]{1,0:T(8,128)(2,1)}) custom-call(bf16[1024,384]{1,0:T(8,128)(2,1)} %bitcast.66, bf16[320,320]{1,0:T(8,128)(2,1)} %constant.93.clone.hc, bf16[320,320]{1,0:T(8,128)(2,1)} %constant.94.clone.hs, bf16[384,384]{1,0:T(8,128)(2,1)} %copy.46.w_freq, f32[1,3]{1,0:T(1,128)} %or_select_fusion.weight, ...), custom_call_target="tpu_custom_call" | custom-call | flops 3221225472 | bytes 7340032 | tf_op jit(solution)/shard_map/frequency/pallas_call | solution.py:81
  80.9 8.1 %all-to-all-start.2 = ((bf16[64,16,384]{2,1,0:T(8,128)(2,1)}), bf16[64,16,384]{2,1,0:T(8,128)(2,1)S(1)}, u32[]{:S(2)}, u32[]{:S(2)}) async-start(bf16[64,16,384]{2,1,0:T(8,128)(2,1)} %bitcast.67), calls=%async_computation.2 | async-start | bytes 1572864 | tf_op jit(solution)/shard_map/all_to_all | solution.py:392
  90.5 8.7 %conv.1.pre = f32[5,320,512]{2,1,0:T(8,128)} custom-call(bf16[1,320,512]{2,1,0:T(8,128)(2,1)} %collective-permute-done.2.above, bf16[5,320,512]{2,1,0:T(8,128)(2,1)} %get-tuple-element.80.masked, bf16[1,320,512]{2,1,0:T(8,128)(2,1)} %copy-done.23, bf16[3,512,384]{2,1,0:T(8,128)(2,1)} %copy.47.w_local, bf16[384,1152]{1,0:T(8,128)(2,1)} %bitcast.60), custom_call_target="tpu_custom_call" | custom-call | flops 3303014400 | bytes 9437184 | tf_op jit(solution)/shard_map/conv/pallas_call | solution.py:81
  99.2 5.2 %all-to-all-done.2 = bf16[64,16,384]{2,1,0:T(8,128)(2,1)S(1)} async-done(((bf16[64,16,384]{2,1,0:T(8,128)(2,1)}), bf16[64,16,384]{2,1,0:T(8,128)(2,1)S(1)}, u32[]{:S(2)}, u32[]{:S(2)}) %all-to-all-start.2) | async-done | bytes 786464 | tf_op jit(solution)/shard_map/all_to_all | solution.py:392
  105.4 11.6 %middle.1 = (bf16[5,320,512]{2,1,0:T(8,128)(2,1)}, bf16[5,320,512]{2,1,0:T(8,128)(2,1)}, bf16[5,320,256]{2,1,0:T(8,128)(2,1)}, bf16[1024,384]{1,0:T(8,128)(2,1)}, bf16[192,384]{1,0:T(8,128)(2,1)}) custom-call(bf16[1024,384]{1,0:T(8,128)(2,1)} %bitcast.65, bf16[320,192]{1,0:T(8,128)(2,1)} %constant.89.clone.tct, bf16[320,192]{1,0:T(8,128)(2,1)} %constant.90.clone.tst, ...), custom_call_target="tpu_custom_call" | custom-call | flops 3221225472 | bytes 12582912 | tf_op jit(solution)/shard_map/middle/pallas_call | solution.py:81
  117.0 4.7 %all-to-all-start.3 = ((bf16[64,16,384]{2,1,0:T(8,128)(2,1)}), bf16[64,16,384]{2,1,0:T(8,128)(2,1)S(1)}, u32[]{:S(2)}, u32[]{:S(2)}) async-start(bf16[64,16,384]{2,1,0:T(8,128)(2,1)} %bitcast.62), calls=%async_computation.3 | async-start | bytes 1572864 | tf_op jit(solution)/shard_map/all_to_all | solution.py:392
  121.7 11.1 %conv_grad.1 = (bf16[1536,384]{1,0:T(8,128)(2,1)}, bf16[1536,384]{1,0:T(8,128)(2,1)}) custom-call(bf16[1,320,512]{2,1,0:T(8,128)(2,1)} %collective-permute-done.2.above, bf16[5,320,512]{2,1,0:T(8,128)(2,1)} %get-tuple-element.80.masked, bf16[1,320,512]{2,1,0:T(8,128)(2,1)} %copy-done.23, bf16[5,320,512]{2,1,0:T(8,128)(2,1)} %get-tuple-element.99.d_out, ...), custom_call_target="tpu_custom_call" | custom-call | flops 3303014400 | bytes 7340032 | tf_op jit(solution)/shard_map/conv_grad/pallas_call | solution.py:81
  148.1 4.9 %collective-permute-start.7 = (bf16[1,320,512]{2,1,0:T(8,128)(2,1)S(1)}, bf16[1,320,512]{2,1,0:T(8,128)(2,1)S(1)}, u32[]{:S(2)}, u32[]{:S(2)}) collective-permute-start(bf16[1,320,512]{2,1,0:T(8,128)(2,1)S(1)} %get-tuple-element.135), channel_id=1, source_target_pairs={{1,0},{2,1},{3,2},{4,3},{5,4},{6,5},{7,6},{8,7},{9,8},{10,9},{11,1... | collective-permute-start | bytes 983048 | tf_op jit(solution)/shard_map/ppermute | solution.py:424
  155.2 9.5 %frequency_back.1 = (bf16[1024,384]{1,0:T(8,128)(2,1)}, bf16[384,384]{1,0:T(8,128)(2,1)}) custom-call(bf16[1024,384]{1,0:T(8,128)(2,1)} %bitcast.61, bf16[320,320]{1,0:T(8,128)(2,1)} %constant.93.clone.hc, bf16[320,320]{1,0:T(8,128)(2,1)} %constant.94.clone.hs, bf16[384,384]{1,0:T(8,128)(2,1)} %copy.46.w_freq, bf16[384,384]{1,0:T(8,128)(2,1)} %bitcast.57, ...), custom_call_target="tpu_custom_call" | custom-call | flops 3221225472 | bytes 8388608 | tf_op jit(solution)/shard_map/frequency_back/pallas_call | solution.py:81
  170.1 7.5 %all-to-all-start.5 = ((bf16[64,16,384]{2,1,0:T(8,128)(2,1)}), bf16[64,16,384]{2,1,0:T(8,128)(2,1)S(1)}, u32[]{:S(2)}, u32[]{:S(2)}) async-start(bf16[64,16,384]{2,1,0:T(8,128)(2,1)} %bitcast.63), calls=%async_computation.5 | async-start | bytes 1572864 | tf_op jit(solution)/shard_map/all_to_all | solution.py:392
  177.6 10.5 %conv_back.1.d_conv = f32[5,320,512]{2,1,0:T(8,128)} custom-call(bf16[1,320,512]{2,1,0:T(8,128)(2,1)} %copy-done.25, bf16[5,320,512]{2,1,0:T(8,128)(2,1)} %get-tuple-element.99.d_out, bf16[1,320,512]{2,1,0:T(8,128)(2,1)} %copy-done.24, bf16[3,384,512]{2,1,0:T(8,128)(2,1)} %bitcast.58, bf16[3,1152,128]{2,1,0:T(8,128)(2,1)} %bitcast.59), custom_call_target="tpu_custom_call" | custom-call | flops 3303014400 | bytes 9437184 | tf_op jit(solution)/shard_map/conv_back/pallas_call | solution.py:81
  188.1 4.9 %all-to-all-done.5 = bf16[64,16,384]{2,1,0:T(8,128)(2,1)S(1)} async-done(((bf16[64,16,384]{2,1,0:T(8,128)(2,1)}), bf16[64,16,384]{2,1,0:T(8,128)(2,1)S(1)}, u32[]{:S(2)}, u32[]{:S(2)}) %all-to-all-start.5) | async-done | bytes 786464 | tf_op jit(solution)/shard_map/all_to_all | solution.py:392
  198.2 8.0 %tail.1 = (bf16[5,320,256]{2,1,0:T(8,128)(2,1)}, bf16[2048,128]{1,0:T(8,128)(2,1)}) custom-call(bf16[1024,384]{1,0:T(8,128)(2,1)} %bitcast.51, bf16[320,192]{1,0:T(8,128)(2,1)} %constant.89.clone.tct, bf16[320,192]{1,0:T(8,128)(2,1)} %constant.90.clone.tst, bf16[5,320,512]{2,1,0:T(8,128)(2,1)} %get-tuple-element.80.masked, ...), custom_call_target="tpu_custom_call" | custom-call | flops 1073741824 | bytes 5242880 | tf_op jit(solution)/shard_map/tail/pallas_call | solution.py:81
  206.1 9.5 %all-to-all-done.6 = bf16[32,48,384]{2,1,0:T(8,128)(2,1)S(1)} async-done(((bf16[32,48,384]{2,1,0:T(8,128)(2,1)}), bf16[32,48,384]{2,1,0:T(8,128)(2,1)S(1)}, u32[]{:S(2)}, u32[]{:S(2)}) %all-to-all-start.6) | async-done | bytes 1179680 | tf_op jit(solution)/shard_map/all_to_all | solution.py:419
  217.4 5.0 %all-to-all-start.7 = ((bf16[64,32,128]{2,1,0:T(8,128)(2,1)}), bf16[64,32,128]{2,1,0:T(8,128)(2,1)S(1)}, u32[]{:S(2)}, u32[]{:S(2)}) async-start(bf16[64,32,128]{2,1,0:T(8,128)(2,1)} %bitcast.69), calls=%async_computation.7 | async-start | bytes 1048576 | tf_op jit(solution)/shard_map/all_to_all | solution.py:429
  222.5 5.5 %finish.1 = bf16[5,320,512]{2,1,0:T(8,128)(2,1)} custom-call(bf16[4,5,80,512]{3,2,1,0:T(8,128)(2,1)} %copy-done, bf16[5,320,256]{2,1,0:T(8,128)(2,1)} %get-tuple-element.122.d_unit, f32[5,320,512]{2,1,0:T(8,128)} %conv_back.1.d_conv, bf16[256,384]{1,0:T(8,128)(2,1)} %pad.7.w_in_t), custom_call_target="tpu_custom_call" | custom-call | flops 314572800 | bytes 7340032 | tf_op jit(solution)/shard_map/finish/pallas_call | solution.py:81
  228.0 7.1 %all-to-all-done.7 = bf16[64,32,128]{2,1,0:T(8,128)(2,1)S(1)} async-done(((bf16[64,32,128]{2,1,0:T(8,128)(2,1)}), bf16[64,32,128]{2,1,0:T(8,128)(2,1)S(1)}, u32[]{:S(2)}, u32[]{:S(2)}) %all-to-all-start.7) | async-done | bytes 524320 | tf_op jit(solution)/shard_map/all_to_all | solution.py:429
  236.1 4.6 %all-to-all-start.8 = ((bf16[64,32,128]{2,1,0:T(8,128)(2,1)}), bf16[64,32,128]{2,1,0:T(8,128)(2,1)S(1)}, u32[]{:S(2)}, u32[]{:S(2)}) async-start(bf16[64,32,128]{2,1,0:T(8,128)(2,1)} %broadcast_in_dim.44), calls=%async_computation.8 | async-start | bytes 1048576 | tf_op jit(solution)/shard_map/all_to_all | solution.py:434
  245.8 7.7 %all-to-all-done.8 = bf16[64,32,128]{2,1,0:T(8,128)(2,1)S(1)} async-done(((bf16[64,32,128]{2,1,0:T(8,128)(2,1)}), bf16[64,32,128]{2,1,0:T(8,128)(2,1)S(1)}, u32[]{:S(2)}, u32[]{:S(2)}) %all-to-all-start.8) | async-done | bytes 524320 | tf_op jit(solution)/shard_map/all_to_all | solution.py:434
  (119 shorter events, 80.0 us)
Async XLA Ops:
  4.3 25.5 %all-to-all-start = ((bf16[4,5,80,512]{3,2,1,0:T(8,128)(2,1)}), bf16[4,5,80,512]{3,2,1,0:T(8,128)(2,1)S(1)}, u32[]{:S(2)}, u32[]{:S(2)}) async-start(bf16[4,5,80,512]{3,2,1,0:T(8,128)(2,1)} %broadcast_select_fusion), calls=%async_computation | async-start | bytes 3276800 | tf_op jit(solution)/shard_map/all_to_all | solution.py:397
  22.3 11.5 %copy-start.13 = (bf16[128,384]{0,1:T(8,128)(2,1)S(1)}, bf16[128,384]{0,1:T(8,128)(2,1)}, u32[]{:S(2)}) copy-start(bf16[128,384]{0,1:T(8,128)(2,1)} %copy-done.12) | copy-start | bytes 294916
  22.3 11.5 %copy-start.17 = (bf16[384,192]{0,1:T(8,128)(2,1)S(1)}, bf16[384,192]{0,1:T(8,128)(2,1)}, u32[]{:S(2)}) copy-start(bf16[384,192]{0,1:T(8,128)(2,1)} %slice.78) | copy-start | bytes 442372
  29.8 11.8 %collective-permute-start = (bf16[5,80,512]{2,1,0:T(8,128)(2,1)}, bf16[5,80,512]{2,1,0:T(8,128)(2,1)S(1)}, u32[]{:S(2)}, u32[]{:S(2)}) collective-permute-start(bf16[5,80,512]{2,1,0:T(8,128)(2,1)} %get-tuple-element.74), channel_id=1, source_target_pairs={{0,1},{1,2},{2,3},{3,0},{4,5},{5,6},{6,7},{7,4},{8,9},{9,10},{10,1... | collective-permute-start | bytes 1228808 | tf_op jit(solution)/shard_map/ppermute | solution.py:407
  30.1 11.6 %collective-permute-start.1 = (bf16[5,80,512]{2,1,0:T(8,128)(2,1)S(1)}, bf16[5,80,512]{2,1,0:T(8,128)(2,1)S(1)}, u32[]{:S(2)}, u32[]{:S(2)}) collective-permute-start(bf16[5,80,512]{2,1,0:T(8,128)(2,1)S(1)} %get-tuple-element.75), channel_id=1, source_target_pairs={{0,3},{1,0},{2,1},{3,2},{4,7},{5,4},{6,5},{7,6},{8,11},{9,8},{10,9... | collective-permute-start | bytes 1228808 | tf_op jit(solution)/shard_map/ppermute | solution.py:407
  33.9 28.4 %copy-start.11 = (bf16[384,384]{0,1:T(8,128)(2,1)}, bf16[384,384]{0,1:T(8,128)(2,1)S(1)}, u32[]{:S(2)}) copy-start(bf16[384,384]{0,1:T(8,128)(2,1)S(1)} %fusion.10) | copy-start | bytes 884740
  43.1 25.4 %all-to-all-start.1 = ((bf16[64,16,384]{2,1,0:T(8,128)(2,1)}), bf16[64,16,384]{2,1,0:T(8,128)(2,1)S(1)}, u32[]{:S(2)}, u32[]{:S(2)}) async-start(bf16[64,16,384]{2,1,0:T(8,128)(2,1)} %bitcast.64), calls=%async_computation.1 | async-start | bytes 1572864 | tf_op jit(solution)/shard_map/all_to_all | solution.py:392
  52.9 28.0 %collective-permute-start.4 = (bf16[5,80,512]{2,1,0:T(8,128)(2,1)S(1)}, bf16[5,80,512]{2,1,0:T(8,128)(2,1)S(1)}, u32[]{:S(2)}, u32[]{:S(2)}) collective-permute-start(bf16[5,80,512]{2,1,0:T(8,128)(2,1)S(1)} %get-tuple-element.83), channel_id=1, source_target_pairs={{0,2},{1,3},{2,0},{3,1},{4,6},{5,7},{6,4},{7,5},{8,10},{9,11},{10,... | collective-permute-start | bytes 1228808 | tf_op jit(solution)/shard_map/ppermute | solution.py:407
  57.0 22.1 %collective-permute-start.3 = (bf16[1,320,512]{2,1,0:T(8,128)(2,1)S(1)}, bf16[1,320,512]{2,1,0:T(8,128)(2,1)S(1)}, u32[]{:S(2)}, u32[]{:S(2)}) collective-permute-start(bf16[1,320,512]{2,1,0:T(8,128)(2,1)S(1)} %get-tuple-element.137), channel_id=1, source_target_pairs={{1,0},{2,1},{3,2},{4,3},{5,4},{6,5},{7,6},{8,7},{9,8},{10,9},{11,1... | collective-permute-start | bytes 983048 | tf_op jit(solution)/shard_map/ppermute | solution.py:424
  60.3 20.6 %collective-permute-start.2 = (bf16[1,320,512]{2,1,0:T(8,128)(2,1)S(1)}, bf16[1,320,512]{2,1,0:T(8,128)(2,1)}, u32[]{:S(2)}, u32[]{:S(2)}) collective-permute-start(bf16[1,320,512]{2,1,0:T(8,128)(2,1)S(1)} %get-tuple-element.138), channel_id=1, source_target_pairs={{0,1},{1,2},{2,3},{3,4},{4,5},{5,6},{6,7},{7,8},{8,9},{9,10},{10,1... | collective-permute-start | bytes 983048 | tf_op jit(solution)/shard_map/ppermute | solution.py:423
  76.6 12.4 %copy-start.3 = (bf16[3,3,512,128]{2,3,1,0:T(8,128)(2,1)S(1)}, bf16[3,3,512,128]{2,3,1,0:T(8,128)(2,1)}, u32[]{:S(2)}) copy-start(bf16[3,3,512,128]{2,3,1,0:T(8,128)(2,1)} %copy.42) | copy-start | bytes 3538948
  79.1 11.3 %copy-start.23 = (bf16[1,320,512]{2,1,0:T(8,128)(2,1)}, bf16[1,320,512]{2,1,0:T(8,128)(2,1)S(1)}, u32[]{:S(2)}) copy-start(bf16[1,320,512]{2,1,0:T(8,128)(2,1)S(1)} %collective-permute-done.3.below) | copy-start | bytes 983044
  80.9 23.5 %all-to-all-start.2 = ((bf16[64,16,384]{2,1,0:T(8,128)(2,1)}), bf16[64,16,384]{2,1,0:T(8,128)(2,1)S(1)}, u32[]{:S(2)}, u32[]{:S(2)}) async-start(bf16[64,16,384]{2,1,0:T(8,128)(2,1)} %bitcast.67), calls=%async_computation.2 | async-start | bytes 1572864 | tf_op jit(solution)/shard_map/all_to_all | solution.py:392
  117.0 20.2 %all-to-all-start.3 = ((bf16[64,16,384]{2,1,0:T(8,128)(2,1)}), bf16[64,16,384]{2,1,0:T(8,128)(2,1)S(1)}, u32[]{:S(2)}, u32[]{:S(2)}) async-start(bf16[64,16,384]{2,1,0:T(8,128)(2,1)} %bitcast.62), calls=%async_computation.3 | async-start | bytes 1572864 | tf_op jit(solution)/shard_map/all_to_all | solution.py:392
  137.2 3.3 %collective-permute-start.5 = (bf16[1536,384]{1,0:T(8,128)(2,1)}, bf16[1536,384]{1,0:T(8,128)(2,1)S(1)}, u32[]{:S(2)}, u32[]{:S(2)}) collective-permute-start(bf16[1536,384]{1,0:T(8,128)(2,1)} %get-tuple-element.104), channel_id=1, source_target_pairs={{0,4},{4,0},{8,12},{12,8},{16,20},{20,16},{24,28},{28,24},{32,36},... | collective-permute-start | bytes 3538952 | tf_op jit(solution)/shard_map/ppermute | solution.py:411
  143.1 27.0 %all-to-all-start.4 = ((bf16[32,48,384]{2,1,0:T(8,128)(2,1)}), bf16[32,48,384]{2,1,0:T(8,128)(2,1)S(1)}, u32[]{:S(2)}, u32[]{:S(2)}) async-start(bf16[32,48,384]{2,1,0:T(8,128)(2,1)} %bitcast.25), calls=%async_computation.4 | async-start | bytes 2359296 | tf_op jit(solution)/shard_map/all_to_all | solution.py:419
  148.1 20.1 %collective-permute-start.7 = (bf16[1,320,512]{2,1,0:T(8,128)(2,1)S(1)}, bf16[1,320,512]{2,1,0:T(8,128)(2,1)S(1)}, u32[]{:S(2)}, u32[]{:S(2)}) collective-permute-start(bf16[1,320,512]{2,1,0:T(8,128)(2,1)S(1)} %get-tuple-element.135), channel_id=1, source_target_pairs={{1,0},{2,1},{3,2},{4,3},{5,4},{6,5},{7,6},{8,7},{9,8},{10,9},{11,1... | collective-permute-start | bytes 983048 | tf_op jit(solution)/shard_map/ppermute | solution.py:424
  153.0 17.0 %collective-permute-start.6 = (bf16[1,320,512]{2,1,0:T(8,128)(2,1)S(1)}, bf16[1,320,512]{2,1,0:T(8,128)(2,1)S(1)}, u32[]{:S(2)}, u32[]{:S(2)}) collective-permute-start(bf16[1,320,512]{2,1,0:T(8,128)(2,1)S(1)} %get-tuple-element.136), channel_id=1, source_target_pairs={{0,1},{1,2},{2,3},{3,4},{4,5},{5,6},{6,7},{7,8},{8,9},{9,10},{10,1... | collective-permute-start | bytes 983048 | tf_op jit(solution)/shard_map/ppermute | solution.py:423
  170.1 22.9 %all-to-all-start.5 = ((bf16[64,16,384]{2,1,0:T(8,128)(2,1)}), bf16[64,16,384]{2,1,0:T(8,128)(2,1)S(1)}, u32[]{:S(2)}, u32[]{:S(2)}) async-start(bf16[64,16,384]{2,1,0:T(8,128)(2,1)} %bitcast.63), calls=%async_computation.5 | async-start | bytes 1572864 | tf_op jit(solution)/shard_map/all_to_all | solution.py:392
  194.2 21.4 %all-to-all-start.6 = ((bf16[32,48,384]{2,1,0:T(8,128)(2,1)}), bf16[32,48,384]{2,1,0:T(8,128)(2,1)S(1)}, u32[]{:S(2)}, u32[]{:S(2)}) async-start(bf16[32,48,384]{2,1,0:T(8,128)(2,1)} %reshape_tile.3), calls=%async_computation.6 | async-start | bytes 2359296 | tf_op jit(solution)/shard_map/all_to_all | solution.py:419
  215.7 12.3 %copy-start.1 = (bf16[32,48,384]{2,1,0:T(8,128)(2,1)}, bf16[32,48,384]{2,1,0:T(8,128)(2,1)S(1)}, u32[]{:S(2)}) copy-start(bf16[32,48,384]{2,1,0:T(8,128)(2,1)S(1)} %all-to-all-done.6) | copy-start | bytes 3538948
  215.7 25.0 %collective-permute-start.8 = (bf16[1536,384]{1,0:T(8,128)(2,1)S(1)}, bf16[1536,384]{1,0:T(8,128)(2,1)S(1)}, u32[]{:S(2)}, u32[]{:S(2)}) collective-permute-start(bf16[1536,384]{1,0:T(8,128)(2,1)S(1)} %bitcast.44), channel_id=1, source_target_pairs={{0,4},{4,0},{8,12},{12,8},{16,20},{20,16},{24,28},{28,24},{32,36},... | collective-permute-start | bytes 3538952 | tf_op jit(solution)/shard_map/ppermute | solution.py:411
  217.4 17.7 %all-to-all-start.7 = ((bf16[64,32,128]{2,1,0:T(8,128)(2,1)}), bf16[64,32,128]{2,1,0:T(8,128)(2,1)S(1)}, u32[]{:S(2)}, u32[]{:S(2)}) async-start(bf16[64,32,128]{2,1,0:T(8,128)(2,1)} %bitcast.69), calls=%async_computation.7 | async-start | bytes 1048576 | tf_op jit(solution)/shard_map/all_to_all | solution.py:429
  236.1 17.4 %all-to-all-start.8 = ((bf16[64,32,128]{2,1,0:T(8,128)(2,1)}), bf16[64,32,128]{2,1,0:T(8,128)(2,1)S(1)}, u32[]{:S(2)}, u32[]{:S(2)}) async-start(bf16[64,32,128]{2,1,0:T(8,128)(2,1)} %broadcast_in_dim.44), calls=%async_computation.8 | async-start | bytes 1048576 | tf_op jit(solution)/shard_map/all_to_all | solution.py:434
  (25 other events, 112.5 us)

commit v7 on v6

--- a/solution.py
+++ b/solution.py
@@ -34,7 +34,7 @@
 
 
 def slope_and_silu(value):
-    sigma = 1.0 / (1.0 + jnp.exp(-value))
+    sigma = 0.5 + 0.5 * jnp.tanh(0.5 * value)
     return sigma * (1.0 + value * (1.0 - sigma)), value * sigma
 
 
@@ -208,7 +208,7 @@
     norm, sizes, cl, cols, got, tct, tst, tc, ts, unit, pre, w_out, w_out_t, my_col, *refs,
 ):
     cots = refs[:cols]
-    output, d_out, d_joined, sent, grad, got_x, got_s, cot, v, z, acc_g = refs[cols:]
+    output, d_out, d_joined, sent, joined_out, got_x, got_s, cot, v, z = refs[cols:]
     y = pl.program_id(0)
     w = cots[0].shape[1]
     for k in range(cols):
@@ -217,6 +217,7 @@
 
     back = line_back(y, norm, sizes, got, tct, tst, z, got_x, got_s)
     joined = (unit[0].astype(F32) + back.astype(F32)).astype(BF)
+    joined_out[0] = joined
     pre_all = jnp.concatenate([pre[0, :, :cl], pre[0, :, cl:] + dot(joined, w_out[...])], 1)
     slope, silu = slope_and_silu(pre_all)
     output[0] = silu.astype(BF)
@@ -224,21 +225,7 @@
     d_out[0] = d
     dj = dot(d[:, cl:], w_out_t[...]).astype(BF)
     d_joined[0] = dj
-    g = dot(joined, d[:, cl:], ROWS_OF)
-
-    @pl.when(y == 0)
-    def _():
-        acc_g[...] = g
-
-    @pl.when(y > 0)
-    def _():
-        acc_g[...] += g
-
     transform_out(y, norm, sizes, dj, tc, ts, sent, v, z)
-
-    @pl.when(y == pl.num_programs(0) - 1)
-    def _():
-        grad[...] = acc_g[0 : grad.shape[0], :].astype(BF)
 
 
 def tail_kernel(
@@ -309,7 +296,7 @@
     pre[0, :, cl:] = shifted(cross[:, :g], 1) + cross[:, g : 2 * g] + shifted(cross[:, 2 * g :], -1)
 
 
-def conv_grad_kernel(cl, above, masked, below, d_out, g_out, core, mine, other, pad, acc_l, acc_c):
+def conv_grad_kernel(cl, above, masked, below, d_out, joined, core, mine, other, pad, acc_l, acc_c, acc_g):
     y = pl.program_id(0)
     rows = masked.shape[0]
 
@@ -320,10 +307,12 @@
         pad[rows + 1] = below[0]
         acc_l[...] = jnp.zeros_like(acc_l)
         acc_c[...] = jnp.zeros_like(acc_c)
+        acc_g[...] = jnp.zeros_like(acc_g)
 
     d_local = three(d_out[0, :, :cl])
     d_global = three(d_out[0, :, cl:])
     g = d_global.shape[1] // 3
+    acc_g[...] += dot(joined[0], d_out[0, :, cl:], ROWS_OF)
     for i in range(3):
         x = pad[y + i]
         acc_l[i] += dot(x, d_local, ROWS_OF)
@@ -336,8 +325,8 @@
             for j in range(3):
                 at = (3 * i + j) * cl
                 rest[at : at + cl, :] = acc_c[i, :, j * g : (j + 1) * g].astype(BF)
-        at, size = 9 * cl, g_out.shape[0]
-        rest[at : at + size, :] = g_out[...]
+        at, size = 9 * cl, 192
+        rest[at : at + size, :] = acc_g[0:size, :].astype(BF)
         rest[at + size :, :] = jnp.zeros((rest.shape[0] - at - size, g), BF)
 
     last = y == pl.num_programs(0) - 1
@@ -531,7 +520,7 @@
         [vm((rows + 2, width, ch), BF)],
         flops=18 * pix * (ch * cl + cl * cg), bytes_=9 << 20,
     )
-    output, d_out, d_joined, sent, grad_out = call(
+    output, d_out, d_joined, sent, joined = call(
         functools.partial(middle_kernel, norm_w, sizes, cl, cols),
         "middle",
         (rows,),
@@ -543,9 +532,9 @@
         + [(c, (1, w, ch), at_y) for c in cots],
         [
             (wide, BF, one_row(ch), at_y), (wide, BF, one_row(ch), at_y), ((rows, width, 256), BF, one_row(256), at_y),
-            ((n, 384), BF, None, None), ((cs, cg), BF, None, None),
+            ((n, 384), BF, None, None), ((rows, width, 256), BF, one_row(256), at_y),
         ],
-        [vm((used, 384), BF), vm((used, 256), BF), vm((width, ch), BF), vm(lined, F32), vm((3, n, 128), F32), vm((256, cg), F32)],
+        [vm((used, 384), BF), vm((used, 256), BF), vm((width, ch), BF), vm(lined, F32), vm((3, n, 128), F32)],
         flops=3 << 30, bytes_=12 << 20,
     )
     got = swap(sent, count)
@@ -555,9 +544,9 @@
         functools.partial(conv_grad_kernel, cl),
         "conv_grad",
         (rows,),
-        [(above, None, None), (masked, None, None), (below, None, None), (d_out, one_row(ch), at_y), (grad_out, None, None), (my_core, None, None)],
+        [(above, None, None), (masked, None, None), (below, None, None), (d_out, one_row(ch), at_y), (joined, one_row(256), at_y), (my_core, None, None)],
         [((3 * ch, 384), BF, None, None), ((3 * ch, 384), BF, None, None)],
-        [vm((rows + 2, width, ch), BF), vm((3, ch, 3 * cl), F32), vm((3, cl, 3 * cg), F32)],
+        [vm((rows + 2, width, ch), BF), vm((3, ch, 3 * cl), F32), vm((3, cl, 3 * cg), F32), vm((256, cg), F32)],
         flops=18 * pix * (ch * cl + cl * cg), bytes_=7 << 20,
     )
     got, other = tied(got, other)
@@ -586,9 +575,9 @@
         [vm((rows + 2, width, 3 * cl), BF), vm((rows + 2, width, 3 * cg), BF)],
         flops=18 * pix * (ch * cl + cl * cg), bytes_=9 << 20,
     )
+    early = jnp.tile(early.astype(F32).sum(0).astype(BF), (count // 2, 1))
     got, d_conv, early = tied(got, d_conv, early)
-    early = early.astype(F32).sum(0).astype(BF)
-    early = core_exchange(jnp.tile(early, (count // 2, 1)), count).reshape(-1, 384)
+    early = core_exchange(early, count).reshape(-1, 384)
     late_rows = -(-(3 * 384 + 3 * cs) // (16 * count)) * 16 * count
     d_unit, late = call(
         functools.partial(tail_kernel, norm_w, sizes, cl),

time: 257 us -> 257 us (level)
  transfers between devices with their start and end apart: 18 -> 18, of which waited for: 13 -> 13; matrix products, arithmetic and copies ran while one was open for 9% -> 9% of each run, Pallas kernels for 28% -> 29%
where the time goes in v7:
time: 257 us; the launch traced here: 255 us
  Pallas kernels  84.1 us (33%)
  starting transfers between devices  73.2 us (28%)
  waiting for transfers between devices  60.5 us (24%)
  local copies, waits for them, and re-layouts  25.6 us (10%)
  other arithmetic  10.5 us (4%)
    pallas_call x10, Pallas kernels, call(): pl.pallas_call(body, grid=grid, in_specs=[spec(a.shape, block, index) for...  84.1 us
    all_to_all x4, starting transfers between devices, swap(): lax.all_to_all(x.reshape(count, -1, x.shape[-1]), AXES, 0, 0, tiled=True)  29.9 us
    all_to_all x4, waiting for transfers between devices, swap(): lax.all_to_all(x.reshape(count, -1, x.shape[-1]), AXES, 0, 0, tiled=True)  18.8 us
    all_to_all x2, waiting for transfers between devices, core_exchange(): return lax.all_to_all(x, AXES, 0, 0, axis_index_groups=groups, tiled=True)  9.55 us
    ppermute x2, starting transfers between devices, edges(): up = lax.ppermute(field[:1], AXES, [(i + 1, i) for i in range(count - 1)])  8.46 us
    all_to_all x2, starting transfers between devices, core_exchange(): return lax.all_to_all(x, AXES, 0, 0, axis_index_groups=groups, tiled=True)  8.44 us
    unnamed x59, local copies, waits for them, and re-layouts  7.88 us
    all_to_all x1, waiting for transfers between devices, gather(): lax.all_to_all(jnp.broadcast_to(x[None], (count,) + x.shape), AXES, 0, 0,...  7.7 us
  transfers between devices with their start and end apart: 18, of which 13 were waited for; matrix products, arithmetic and copies ran while one was open for 9% of the time, Pallas kernels for 29%

profile of v7, /device:TPU:1, one launch (start us, length us, event | category | flops | bytes accessed | tf_op | source)
XLA Modules:
  0.0 254.9 jit_solution(9836102638528213173)
XLA Ops:
  4.3 5.0 %all-to-all-start = ((bf16[4,5,80,512]{3,2,1,0:T(8,128)(2,1)}), bf16[4,5,80,512]{3,2,1,0:T(8,128)(2,1)S(1)}, u32[]{:S(2)}, u32[]{:S(2)}) async-start(bf16[4,5,80,512]{3,2,1,0:T(8,128)(2,1)} %broadcast_select_fusion), calls=%async_computation | async-start | bytes 3276800 | tf_op jit(solution)/shard_map/all_to_all | solution.py:386
  24.8 5.0 %all-to-all-done.marked = bf16[4,5,80,512]{3,2,1,0:T(8,128)(2,1)S(1)} async-done(((bf16[4,5,80,512]{3,2,1,0:T(8,128)(2,1)}), bf16[4,5,80,512]{3,2,1,0:T(8,128)(2,1)S(1)}, u32[]{:S(2)}, u32[]{:S(2)}) %all-to-all-start) | async-done | bytes 1638432 | tf_op jit(solution)/shard_map/all_to_all | solution.py:386
  34.0 7.6 %head.1 = (bf16[5,320,512]{2,1,0:T(8,128)(2,1)}, bf16[5,320,256]{2,1,0:T(8,128)(2,1)}, bf16[1024,384]{1,0:T(8,128)(2,1)}) custom-call(bf16[4,5,80,512]{3,2,1,0:T(8,128)(2,1)} %copy-done, bf16[384,256]{1,0:T(8,128)(2,1)} %pad_maximum_fusion.1.w_in, bf16[192,320]{1,0:T(8,128)(2,1)} %constant.91.clone.tc, bf16[192,320]{1,0:T(8,128)(2,1)} %constant.92.clone.ts), custom_call_target="tpu_custom_call" | custom-call | flops 1073741824 | bytes 6291456 | tf_op jit(solution)/shard_map/head/pallas_call | solution.py:81
  43.1 9.8 %all-to-all-start.1 = ((bf16[64,16,384]{2,1,0:T(8,128)(2,1)}), bf16[64,16,384]{2,1,0:T(8,128)(2,1)S(1)}, u32[]{:S(2)}, u32[]{:S(2)}) async-start(bf16[64,16,384]{2,1,0:T(8,128)(2,1)} %bitcast.66), calls=%async_computation.1 | async-start | bytes 1572864 | tf_op jit(solution)/shard_map/all_to_all | solution.py:381
  63.2 5.3 %all-to-all-done.1 = bf16[64,16,384]{2,1,0:T(8,128)(2,1)S(1)} async-done(((bf16[64,16,384]{2,1,0:T(8,128)(2,1)}), bf16[64,16,384]{2,1,0:T(8,128)(2,1)S(1)}, u32[]{:S(2)}, u32[]{:S(2)}) %all-to-all-start.1) | async-done | bytes 786464 | tf_op jit(solution)/shard_map/all_to_all | solution.py:381
  69.4 7.1 %frequency.1 = (bf16[3,320,384]{2,1,0:T(8,128)(2,1)}, bf16[1024,384]{1,0:T(8,128)(2,1)}) custom-call(bf16[1024,384]{1,0:T(8,128)(2,1)} %bitcast.68, bf16[320,320]{1,0:T(8,128)(2,1)} %constant.93.clone.hc, bf16[320,320]{1,0:T(8,128)(2,1)} %constant.94.clone.hs, bf16[384,384]{1,0:T(8,128)(2,1)} %copy.46.w_freq, f32[1,3]{1,0:T(1,128)} %or_select_fusion.weight, ...), custom_call_target="tpu_custom_call" | custom-call | flops 3221225472 | bytes 7340032 | tf_op jit(solution)/shard_map/frequency/pallas_call | solution.py:81
  80.9 8.0 %all-to-all-start.2 = ((bf16[64,16,384]{2,1,0:T(8,128)(2,1)}), bf16[64,16,384]{2,1,0:T(8,128)(2,1)S(1)}, u32[]{:S(2)}, u32[]{:S(2)}) async-start(bf16[64,16,384]{2,1,0:T(8,128)(2,1)} %bitcast.69), calls=%async_computation.2 | async-start | bytes 1572864 | tf_op jit(solution)/shard_map/all_to_all | solution.py:381
  90.4 8.7 %conv.1.pre = f32[5,320,512]{2,1,0:T(8,128)} custom-call(bf16[1,320,512]{2,1,0:T(8,128)(2,1)} %collective-permute-done.2.above, bf16[5,320,512]{2,1,0:T(8,128)(2,1)} %get-tuple-element.80.masked, bf16[1,320,512]{2,1,0:T(8,128)(2,1)} %copy-done.23, bf16[3,512,384]{2,1,0:T(8,128)(2,1)} %copy.47.w_local, bf16[384,1152]{1,0:T(8,128)(2,1)} %bitcast.62), custom_call_target="tpu_custom_call" | custom-call | flops 3303014400 | bytes 9437184 | tf_op jit(solution)/shard_map/conv/pallas_call | solution.py:81
  99.1 5.2 %all-to-all-done.2 = bf16[64,16,384]{2,1,0:T(8,128)(2,1)S(1)} async-done(((bf16[64,16,384]{2,1,0:T(8,128)(2,1)}), bf16[64,16,384]{2,1,0:T(8,128)(2,1)S(1)}, u32[]{:S(2)}, u32[]{:S(2)}) %all-to-all-start.2) | async-done | bytes 786464 | tf_op jit(solution)/shard_map/all_to_all | solution.py:381
  105.2 11.3 %middle.1 = (bf16[5,320,512]{2,1,0:T(8,128)(2,1)}, bf16[5,320,512]{2,1,0:T(8,128)(2,1)}, bf16[5,320,256]{2,1,0:T(8,128)(2,1)}, bf16[1024,384]{1,0:T(8,128)(2,1)}, bf16[5,320,256]{2,1,0:T(8,128)(2,1)}) custom-call(bf16[1024,384]{1,0:T(8,128)(2,1)} %bitcast.67, bf16[320,192]{1,0:T(8,128)(2,1)} %constant.89.clone.tct, bf16[320,192]{1,0:T(8,128)(2,1)} %constant.90.clone.tst, ...), custom_call_target="tpu_custom_call" | custom-call | flops 3221225472 | bytes 12582912 | tf_op jit(solution)/shard_map/middle/pallas_call | solution.py:81
  116.5 4.7 %all-to-all-start.3 = ((bf16[64,16,384]{2,1,0:T(8,128)(2,1)}), bf16[64,16,384]{2,1,0:T(8,128)(2,1)S(1)}, u32[]{:S(2)}, u32[]{:S(2)}) async-start(bf16[64,16,384]{2,1,0:T(8,128)(2,1)} %bitcast.64), calls=%async_computation.3 | async-start | bytes 1572864 | tf_op jit(solution)/shard_map/all_to_all | solution.py:381
  121.2 11.9 %conv_grad.1 = (bf16[1536,384]{1,0:T(8,128)(2,1)}, bf16[1536,384]{1,0:T(8,128)(2,1)}) custom-call(bf16[1,320,512]{2,1,0:T(8,128)(2,1)} %collective-permute-done.2.above, bf16[5,320,512]{2,1,0:T(8,128)(2,1)} %get-tuple-element.80.masked, bf16[1,320,512]{2,1,0:T(8,128)(2,1)} %copy-done.23, bf16[5,320,512]{2,1,0:T(8,128)(2,1)} %get-tuple-element.99.d_out, ...), custom_call_target="tpu_custom_call" | custom-call | flops 3303014400 | bytes 7340032 | tf_op jit(solution)/shard_map/conv_grad/pallas_call | solution.py:81
  148.2 5.1 %collective-permute-start.7 = (bf16[1,320,512]{2,1,0:T(8,128)(2,1)S(1)}, bf16[1,320,512]{2,1,0:T(8,128)(2,1)S(1)}, u32[]{:S(2)}, u32[]{:S(2)}) collective-permute-start(bf16[1,320,512]{2,1,0:T(8,128)(2,1)S(1)} %get-tuple-element.135), channel_id=1, source_target_pairs={{1,0},{2,1},{3,2},{4,3},{5,4},{6,5},{7,6},{8,7},{9,8},{10,9},{11,1... | collective-permute-start | bytes 983048 | tf_op jit(solution)/shard_map/ppermute | solution.py:413
  155.5 9.4 %frequency_back.1 = (bf16[1024,384]{1,0:T(8,128)(2,1)}, bf16[384,384]{1,0:T(8,128)(2,1)}) custom-call(bf16[1024,384]{1,0:T(8,128)(2,1)} %bitcast.63, bf16[320,320]{1,0:T(8,128)(2,1)} %constant.93.clone.hc, bf16[320,320]{1,0:T(8,128)(2,1)} %constant.94.clone.hs, bf16[384,384]{1,0:T(8,128)(2,1)} %copy.46.w_freq, bf16[384,384]{1,0:T(8,128)(2,1)} %bitcast.59, ...), custom_call_target="tpu_custom_call" | custom-call | flops 3221225472 | bytes 8388608 | tf_op jit(solution)/shard_map/frequency_back/pallas_call | solution.py:81
  170.3 7.4 %all-to-all-start.5 = ((bf16[64,16,384]{2,1,0:T(8,128)(2,1)}), bf16[64,16,384]{2,1,0:T(8,128)(2,1)S(1)}, u32[]{:S(2)}, u32[]{:S(2)}) async-start(bf16[64,16,384]{2,1,0:T(8,128)(2,1)} %bitcast.65), calls=%async_computation.5 | async-start | bytes 1572864 | tf_op jit(solution)/shard_map/all_to_all | solution.py:381
  177.8 10.5 %conv_back.1.d_conv = f32[5,320,512]{2,1,0:T(8,128)} custom-call(bf16[1,320,512]{2,1,0:T(8,128)(2,1)} %copy-done.25, bf16[5,320,512]{2,1,0:T(8,128)(2,1)} %get-tuple-element.99.d_out, bf16[1,320,512]{2,1,0:T(8,128)(2,1)} %copy-done.24, bf16[3,384,512]{2,1,0:T(8,128)(2,1)} %bitcast.60, bf16[3,1152,128]{2,1,0:T(8,128)(2,1)} %bitcast.61), custom_call_target="tpu_custom_call" | custom-call | flops 3303014400 | bytes 9437184 | tf_op jit(solution)/shard_map/conv_back/pallas_call | solution.py:81
  188.4 4.7 %all-to-all-done.5 = bf16[64,16,384]{2,1,0:T(8,128)(2,1)S(1)} async-done(((bf16[64,16,384]{2,1,0:T(8,128)(2,1)}), bf16[64,16,384]{2,1,0:T(8,128)(2,1)S(1)}, u32[]{:S(2)}, u32[]{:S(2)}) %all-to-all-start.5) | async-done | bytes 786464 | tf_op jit(solution)/shard_map/all_to_all | solution.py:381
  198.3 7.9 %tail.1 = (bf16[5,320,256]{2,1,0:T(8,128)(2,1)}, bf16[2048,128]{1,0:T(8,128)(2,1)}) custom-call(bf16[1024,384]{1,0:T(8,128)(2,1)} %bitcast.53, bf16[320,192]{1,0:T(8,128)(2,1)} %constant.89.clone.tct, bf16[320,192]{1,0:T(8,128)(2,1)} %constant.90.clone.tst, bf16[5,320,512]{2,1,0:T(8,128)(2,1)} %get-tuple-element.80.masked, ...), custom_call_target="tpu_custom_call" | custom-call | flops 1073741824 | bytes 5242880 | tf_op jit(solution)/shard_map/tail/pallas_call | solution.py:81
  206.2 9.5 %all-to-all-done.6 = bf16[32,48,384]{2,1,0:T(8,128)(2,1)S(1)} async-done(((bf16[32,48,384]{2,1,0:T(8,128)(2,1)}), bf16[32,48,384]{2,1,0:T(8,128)(2,1)S(1)}, u32[]{:S(2)}, u32[]{:S(2)}) %all-to-all-start.6) | async-done | bytes 1179680 | tf_op jit(solution)/shard_map/all_to_all | solution.py:408
  217.5 4.8 %all-to-all-start.7 = ((bf16[64,32,128]{2,1,0:T(8,128)(2,1)}), bf16[64,32,128]{2,1,0:T(8,128)(2,1)S(1)}, u32[]{:S(2)}, u32[]{:S(2)}) async-start(bf16[64,32,128]{2,1,0:T(8,128)(2,1)} %bitcast.71), calls=%async_computation.7 | async-start | bytes 1048576 | tf_op jit(solution)/shard_map/all_to_all | solution.py:418
  222.3 5.5 %finish.1 = bf16[5,320,512]{2,1,0:T(8,128)(2,1)} custom-call(bf16[4,5,80,512]{3,2,1,0:T(8,128)(2,1)} %copy-done, bf16[5,320,256]{2,1,0:T(8,128)(2,1)} %get-tuple-element.122.d_unit, f32[5,320,512]{2,1,0:T(8,128)} %conv_back.1.d_conv, bf16[256,384]{1,0:T(8,128)(2,1)} %pad.7.w_in_t), custom_call_target="tpu_custom_call" | custom-call | flops 314572800 | bytes 7340032 | tf_op jit(solution)/shard_map/finish/pallas_call | solution.py:81
  227.8 7.1 %all-to-all-done.7 = bf16[64,32,128]{2,1,0:T(8,128)(2,1)S(1)} async-done(((bf16[64,32,128]{2,1,0:T(8,128)(2,1)}), bf16[64,32,128]{2,1,0:T(8,128)(2,1)S(1)}, u32[]{:S(2)}, u32[]{:S(2)}) %all-to-all-start.7) | async-done | bytes 524320 | tf_op jit(solution)/shard_map/all_to_all | solution.py:418
  235.9 4.6 %all-to-all-start.8 = ((bf16[64,32,128]{2,1,0:T(8,128)(2,1)}), bf16[64,32,128]{2,1,0:T(8,128)(2,1)S(1)}, u32[]{:S(2)}, u32[]{:S(2)}) async-start(bf16[64,32,128]{2,1,0:T(8,128)(2,1)} %broadcast_in_dim.44), calls=%async_computation.8 | async-start | bytes 1048576 | tf_op jit(solution)/shard_map/all_to_all | solution.py:423
  245.6 7.7 %all-to-all-done.8 = bf16[64,32,128]{2,1,0:T(8,128)(2,1)S(1)} async-done(((bf16[64,32,128]{2,1,0:T(8,128)(2,1)}), bf16[64,32,128]{2,1,0:T(8,128)(2,1)S(1)}, u32[]{:S(2)}, u32[]{:S(2)}) %all-to-all-start.8) | async-done | bytes 524320 | tf_op jit(solution)/shard_map/all_to_all | solution.py:423
  (119 shorter events, 79.9 us)
Async XLA Ops:
  4.3 25.5 %all-to-all-start = ((bf16[4,5,80,512]{3,2,1,0:T(8,128)(2,1)}), bf16[4,5,80,512]{3,2,1,0:T(8,128)(2,1)S(1)}, u32[]{:S(2)}, u32[]{:S(2)}) async-start(bf16[4,5,80,512]{3,2,1,0:T(8,128)(2,1)} %broadcast_select_fusion), calls=%async_computation | async-start | bytes 3276800 | tf_op jit(solution)/shard_map/all_to_all | solution.py:386
  22.4 11.5 %copy-start.13 = (bf16[128,384]{0,1:T(8,128)(2,1)S(1)}, bf16[128,384]{0,1:T(8,128)(2,1)}, u32[]{:S(2)}) copy-start(bf16[128,384]{0,1:T(8,128)(2,1)} %copy-done.12) | copy-start | bytes 294916
  22.4 11.5 %copy-start.17 = (bf16[384,192]{0,1:T(8,128)(2,1)S(1)}, bf16[384,192]{0,1:T(8,128)(2,1)}, u32[]{:S(2)}) copy-start(bf16[384,192]{0,1:T(8,128)(2,1)} %slice.78) | copy-start | bytes 442372
  29.8 11.8 %collective-permute-start = (bf16[5,80,512]{2,1,0:T(8,128)(2,1)}, bf16[5,80,512]{2,1,0:T(8,128)(2,1)S(1)}, u32[]{:S(2)}, u32[]{:S(2)}) collective-permute-start(bf16[5,80,512]{2,1,0:T(8,128)(2,1)} %get-tuple-element.74), channel_id=1, source_target_pairs={{0,1},{1,2},{2,3},{3,0},{4,5},{5,6},{6,7},{7,4},{8,9},{9,10},{10,1... | collective-permute-start | bytes 1228808 | tf_op jit(solution)/shard_map/ppermute | solution.py:396
  30.1 11.6 %collective-permute-start.1 = (bf16[5,80,512]{2,1,0:T(8,128)(2,1)S(1)}, bf16[5,80,512]{2,1,0:T(8,128)(2,1)S(1)}, u32[]{:S(2)}, u32[]{:S(2)}) collective-permute-start(bf16[5,80,512]{2,1,0:T(8,128)(2,1)S(1)} %get-tuple-element.75), channel_id=1, source_target_pairs={{0,3},{1,0},{2,1},{3,2},{4,7},{5,4},{6,5},{7,6},{8,11},{9,8},{10,9... | collective-permute-start | bytes 1228808 | tf_op jit(solution)/shard_map/ppermute | solution.py:396
  34.0 28.3 %copy-start.11 = (bf16[384,384]{0,1:T(8,128)(2,1)}, bf16[384,384]{0,1:T(8,128)(2,1)S(1)}, u32[]{:S(2)}) copy-start(bf16[384,384]{0,1:T(8,128)(2,1)S(1)} %fusion.10) | copy-start | bytes 884740
  43.1 25.4 %all-to-all-start.1 = ((bf16[64,16,384]{2,1,0:T(8,128)(2,1)}), bf16[64,16,384]{2,1,0:T(8,128)(2,1)S(1)}, u32[]{:S(2)}, u32[]{:S(2)}) async-start(bf16[64,16,384]{2,1,0:T(8,128)(2,1)} %bitcast.66), calls=%async_computation.1 | async-start | bytes 1572864 | tf_op jit(solution)/shard_map/all_to_all | solution.py:381
  52.9 28.0 %collective-permute-start.4 = (bf16[5,80,512]{2,1,0:T(8,128)(2,1)S(1)}, bf16[5,80,512]{2,1,0:T(8,128)(2,1)S(1)}, u32[]{:S(2)}, u32[]{:S(2)}) collective-permute-start(bf16[5,80,512]{2,1,0:T(8,128)(2,1)S(1)} %get-tuple-element.83), channel_id=1, source_target_pairs={{0,2},{1,3},{2,0},{3,1},{4,6},{5,7},{6,4},{7,5},{8,10},{9,11},{10,... | collective-permute-start | bytes 1228808 | tf_op jit(solution)/shard_map/ppermute | solution.py:396
  57.0 22.1 %collective-permute-start.3 = (bf16[1,320,512]{2,1,0:T(8,128)(2,1)S(1)}, bf16[1,320,512]{2,1,0:T(8,128)(2,1)S(1)}, u32[]{:S(2)}, u32[]{:S(2)}) collective-permute-start(bf16[1,320,512]{2,1,0:T(8,128)(2,1)S(1)} %get-tuple-element.137), channel_id=1, source_target_pairs={{1,0},{2,1},{3,2},{4,3},{5,4},{6,5},{7,6},{8,7},{9,8},{10,9},{11,1... | collective-permute-start | bytes 983048 | tf_op jit(solution)/shard_map/ppermute | solution.py:413
  60.3 20.6 %collective-permute-start.2 = (bf16[1,320,512]{2,1,0:T(8,128)(2,1)S(1)}, bf16[1,320,512]{2,1,0:T(8,128)(2,1)}, u32[]{:S(2)}, u32[]{:S(2)}) collective-permute-start(bf16[1,320,512]{2,1,0:T(8,128)(2,1)S(1)} %get-tuple-element.138), channel_id=1, source_target_pairs={{0,1},{1,2},{2,3},{3,4},{4,5},{5,6},{6,7},{7,8},{8,9},{9,10},{10,1... | collective-permute-start | bytes 983048 | tf_op jit(solution)/shard_map/ppermute | solution.py:412
  76.5 12.4 %copy-start.3 = (bf16[3,3,512,128]{2,3,1,0:T(8,128)(2,1)S(1)}, bf16[3,3,512,128]{2,3,1,0:T(8,128)(2,1)}, u32[]{:S(2)}) copy-start(bf16[3,3,512,128]{2,3,1,0:T(8,128)(2,1)} %copy.42) | copy-start | bytes 3538948
  79.1 11.2 %copy-start.23 = (bf16[1,320,512]{2,1,0:T(8,128)(2,1)}, bf16[1,320,512]{2,1,0:T(8,128)(2,1)S(1)}, u32[]{:S(2)}) copy-start(bf16[1,320,512]{2,1,0:T(8,128)(2,1)S(1)} %collective-permute-done.3.below) | copy-start | bytes 983044
  80.9 23.4 %all-to-all-start.2 = ((bf16[64,16,384]{2,1,0:T(8,128)(2,1)}), bf16[64,16,384]{2,1,0:T(8,128)(2,1)S(1)}, u32[]{:S(2)}, u32[]{:S(2)}) async-start(bf16[64,16,384]{2,1,0:T(8,128)(2,1)} %bitcast.69), calls=%async_computation.2 | async-start | bytes 1572864 | tf_op jit(solution)/shard_map/all_to_all | solution.py:381
  116.5 20.2 %all-to-all-start.3 = ((bf16[64,16,384]{2,1,0:T(8,128)(2,1)}), bf16[64,16,384]{2,1,0:T(8,128)(2,1)S(1)}, u32[]{:S(2)}, u32[]{:S(2)}) async-start(bf16[64,16,384]{2,1,0:T(8,128)(2,1)} %bitcast.64), calls=%async_computation.3 | async-start | bytes 1572864 | tf_op jit(solution)/shard_map/all_to_all | solution.py:381
  136.7 3.3 %collective-permute-start.5 = (bf16[1536,384]{1,0:T(8,128)(2,1)}, bf16[1536,384]{1,0:T(8,128)(2,1)S(1)}, u32[]{:S(2)}, u32[]{:S(2)}) collective-permute-start(bf16[1536,384]{1,0:T(8,128)(2,1)} %get-tuple-element.104), channel_id=1, source_target_pairs={{0,4},{4,0},{8,12},{12,8},{16,20},{20,16},{24,28},{28,24},{32,36},... | collective-permute-start | bytes 3538952 | tf_op jit(solution)/shard_map/ppermute | solution.py:400
  142.6 27.7 %all-to-all-start.4 = ((bf16[32,48,384]{2,1,0:T(8,128)(2,1)}), bf16[32,48,384]{2,1,0:T(8,128)(2,1)S(1)}, u32[]{:S(2)}, u32[]{:S(2)}) async-start(bf16[32,48,384]{2,1,0:T(8,128)(2,1)} %bitcast.25), calls=%async_computation.4 | async-start | bytes 2359296 | tf_op jit(solution)/shard_map/all_to_all | solution.py:408
  148.2 20.0 %collective-permute-start.7 = (bf16[1,320,512]{2,1,0:T(8,128)(2,1)S(1)}, bf16[1,320,512]{2,1,0:T(8,128)(2,1)S(1)}, u32[]{:S(2)}, u32[]{:S(2)}) collective-permute-start(bf16[1,320,512]{2,1,0:T(8,128)(2,1)S(1)} %get-tuple-element.135), channel_id=1, source_target_pairs={{1,0},{2,1},{3,2},{4,3},{5,4},{6,5},{7,6},{8,7},{9,8},{10,9},{11,1... | collective-permute-start | bytes 983048 | tf_op jit(solution)/shard_map/ppermute | solution.py:413
  153.4 16.9 %collective-permute-start.6 = (bf16[1,320,512]{2,1,0:T(8,128)(2,1)S(1)}, bf16[1,320,512]{2,1,0:T(8,128)(2,1)S(1)}, u32[]{:S(2)}, u32[]{:S(2)}) collective-permute-start(bf16[1,320,512]{2,1,0:T(8,128)(2,1)S(1)} %get-tuple-element.136), channel_id=1, source_target_pairs={{0,1},{1,2},{2,3},{3,4},{4,5},{5,6},{6,7},{7,8},{8,9},{9,10},{10,1... | collective-permute-start | bytes 983048 | tf_op jit(solution)/shard_map/ppermute | solution.py:412
  170.3 22.8 %all-to-all-start.5 = ((bf16[64,16,384]{2,1,0:T(8,128)(2,1)}), bf16[64,16,384]{2,1,0:T(8,128)(2,1)S(1)}, u32[]{:S(2)}, u32[]{:S(2)}) async-start(bf16[64,16,384]{2,1,0:T(8,128)(2,1)} %bitcast.65), calls=%async_computation.5 | async-start | bytes 1572864 | tf_op jit(solution)/shard_map/all_to_all | solution.py:381
  194.3 21.4 %all-to-all-start.6 = ((bf16[32,48,384]{2,1,0:T(8,128)(2,1)}), bf16[32,48,384]{2,1,0:T(8,128)(2,1)S(1)}, u32[]{:S(2)}, u32[]{:S(2)}) async-start(bf16[32,48,384]{2,1,0:T(8,128)(2,1)} %bitcast.29), calls=%async_computation.6 | async-start | bytes 2359296 | tf_op jit(solution)/shard_map/all_to_all | solution.py:408
  215.7 12.1 %copy-start.1 = (bf16[32,48,384]{2,1,0:T(8,128)(2,1)}, bf16[32,48,384]{2,1,0:T(8,128)(2,1)S(1)}, u32[]{:S(2)}) copy-start(bf16[32,48,384]{2,1,0:T(8,128)(2,1)S(1)} %all-to-all-done.6) | copy-start | bytes 3538948
  215.7 24.8 %collective-permute-start.8 = (bf16[1536,384]{1,0:T(8,128)(2,1)S(1)}, bf16[1536,384]{1,0:T(8,128)(2,1)S(1)}, u32[]{:S(2)}, u32[]{:S(2)}) collective-permute-start(bf16[1536,384]{1,0:T(8,128)(2,1)S(1)} %bitcast.46), channel_id=1, source_target_pairs={{0,4},{4,0},{8,12},{12,8},{16,20},{20,16},{24,28},{28,24},{32,36},... | collective-permute-start | bytes 3538952 | tf_op jit(solution)/shard_map/ppermute | solution.py:400
  217.5 17.5 %all-to-all-start.7 = ((bf16[64,32,128]{2,1,0:T(8,128)(2,1)}), bf16[64,32,128]{2,1,0:T(8,128)(2,1)S(1)}, u32[]{:S(2)}, u32[]{:S(2)}) async-start(bf16[64,32,128]{2,1,0:T(8,128)(2,1)} %bitcast.71), calls=%async_computation.7 | async-start | bytes 1048576 | tf_op jit(solution)/shard_map/all_to_all | solution.py:418
  235.9 17.4 %all-to-all-start.8 = ((bf16[64,32,128]{2,1,0:T(8,128)(2,1)}), bf16[64,32,128]{2,1,0:T(8,128)(2,1)S(1)}, u32[]{:S(2)}, u32[]{:S(2)}) async-start(bf16[64,32,128]{2,1,0:T(8,128)(2,1)} %broadcast_in_dim.44), calls=%async_computation.8 | async-start | bytes 1048576 | tf_op jit(solution)/shard_map/all_to_all | solution.py:423
  (25 other events, 112.6 us)

commit v8 on v6

--- a/solution.py
+++ b/solution.py
@@ -34,7 +34,7 @@
 
 
 def slope_and_silu(value):
-    sigma = 1.0 / (1.0 + jnp.exp(-value))
+    sigma = 0.5 + 0.5 * jnp.tanh(0.5 * value)
     return sigma * (1.0 + value * (1.0 - sigma)), value * sigma
 
 
@@ -586,9 +586,9 @@
         [vm((rows + 2, width, 3 * cl), BF), vm((rows + 2, width, 3 * cg), BF)],
         flops=18 * pix * (ch * cl + cl * cg), bytes_=9 << 20,
     )
+    early = jnp.tile(early.astype(F32).sum(0).astype(BF), (count // 2, 1))
     got, d_conv, early = tied(got, d_conv, early)
-    early = early.astype(F32).sum(0).astype(BF)
-    early = core_exchange(jnp.tile(early, (count // 2, 1)), count).reshape(-1, 384)
+    early = core_exchange(early, count).reshape(-1, 384)
     late_rows = -(-(3 * 384 + 3 * cs) // (16 * count)) * 16 * count
     d_unit, late = call(
         functools.partial(tail_kernel, norm_w, sizes, cl),

time: 257 us -> 256 us (level)
  no operation moved by 1% of the time
where the time goes in v8:
time: 256 us; the launch traced here: 255 us
  Pallas kernels  83.5 us (33%)
  starting transfers between devices  72.5 us (28%)
  waiting for transfers between devices  61.4 us (24%)
  local copies, waits for them, and re-layouts  25.7 us (10%)
  other arithmetic  10.5 us (4%)
    pallas_call x10, Pallas kernels, call(): pl.pallas_call(body, grid=grid, in_specs=[spec(a.shape, block, index) for...  83.5 us
    all_to_all x4, starting transfers between devices, swap(): lax.all_to_all(x.reshape(count, -1, x.shape[-1]), AXES, 0, 0, tiled=True)  30 us
    all_to_all x4, waiting for transfers between devices, swap(): lax.all_to_all(x.reshape(count, -1, x.shape[-1]), AXES, 0, 0, tiled=True)  19.6 us
    all_to_all x2, waiting for transfers between devices, core_exchange(): return lax.all_to_all(x, AXES, 0, 0, axis_index_groups=groups, tiled=True)  9.55 us
    ppermute x2, starting transfers between devices, edges(): up = lax.ppermute(field[:1], AXES, [(i + 1, i) for i in range(count - 1)])  8.22 us
    unnamed x59, local copies, waits for them, and re-layouts  7.96 us
    all_to_all x2, starting transfers between devices, core_exchange(): return lax.all_to_all(x, AXES, 0, 0, axis_index_groups=groups, tiled=True)  7.88 us
    all_to_all x1, waiting for transfers between devices, gather(): lax.all_to_all(jnp.broadcast_to(x[None], (count,) + x.shape), AXES, 0, 0,...  7.7 us
  transfers between devices with their start and end apart: 18, of which 13 were waited for; matrix products, arithmetic and copies ran while one was open for 9% of the time, Pallas kernels for 28%

profile of v8, /device:TPU:1, one launch (start us, length us, event | category | flops | bytes accessed | tf_op | source)
XLA Modules:
  0.0 254.7 jit_solution(5204460169173201963)
XLA Ops:
  4.3 5.0 %all-to-all-start = ((bf16[4,5,80,512]{3,2,1,0:T(8,128)(2,1)}), bf16[4,5,80,512]{3,2,1,0:T(8,128)(2,1)S(1)}, u32[]{:S(2)}, u32[]{:S(2)}) async-start(bf16[4,5,80,512]{3,2,1,0:T(8,128)(2,1)} %broadcast_select_fusion), calls=%async_computation | async-start | bytes 3276800 | tf_op jit(solution)/shard_map/all_to_all | solution.py:397
  24.8 5.0 %all-to-all-done.marked = bf16[4,5,80,512]{3,2,1,0:T(8,128)(2,1)S(1)} async-done(((bf16[4,5,80,512]{3,2,1,0:T(8,128)(2,1)}), bf16[4,5,80,512]{3,2,1,0:T(8,128)(2,1)S(1)}, u32[]{:S(2)}, u32[]{:S(2)}) %all-to-all-start) | async-done | bytes 1638432 | tf_op jit(solution)/shard_map/all_to_all | solution.py:397
  34.0 7.6 %head.1 = (bf16[5,320,512]{2,1,0:T(8,128)(2,1)}, bf16[5,320,256]{2,1,0:T(8,128)(2,1)}, bf16[1024,384]{1,0:T(8,128)(2,1)}) custom-call(bf16[4,5,80,512]{3,2,1,0:T(8,128)(2,1)} %copy-done, bf16[384,256]{1,0:T(8,128)(2,1)} %pad_maximum_fusion.1.w_in, bf16[192,320]{1,0:T(8,128)(2,1)} %constant.91.clone.tc, bf16[192,320]{1,0:T(8,128)(2,1)} %constant.92.clone.ts), custom_call_target="tpu_custom_call" | custom-call | flops 1073741824 | bytes 6291456 | tf_op jit(solution)/shard_map/head/pallas_call | solution.py:81
  43.1 9.8 %all-to-all-start.1 = ((bf16[64,16,384]{2,1,0:T(8,128)(2,1)}), bf16[64,16,384]{2,1,0:T(8,128)(2,1)S(1)}, u32[]{:S(2)}, u32[]{:S(2)}) async-start(bf16[64,16,384]{2,1,0:T(8,128)(2,1)} %bitcast.66), calls=%async_computation.1 | async-start | bytes 1572864 | tf_op jit(solution)/shard_map/all_to_all | solution.py:392
  63.2 5.3 %all-to-all-done.1 = bf16[64,16,384]{2,1,0:T(8,128)(2,1)S(1)} async-done(((bf16[64,16,384]{2,1,0:T(8,128)(2,1)}), bf16[64,16,384]{2,1,0:T(8,128)(2,1)S(1)}, u32[]{:S(2)}, u32[]{:S(2)}) %all-to-all-start.1) | async-done | bytes 786464 | tf_op jit(solution)/shard_map/all_to_all | solution.py:392
  69.4 7.1 %frequency.1 = (bf16[3,320,384]{2,1,0:T(8,128)(2,1)}, bf16[1024,384]{1,0:T(8,128)(2,1)}) custom-call(bf16[1024,384]{1,0:T(8,128)(2,1)} %bitcast.68, bf16[320,320]{1,0:T(8,128)(2,1)} %constant.93.clone.hc, bf16[320,320]{1,0:T(8,128)(2,1)} %constant.94.clone.hs, bf16[384,384]{1,0:T(8,128)(2,1)} %copy.46.w_freq, f32[1,3]{1,0:T(1,128)} %or_select_fusion.weight, ...), custom_call_target="tpu_custom_call" | custom-call | flops 3221225472 | bytes 7340032 | tf_op jit(solution)/shard_map/frequency/pallas_call | solution.py:81
  80.9 8.0 %all-to-all-start.2 = ((bf16[64,16,384]{2,1,0:T(8,128)(2,1)}), bf16[64,16,384]{2,1,0:T(8,128)(2,1)S(1)}, u32[]{:S(2)}, u32[]{:S(2)}) async-start(bf16[64,16,384]{2,1,0:T(8,128)(2,1)} %bitcast.69), calls=%async_computation.2 | async-start | bytes 1572864 | tf_op jit(solution)/shard_map/all_to_all | solution.py:392
  90.4 8.7 %conv.1.pre = f32[5,320,512]{2,1,0:T(8,128)} custom-call(bf16[1,320,512]{2,1,0:T(8,128)(2,1)} %collective-permute-done.2.above, bf16[5,320,512]{2,1,0:T(8,128)(2,1)} %get-tuple-element.80.masked, bf16[1,320,512]{2,1,0:T(8,128)(2,1)} %copy-done.23, bf16[3,512,384]{2,1,0:T(8,128)(2,1)} %copy.47.w_local, bf16[384,1152]{1,0:T(8,128)(2,1)} %bitcast.62), custom_call_target="tpu_custom_call" | custom-call | flops 3303014400 | bytes 9437184 | tf_op jit(solution)/shard_map/conv/pallas_call | solution.py:81
  99.1 5.2 %all-to-all-done.2 = bf16[64,16,384]{2,1,0:T(8,128)(2,1)S(1)} async-done(((bf16[64,16,384]{2,1,0:T(8,128)(2,1)}), bf16[64,16,384]{2,1,0:T(8,128)(2,1)S(1)}, u32[]{:S(2)}, u32[]{:S(2)}) %all-to-all-start.2) | async-done | bytes 786464 | tf_op jit(solution)/shard_map/all_to_all | solution.py:392
  105.3 11.5 %middle.1 = (bf16[5,320,512]{2,1,0:T(8,128)(2,1)}, bf16[5,320,512]{2,1,0:T(8,128)(2,1)}, bf16[5,320,256]{2,1,0:T(8,128)(2,1)}, bf16[1024,384]{1,0:T(8,128)(2,1)}, bf16[192,384]{1,0:T(8,128)(2,1)}) custom-call(bf16[1024,384]{1,0:T(8,128)(2,1)} %bitcast.67, bf16[320,192]{1,0:T(8,128)(2,1)} %constant.89.clone.tct, bf16[320,192]{1,0:T(8,128)(2,1)} %constant.90.clone.tst, ...), custom_call_target="tpu_custom_call" | custom-call | flops 3221225472 | bytes 12582912 | tf_op jit(solution)/shard_map/middle/pallas_call | solution.py:81
  116.8 4.7 %all-to-all-start.3 = ((bf16[64,16,384]{2,1,0:T(8,128)(2,1)}), bf16[64,16,384]{2,1,0:T(8,128)(2,1)S(1)}, u32[]{:S(2)}, u32[]{:S(2)}) async-start(bf16[64,16,384]{2,1,0:T(8,128)(2,1)} %bitcast.64), calls=%async_computation.3 | async-start | bytes 1572864 | tf_op jit(solution)/shard_map/all_to_all | solution.py:392
  121.5 11.1 %conv_grad.1 = (bf16[1536,384]{1,0:T(8,128)(2,1)}, bf16[1536,384]{1,0:T(8,128)(2,1)}) custom-call(bf16[1,320,512]{2,1,0:T(8,128)(2,1)} %collective-permute-done.2.above, bf16[5,320,512]{2,1,0:T(8,128)(2,1)} %get-tuple-element.80.masked, bf16[1,320,512]{2,1,0:T(8,128)(2,1)} %copy-done.23, bf16[5,320,512]{2,1,0:T(8,128)(2,1)} %get-tuple-element.99.d_out, ...), custom_call_target="tpu_custom_call" | custom-call | flops 3303014400 | bytes 7340032 | tf_op jit(solution)/shard_map/conv_grad/pallas_call | solution.py:81
  148.0 4.9 %collective-permute-start.7 = (bf16[1,320,512]{2,1,0:T(8,128)(2,1)S(1)}, bf16[1,320,512]{2,1,0:T(8,128)(2,1)S(1)}, u32[]{:S(2)}, u32[]{:S(2)}) collective-permute-start(bf16[1,320,512]{2,1,0:T(8,128)(2,1)S(1)} %get-tuple-element.135), channel_id=1, source_target_pairs={{1,0},{2,1},{3,2},{4,3},{5,4},{6,5},{7,6},{8,7},{9,8},{10,9},{11,1... | collective-permute-start | bytes 983048 | tf_op jit(solution)/shard_map/ppermute | solution.py:424
  155.0 9.4 %frequency_back.1 = (bf16[1024,384]{1,0:T(8,128)(2,1)}, bf16[384,384]{1,0:T(8,128)(2,1)}) custom-call(bf16[1024,384]{1,0:T(8,128)(2,1)} %bitcast.63, bf16[320,320]{1,0:T(8,128)(2,1)} %constant.93.clone.hc, bf16[320,320]{1,0:T(8,128)(2,1)} %constant.94.clone.hs, bf16[384,384]{1,0:T(8,128)(2,1)} %copy.46.w_freq, bf16[384,384]{1,0:T(8,128)(2,1)} %bitcast.59, ...), custom_call_target="tpu_custom_call" | custom-call | flops 3221225472 | bytes 8388608 | tf_op jit(solution)/shard_map/frequency_back/pallas_call | solution.py:81
  169.9 7.5 %all-to-all-start.5 = ((bf16[64,16,384]{2,1,0:T(8,128)(2,1)}), bf16[64,16,384]{2,1,0:T(8,128)(2,1)S(1)}, u32[]{:S(2)}, u32[]{:S(2)}) async-start(bf16[64,16,384]{2,1,0:T(8,128)(2,1)} %bitcast.65), calls=%async_computation.5 | async-start | bytes 1572864 | tf_op jit(solution)/shard_map/all_to_all | solution.py:392
  177.6 10.5 %conv_back.1.d_conv = f32[5,320,512]{2,1,0:T(8,128)} custom-call(bf16[1,320,512]{2,1,0:T(8,128)(2,1)} %copy-done.25, bf16[5,320,512]{2,1,0:T(8,128)(2,1)} %get-tuple-element.99.d_out, bf16[1,320,512]{2,1,0:T(8,128)(2,1)} %copy-done.24, bf16[3,384,512]{2,1,0:T(8,128)(2,1)} %bitcast.60, bf16[3,1152,128]{2,1,0:T(8,128)(2,1)} %bitcast.61), custom_call_target="tpu_custom_call" | custom-call | flops 3303014400 | bytes 9437184 | tf_op jit(solution)/shard_map/conv_back/pallas_call | solution.py:81
  188.1 4.7 %all-to-all-done.5 = bf16[64,16,384]{2,1,0:T(8,128)(2,1)S(1)} async-done(((bf16[64,16,384]{2,1,0:T(8,128)(2,1)}), bf16[64,16,384]{2,1,0:T(8,128)(2,1)S(1)}, u32[]{:S(2)}, u32[]{:S(2)}) %all-to-all-start.5) | async-done | bytes 786464 | tf_op jit(solution)/shard_map/all_to_all | solution.py:392
  198.0 7.9 %tail.1 = (bf16[5,320,256]{2,1,0:T(8,128)(2,1)}, bf16[2048,128]{1,0:T(8,128)(2,1)}) custom-call(bf16[1024,384]{1,0:T(8,128)(2,1)} %bitcast.53, bf16[320,192]{1,0:T(8,128)(2,1)} %constant.89.clone.tct, bf16[320,192]{1,0:T(8,128)(2,1)} %constant.90.clone.tst, bf16[5,320,512]{2,1,0:T(8,128)(2,1)} %get-tuple-element.80.masked, ...), custom_call_target="tpu_custom_call" | custom-call | flops 1073741824 | bytes 5242880 | tf_op jit(solution)/shard_map/tail/pallas_call | solution.py:81
  205.9 9.5 %all-to-all-done.6 = bf16[32,48,384]{2,1,0:T(8,128)(2,1)S(1)} async-done(((bf16[32,48,384]{2,1,0:T(8,128)(2,1)}), bf16[32,48,384]{2,1,0:T(8,128)(2,1)S(1)}, u32[]{:S(2)}, u32[]{:S(2)}) %all-to-all-start.6) | async-done | bytes 1179680 | tf_op jit(solution)/shard_map/all_to_all | solution.py:419
  217.2 4.8 %all-to-all-start.7 = ((bf16[64,32,128]{2,1,0:T(8,128)(2,1)}), bf16[64,32,128]{2,1,0:T(8,128)(2,1)S(1)}, u32[]{:S(2)}, u32[]{:S(2)}) async-start(bf16[64,32,128]{2,1,0:T(8,128)(2,1)} %bitcast.71), calls=%async_computation.7 | async-start | bytes 1048576 | tf_op jit(solution)/shard_map/all_to_all | solution.py:429
  222.0 5.5 %finish.1 = bf16[5,320,512]{2,1,0:T(8,128)(2,1)} custom-call(bf16[4,5,80,512]{3,2,1,0:T(8,128)(2,1)} %copy-done, bf16[5,320,256]{2,1,0:T(8,128)(2,1)} %get-tuple-element.122.d_unit, f32[5,320,512]{2,1,0:T(8,128)} %conv_back.1.d_conv, bf16[256,384]{1,0:T(8,128)(2,1)} %pad.7.w_in_t), custom_call_target="tpu_custom_call" | custom-call | flops 314572800 | bytes 7340032 | tf_op jit(solution)/shard_map/finish/pallas_call | solution.py:81
  227.6 7.1 %all-to-all-done.7 = bf16[64,32,128]{2,1,0:T(8,128)(2,1)S(1)} async-done(((bf16[64,32,128]{2,1,0:T(8,128)(2,1)}), bf16[64,32,128]{2,1,0:T(8,128)(2,1)S(1)}, u32[]{:S(2)}, u32[]{:S(2)}) %all-to-all-start.7) | async-done | bytes 524320 | tf_op jit(solution)/shard_map/all_to_all | solution.py:429
  235.6 4.6 %all-to-all-start.8 = ((bf16[64,32,128]{2,1,0:T(8,128)(2,1)}), bf16[64,32,128]{2,1,0:T(8,128)(2,1)S(1)}, u32[]{:S(2)}, u32[]{:S(2)}) async-start(bf16[64,32,128]{2,1,0:T(8,128)(2,1)} %broadcast_in_dim.44), calls=%async_computation.8 | async-start | bytes 1048576 | tf_op jit(solution)/shard_map/all_to_all | solution.py:434
  245.3 7.7 %all-to-all-done.8 = bf16[64,32,128]{2,1,0:T(8,128)(2,1)S(1)} async-done(((bf16[64,32,128]{2,1,0:T(8,128)(2,1)}), bf16[64,32,128]{2,1,0:T(8,128)(2,1)S(1)}, u32[]{:S(2)}, u32[]{:S(2)}) %all-to-all-start.8) | async-done | bytes 524320 | tf_op jit(solution)/shard_map/all_to_all | solution.py:434
  (119 shorter events, 80.3 us)
Async XLA Ops:
  4.3 25.5 %all-to-all-start = ((bf16[4,5,80,512]{3,2,1,0:T(8,128)(2,1)}), bf16[4,5,80,512]{3,2,1,0:T(8,128)(2,1)S(1)}, u32[]{:S(2)}, u32[]{:S(2)}) async-start(bf16[4,5,80,512]{3,2,1,0:T(8,128)(2,1)} %broadcast_select_fusion), calls=%async_computation | async-start | bytes 3276800 | tf_op jit(solution)/shard_map/all_to_all | solution.py:397
  22.3 11.5 %copy-start.13 = (bf16[128,384]{0,1:T(8,128)(2,1)S(1)}, bf16[128,384]{0,1:T(8,128)(2,1)}, u32[]{:S(2)}) copy-start(bf16[128,384]{0,1:T(8,128)(2,1)} %copy-done.12) | copy-start | bytes 294916
  22.3 11.5 %copy-start.17 = (bf16[384,192]{0,1:T(8,128)(2,1)S(1)}, bf16[384,192]{0,1:T(8,128)(2,1)}, u32[]{:S(2)}) copy-start(bf16[384,192]{0,1:T(8,128)(2,1)} %slice.78) | copy-start | bytes 442372
  29.8 11.8 %collective-permute-start = (bf16[5,80,512]{2,1,0:T(8,128)(2,1)}, bf16[5,80,512]{2,1,0:T(8,128)(2,1)S(1)}, u32[]{:S(2)}, u32[]{:S(2)}) collective-permute-start(bf16[5,80,512]{2,1,0:T(8,128)(2,1)} %get-tuple-element.74), channel_id=1, source_target_pairs={{0,1},{1,2},{2,3},{3,0},{4,5},{5,6},{6,7},{7,4},{8,9},{9,10},{10,1... | collective-permute-start | bytes 1228808 | tf_op jit(solution)/shard_map/ppermute | solution.py:407
  30.1 11.5 %collective-permute-start.1 = (bf16[5,80,512]{2,1,0:T(8,128)(2,1)S(1)}, bf16[5,80,512]{2,1,0:T(8,128)(2,1)S(1)}, u32[]{:S(2)}, u32[]{:S(2)}) collective-permute-start(bf16[5,80,512]{2,1,0:T(8,128)(2,1)S(1)} %get-tuple-element.75), channel_id=1, source_target_pairs={{0,3},{1,0},{2,1},{3,2},{4,7},{5,4},{6,5},{7,6},{8,11},{9,8},{10,9... | collective-permute-start | bytes 1228808 | tf_op jit(solution)/shard_map/ppermute | solution.py:407
  33.9 28.4 %copy-start.11 = (bf16[384,384]{0,1:T(8,128)(2,1)}, bf16[384,384]{0,1:T(8,128)(2,1)S(1)}, u32[]{:S(2)}) copy-start(bf16[384,384]{0,1:T(8,128)(2,1)S(1)} %fusion.10) | copy-start | bytes 884740
  43.1 25.4 %all-to-all-start.1 = ((bf16[64,16,384]{2,1,0:T(8,128)(2,1)}), bf16[64,16,384]{2,1,0:T(8,128)(2,1)S(1)}, u32[]{:S(2)}, u32[]{:S(2)}) async-start(bf16[64,16,384]{2,1,0:T(8,128)(2,1)} %bitcast.66), calls=%async_computation.1 | async-start | bytes 1572864 | tf_op jit(solution)/shard_map/all_to_all | solution.py:392
  52.9 28.0 %collective-permute-start.4 = (bf16[5,80,512]{2,1,0:T(8,128)(2,1)S(1)}, bf16[5,80,512]{2,1,0:T(8,128)(2,1)S(1)}, u32[]{:S(2)}, u32[]{:S(2)}) collective-permute-start(bf16[5,80,512]{2,1,0:T(8,128)(2,1)S(1)} %get-tuple-element.83), channel_id=1, source_target_pairs={{0,2},{1,3},{2,0},{3,1},{4,6},{5,7},{6,4},{7,5},{8,10},{9,11},{10,... | collective-permute-start | bytes 1228808 | tf_op jit(solution)/shard_map/ppermute | solution.py:407
  57.0 22.1 %collective-permute-start.3 = (bf16[1,320,512]{2,1,0:T(8,128)(2,1)S(1)}, bf16[1,320,512]{2,1,0:T(8,128)(2,1)S(1)}, u32[]{:S(2)}, u32[]{:S(2)}) collective-permute-start(bf16[1,320,512]{2,1,0:T(8,128)(2,1)S(1)} %get-tuple-element.137), channel_id=1, source_target_pairs={{1,0},{2,1},{3,2},{4,3},{5,4},{6,5},{7,6},{8,7},{9,8},{10,9},{11,1... | collective-permute-start | bytes 983048 | tf_op jit(solution)/shard_map/ppermute | solution.py:424
  60.3 20.6 %collective-permute-start.2 = (bf16[1,320,512]{2,1,0:T(8,128)(2,1)S(1)}, bf16[1,320,512]{2,1,0:T(8,128)(2,1)}, u32[]{:S(2)}, u32[]{:S(2)}) collective-permute-start(bf16[1,320,512]{2,1,0:T(8,128)(2,1)S(1)} %get-tuple-element.138), channel_id=1, source_target_pairs={{0,1},{1,2},{2,3},{3,4},{4,5},{5,6},{6,7},{7,8},{8,9},{9,10},{10,1... | collective-permute-start | bytes 983048 | tf_op jit(solution)/shard_map/ppermute | solution.py:423
  76.5 12.4 %copy-start.3 = (bf16[3,3,512,128]{2,3,1,0:T(8,128)(2,1)S(1)}, bf16[3,3,512,128]{2,3,1,0:T(8,128)(2,1)}, u32[]{:S(2)}) copy-start(bf16[3,3,512,128]{2,3,1,0:T(8,128)(2,1)} %copy.42) | copy-start | bytes 3538948
  79.1 11.2 %copy-start.23 = (bf16[1,320,512]{2,1,0:T(8,128)(2,1)}, bf16[1,320,512]{2,1,0:T(8,128)(2,1)S(1)}, u32[]{:S(2)}) copy-start(bf16[1,320,512]{2,1,0:T(8,128)(2,1)S(1)} %collective-permute-done.3.below) | copy-start | bytes 983044
  80.9 23.4 %all-to-all-start.2 = ((bf16[64,16,384]{2,1,0:T(8,128)(2,1)}), bf16[64,16,384]{2,1,0:T(8,128)(2,1)S(1)}, u32[]{:S(2)}, u32[]{:S(2)}) async-start(bf16[64,16,384]{2,1,0:T(8,128)(2,1)} %bitcast.69), calls=%async_computation.2 | async-start | bytes 1572864 | tf_op jit(solution)/shard_map/all_to_all | solution.py:392
  116.8 20.2 %all-to-all-start.3 = ((bf16[64,16,384]{2,1,0:T(8,128)(2,1)}), bf16[64,16,384]{2,1,0:T(8,128)(2,1)S(1)}, u32[]{:S(2)}, u32[]{:S(2)}) async-start(bf16[64,16,384]{2,1,0:T(8,128)(2,1)} %bitcast.64), calls=%async_computation.3 | async-start | bytes 1572864 | tf_op jit(solution)/shard_map/all_to_all | solution.py:392
  137.0 3.3 %collective-permute-start.5 = (bf16[1536,384]{1,0:T(8,128)(2,1)}, bf16[1536,384]{1,0:T(8,128)(2,1)S(1)}, u32[]{:S(2)}, u32[]{:S(2)}) collective-permute-start(bf16[1536,384]{1,0:T(8,128)(2,1)} %get-tuple-element.104), channel_id=1, source_target_pairs={{0,4},{4,0},{8,12},{12,8},{16,20},{20,16},{24,28},{28,24},{32,36},... | collective-permute-start | bytes 3538952 | tf_op jit(solution)/shard_map/ppermute | solution.py:411
  142.9 27.0 %all-to-all-start.4 = ((bf16[32,48,384]{2,1,0:T(8,128)(2,1)}), bf16[32,48,384]{2,1,0:T(8,128)(2,1)S(1)}, u32[]{:S(2)}, u32[]{:S(2)}) async-start(bf16[32,48,384]{2,1,0:T(8,128)(2,1)} %bitcast.25), calls=%async_computation.4 | async-start | bytes 2359296 | tf_op jit(solution)/shard_map/all_to_all | solution.py:419
  148.0 20.0 %collective-permute-start.7 = (bf16[1,320,512]{2,1,0:T(8,128)(2,1)S(1)}, bf16[1,320,512]{2,1,0:T(8,128)(2,1)S(1)}, u32[]{:S(2)}, u32[]{:S(2)}) collective-permute-start(bf16[1,320,512]{2,1,0:T(8,128)(2,1)S(1)} %get-tuple-element.135), channel_id=1, source_target_pairs={{1,0},{2,1},{3,2},{4,3},{5,4},{6,5},{7,6},{8,7},{9,8},{10,9},{11,1... | collective-permute-start | bytes 983048 | tf_op jit(solution)/shard_map/ppermute | solution.py:424
  152.9 17.0 %collective-permute-start.6 = (bf16[1,320,512]{2,1,0:T(8,128)(2,1)S(1)}, bf16[1,320,512]{2,1,0:T(8,128)(2,1)S(1)}, u32[]{:S(2)}, u32[]{:S(2)}) collective-permute-start(bf16[1,320,512]{2,1,0:T(8,128)(2,1)S(1)} %get-tuple-element.136), channel_id=1, source_target_pairs={{0,1},{1,2},{2,3},{3,4},{4,5},{5,6},{6,7},{7,8},{8,9},{9,10},{10,1... | collective-permute-start | bytes 983048 | tf_op jit(solution)/shard_map/ppermute | solution.py:423
  169.9 22.9 %all-to-all-start.5 = ((bf16[64,16,384]{2,1,0:T(8,128)(2,1)}), bf16[64,16,384]{2,1,0:T(8,128)(2,1)S(1)}, u32[]{:S(2)}, u32[]{:S(2)}) async-start(bf16[64,16,384]{2,1,0:T(8,128)(2,1)} %bitcast.65), calls=%async_computation.5 | async-start | bytes 1572864 | tf_op jit(solution)/shard_map/all_to_all | solution.py:392
  194.1 21.4 %all-to-all-start.6 = ((bf16[32,48,384]{2,1,0:T(8,128)(2,1)}), bf16[32,48,384]{2,1,0:T(8,128)(2,1)S(1)}, u32[]{:S(2)}, u32[]{:S(2)}) async-start(bf16[32,48,384]{2,1,0:T(8,128)(2,1)} %bitcast.29), calls=%async_computation.6 | async-start | bytes 2359296 | tf_op jit(solution)/shard_map/all_to_all | solution.py:419
  215.5 12.1 %copy-start.1 = (bf16[32,48,384]{2,1,0:T(8,128)(2,1)}, bf16[32,48,384]{2,1,0:T(8,128)(2,1)S(1)}, u32[]{:S(2)}) copy-start(bf16[32,48,384]{2,1,0:T(8,128)(2,1)S(1)} %all-to-all-done.6) | copy-start | bytes 3538948
  215.5 24.8 %collective-permute-start.8 = (bf16[1536,384]{1,0:T(8,128)(2,1)S(1)}, bf16[1536,384]{1,0:T(8,128)(2,1)S(1)}, u32[]{:S(2)}, u32[]{:S(2)}) collective-permute-start(bf16[1536,384]{1,0:T(8,128)(2,1)S(1)} %bitcast.46), channel_id=1, source_target_pairs={{0,4},{4,0},{8,12},{12,8},{16,20},{20,16},{24,28},{28,24},{32,36},... | collective-permute-start | bytes 3538952 | tf_op jit(solution)/shard_map/ppermute | solution.py:411
  217.2 17.5 %all-to-all-start.7 = ((bf16[64,32,128]{2,1,0:T(8,128)(2,1)}), bf16[64,32,128]{2,1,0:T(8,128)(2,1)S(1)}, u32[]{:S(2)}, u32[]{:S(2)}) async-start(bf16[64,32,128]{2,1,0:T(8,128)(2,1)} %bitcast.71), calls=%async_computation.7 | async-start | bytes 1048576 | tf_op jit(solution)/shard_map/all_to_all | solution.py:429
  235.6 17.4 %all-to-all-start.8 = ((bf16[64,32,128]{2,1,0:T(8,128)(2,1)}), bf16[64,32,128]{2,1,0:T(8,128)(2,1)S(1)}, u32[]{:S(2)}, u32[]{:S(2)}) async-start(bf16[64,32,128]{2,1,0:T(8,128)(2,1)} %broadcast_in_dim.44), calls=%async_computation.8 | async-start | bytes 1048576 | tf_op jit(solution)/shard_map/all_to_all | solution.py:434
  (25 other events, 112.7 us)
